TPU v7x, 128 devices: a whole 4x4x4 slice. The times are simulated.
128 devices in a mesh: dp: 16 (over z, y_hi, core), tensor: 8 (over x, y_lo).
Axes of the slice: x: 4, y: 4 (y_hi: 2, y_lo: 2; y = y_hi * 2 + y_lo), z: 4, core: 2. Of those that a mesh axis runs over, the one named last changes fastest.
Arguments:
- activations: bfloat16 [1024, 4608], P('dp', 'tensor'), may hold values from -6 to 6
- enc_weight: bfloat16 [4608, 65536], P(None, ('dp', 'tensor')), may hold values from -0.09375 to 0.09375
- enc_bias: float32 [65536], P(('dp', 'tensor')), may hold values from -3 to 3
- thresholds: float32 [65536], P(('dp', 'tensor')), may hold values from 0.1 to 1
- dec_weight: bfloat16 [65536, 4608], P(('dp', 'tensor')), may hold values from -0.0234375 to 0.0234375
- dec_bias: float32 [4608], replicated, may hold values from -3 to 3
Outputs:
- grad_enc: bfloat16 [4608, 65536], P(None, ('dp', 'tensor'))
- grad_dec: bfloat16 [65536, 4608], P(('dp', 'tensor'))
All inputs are finite; a program needn't handle non-finite values.
Results may differ from a plain program's by a relative error of at most 0.0075.
Values may be sent and summed in bfloat16 or wider, within the bound.
No kernel may reach another device: no remote copies, remote signals or barrier semaphores. Data moves between devices by JAX's collectives and lax.ppermute only.
A program may use at most 128 MiB of HBM per device.

v0:
```python
import math

import jax
import jax.numpy as jnp
from jax import lax
from jax.sharding import PartitionSpec as P

band_width = 0.1
sparsity_coeff = 0.5


def on_device(activations, enc_weight, enc_bias, thresholds, dec_weight, dec_bias):
    wide_rows = lax.all_gather(activations, "tensor", axis=1, tiled=True)
    gathered = lax.all_gather(wide_rows, "dp", axis=0, tiled=True)
    centered = (gathered.astype(jnp.float32) - dec_bias).astype(jnp.bfloat16)
    pre_act = jnp.dot(centered, enc_weight, preferred_element_type=jnp.float32) + enc_bias
    gating = jax.nn.sigmoid((pre_act - thresholds) / band_width)
    code_values = pre_act * gating
    code_half = code_values.astype(jnp.bfloat16)
    row_scale = 1.0 / math.sqrt(gathered.shape[0])
    own_rows = gathered.shape[0] // (lax.axis_size("dp") * lax.axis_size("tensor"))
    recon_sum = lax.psum_scatter(
        jnp.dot(code_half, dec_weight, preferred_element_type=jnp.float32),
        ("dp", "tensor"),
        scatter_dimension=0,
        tiled=True,
    )
    offset = lax.axis_index(("dp", "tensor")) * own_rows
    targets = lax.dynamic_slice_in_dim(gathered, offset, own_rows, 0)
    recon_error = recon_sum + dec_bias - targets.astype(jnp.float32)
    delta_half = (recon_error * row_scale).astype(jnp.bfloat16)
    delta_all = lax.all_gather(delta_half, ("dp", "tensor"), axis=0, tiled=True)
    row_norms = jnp.sqrt(jnp.sum(jnp.square(dec_weight.astype(jnp.float32)), axis=1) + 1e-06)
    code_grad = lax.dot_general(
        delta_all, dec_weight, (((1,), (1,)), ((), ())), preferred_element_type=jnp.float32
    )
    code_grad = code_grad + sparsity_coeff * row_scale * row_norms
    slopes = gating + pre_act * gating * (1.0 - gating) / band_width
    preact_grad = (code_grad * slopes).astype(jnp.bfloat16)
    grad_enc = lax.dot_general(
        centered, preact_grad, (((0,), (0,)), ((), ())), preferred_element_type=jnp.float32
    )
    totals = jnp.sum(code_values, axis=0)
    grad_dec = lax.dot_general(
        code_half, delta_all, (((0,), (0,)), ((), ())), preferred_element_type=jnp.float32
    )
    grad_dec = (
        grad_dec
        + sparsity_coeff
        * row_scale
        * totals[:, None]
        * dec_weight.astype(jnp.float32)
        / row_norms[:, None]
    )
    return (grad_enc.astype(jnp.bfloat16), grad_dec.astype(jnp.bfloat16))


def solution(mesh):
    in_specs = (
        P("dp", "tensor"),
        P(None, ("dp", "tensor")),
        P(("dp", "tensor")),
        P(("dp", "tensor")),
        P(("dp", "tensor"), None),
        P(),
    )
    out_specs = (P(None, ("dp", "tensor")), P(("dp", "tensor"), None))
    return jax.shard_map(
        on_device, mesh=mesh, in_specs=in_specs, out_specs=out_specs, check_vma=False
    )
```

profile of v0, /device:TPU:1, one launch (start us, length us, event | category | flops | bytes accessed | tf_op | source)
XLA Modules:
  0.0 1176.2 jit_solution(17666041471092212975)
XLA Ops:
  7.2 0.0 copy-start
  7.2 0.0 copy-start.1
  7.2 0.0 copy-start.2
  7.2 0.0 all-gather.4.cloned.1.call-start
  7.2 25.0 %all-gather = bf16[8,576,64]{1,2,0:T(8,128)(2,1)S(1)} all-gather(bf16[1,576,64]{1,2,0:T(8,128)(2,1)} %bitcast.12), channel_id=1, replica_groups=mesh['dp'=16,'tensor'=8] {'tensor'}, dimensions={0}, use_global_device_ids=true | all-gather | bytes 663552 | tf_op jit(solution)/shard_map/all_gather | solution.py:13
  32.2 0.4 copy.9
  32.6 1.3 reshape.21
  33.9 0.0 all-gather.4.cloned.1.call-update
  33.9 0.0 reduce-scatter.2.cloned.1.call-start
  33.9 85.4 %all-gather.4.cloned.1.call-done = bf16[1024,4608]{1,0:T(8,128)(2,1)} async-done(((bf16[64,4608]{1,0:T(8,128)(2,1)}), bf16[1024,4608]{1,0:T(8,128)(2,1)}) %all-gather.4.cloned.1.call-update) | async-done | bytes 9437200 | tf_op jit(solution)/shard_map/all_gather | solution.py:14
  119.4 0.0 copy-done
  119.4 0.0 copy-done.1
  119.4 0.0 copy-done.2
  119.4 9.4 fusion.17
  128.8 11.5 fusion.13
  140.3 0.0 reduce-scatter.2.cloned.1.call-update
  140.3 0.2 all-gather.6.cloned.1.call-start
  140.6 656.7 %reduce-scatter.2.cloned.1.call-done = f32[8,4608]{1,0:T(8,128)} async-done(((f32[1024,4608]{1,0:T(8,128)}), f32[8,4608]{1,0:T(8,128)}) %reduce-scatter.2.cloned.1.call-update) | async-done | bytes 147472 | tf_op jit(solution)/shard_map/reduce_scatter | solution.py:22
  797.3 1.6 multiply_convert_fusion.1
  798.9 0.0 all-gather.6.cloned.1.call-update
  798.9 3.3 fusion
  802.3 326.4 %all-gather.6.cloned.1.call-done = bf16[1024,4608]{1,0:T(8,128)(2,1)} async-done(((bf16[8,4608]{1,0:T(8,128)(2,1)}), bf16[1024,4608]{1,0:T(8,128)(2,1)}) %all-gather.6.cloned.1.call-update) | async-done | bytes 9437200 | tf_op jit(solution)/shard_map/all_gather | solution.py:32
  1128.7 28.8 %fusion.6 = bf16[4608,512]{1,0:T(8,128)(2,1)} fusion(bf16[1024,4608]{1,0:T(8,128)(2,1)} %all-gather.4.cloned.1.call-done, f32[4608]{0:T(1024)S(1)} %copy-done, bf16[1024,4608]{1,0:T(8,128)(2,1)} %all-gather.6.cloned.1.call-done, bf16[512,4608]{1,0:T(8,128)(2,1)} %param.10, f32[1024,512]{1,0:T(8,128)S(1)} %get-tuple-element.5, f32[512]{0:T(512)S(1)} %get-tuple-element.3, ...), kind=kOutput, calls=%fused_computation.9 | convolution fusion | flops 9687531520 | bytes 30433280 | tf_op jit(solution)/shard_map/dot_general | solution.py:40
  1157.5 12.2 %fusion.3 = bf16[512,4608]{1,0:T(8,128)(2,1)} fusion(bf16[512,4608]{1,0:T(8,128)(2,1)} %param.10, bf16[1024,4608]{1,0:T(8,128)(2,1)} %all-gather.6.cloned.1.call-done, f32[512]{0:T(512)S(1)} %get-tuple-element.2, f32[512]{0:T(512)S(1)} %broadcast_multiply_fusion, f32[1024,512]{1,0:T(8,128)S(1)} %get-tuple-element.5, f32[512]{0:T(512)S(1)} %copy-done.1, ...), kind=kOutput, calls=%fused_computation.6 | convolution fusion | flops 4847828992 | bytes 20979712 | tf_op jit(solution)/shard_map/dot_general | solution.py:44
  (2 shorter events, 0.0 us)
Async XLA Ops:
  7.2 112.2 %copy-start = (f32[4608]{0:T(1024)S(1)}, f32[4608]{0:T(1024)}, u32[]{:S(2)}) copy-start(f32[4608]{0:T(1024)} %param.11) | copy-start | bytes 55300
  7.2 112.2 %copy-start.1 = (f32[512]{0:T(512)S(1)}, f32[512]{0:T(512)}, u32[]{:S(2)}) copy-start(f32[512]{0:T(512)} %param.9) | copy-start | bytes 6148
  7.2 112.2 %copy-start.2 = (f32[512]{0:T(512)S(1)}, f32[512]{0:T(512)}, u32[]{:S(2)}) copy-start(f32[512]{0:T(512)} %param.8) | copy-start | bytes 6148
  7.2 112.2 %all-gather.4.cloned.1.call-start = ((), (), s32[]{:S(2)}) async-start(), calls=%async_computation.1 | async-start | bytes 10027008 | tf_op jit(solution)/shard_map/all_gather | solution.py:14
  33.9 763.4 %reduce-scatter.2.cloned.1.call-start = ((), (), s32[]{:S(2)}) async-start(), calls=%async_computation.2 | async-start | bytes 19021824 | tf_op jit(solution)/shard_map/reduce_scatter | solution.py:22
  140.3 988.3 %all-gather.6.cloned.1.call-start = ((), (), s32[]{:S(2)}) async-start(), calls=%async_computation.3 | async-start | bytes 9510912 | tf_op jit(solution)/shard_map/all_gather | solution.py:32
Sparse Core Ops, SparseCore 0:
  34.0 85.3 all-gather.3
  140.4 656.8 reduce-scatter.1
  799.6 329.0 all-gather.5
where the time goes:
time: 1180 us
  waiting for transfers between devices  1070 us (91%)
  matrix products  61.9 us (5%)
  blocking collectives  25 us (2%)
  between operations  13.8 us (1%)
    reduce_scatter x1, waiting for transfers between devices, on_device(): lax.psum_scatter(jnp.dot(code_half, dec_weight, preferred_element_type=jn...  657 us
    all_gather x1, waiting for transfers between devices, on_device(): delta_all = lax.all_gather(delta_half, ('dp', 'tensor'), axis=0, tiled=True)  326 us
    all_gather x1, waiting for transfers between devices, on_device(): gathered = lax.all_gather(wide_rows, 'dp', axis=0, tiled=True)  85.4 us
    dot_general x1, matrix products, on_device(): lax.dot_general(centered, preact_grad, (((0,), (0,)), ((), ())), preferre...  28.8 us
    all_gather x1, blocking collectives, on_device(): wide_rows = lax.all_gather(activations, 'tensor', axis=1, tiled=True)  25 us
  transfers between devices with their start and end apart: 3, of which 3 were waited for; matrix products, arithmetic and copies ran while one was open for 0% of the time, Pallas kernels for 0%

commit v1 on v0

v1 whole, which is shorter than its diff:
```python
import math

import jax
import jax.numpy as jnp
from jax import lax
from jax.sharding import Mesh, PartitionSpec as P

band_width = 0.1
sparsity_coeff = 0.5

bf16, f32 = jnp.bfloat16, jnp.float32
MESH = ("z", "yh", "core", "x", "yl")


def device(z, y, x, core):
    return (((z * 2 + y // 2) * 2 + core) * 4 + x) * 2 + y % 2


def cubes(pairing):
    groups = []
    for core in range(2):
        step = (1, 3)[(pairing + core) % 2]
        corners = (0, 1 if step == 3 else 2)
        pairs = [(corner, corner ^ step) for corner in corners]
        for zs in pairs:
            for ys in pairs:
                for xs in pairs:
                    groups.append([device(z, y, x, core) for z in zs for y in ys for x in xs])
    return groups


def trade(blocks, pairing):
    return lax.all_to_all(blocks, MESH, 0, 0, axis_index_groups=cubes(pairing))


def swap(block):
    return lax.ppermute(block, "core", [(0, 1), (1, 0)])


def barrier(*arrays):
    return lax.optimization_barrier(arrays)


def gather(own):
    rows = own
    for pairing in (0, 1):
        copies, = barrier(jnp.broadcast_to(rows, (8, *rows.shape)))
        rows = trade(copies, pairing).reshape(-1, own.shape[1])
    rows, = barrier(rows)
    return rows, swap(rows)


def scatter(blocks):
    for pairing in (1, 0):
        blocks = blocks.astype(bf16).reshape(8, -1, blocks.shape[-1])
        blocks = jnp.sum(trade(blocks, pairing).astype(f32), axis=0)
    return blocks


def on_device(activations, enc_weight, enc_bias, thresholds, dec_weight, dec_bias):
    row_scale = 1.0 / math.sqrt(1024)
    own_rows = lax.all_to_all(activations, ("x", "yl"), split_axis=0, concat_axis=1, tiled=True)
    own_rows = own_rows.astype(f32)
    row_norms = jnp.sqrt(jnp.sum(jnp.square(dec_weight.astype(f32)), axis=1) + 1e-06)
    own_centered, = barrier((own_rows - dec_bias).astype(bf16))
    centered = gather(own_centered)

    def encode(rows):
        pre_act, = barrier(jnp.dot(rows, enc_weight, preferred_element_type=f32) + enc_bias)
        gating = jax.nn.sigmoid((pre_act - thresholds) / band_width)
        code_values = pre_act * gating
        slopes = gating + pre_act * gating * (1.0 - gating) / band_width
        return barrier(code_values.astype(bf16), slopes, jnp.sum(code_values, axis=0))

    code, slopes, totals = zip(*(encode(rows) for rows in centered))
    totals = totals[0] + totals[1]

    recon = []
    for part in jnp.split(dec_weight, 3, axis=1):
        theirs = swap(jnp.dot(code[1], part, preferred_element_type=f32).astype(bf16))
        mine = jnp.dot(code[0], part, preferred_element_type=f32)
        recon.append((mine + theirs.astype(f32)).astype(bf16))
    recon, = barrier(jnp.concatenate(recon, axis=1))
    recon_error = scatter(recon) + dec_bias - own_rows
    own_delta, = barrier((recon_error * row_scale).astype(bf16))
    delta = gather(own_delta)

    grads = []
    for rows, code_rows, slope, delta_rows in zip(centered, code, slopes, delta):
        code_grad = lax.dot_general(
            delta_rows, dec_weight, (((1,), (1,)), ((), ())), preferred_element_type=f32
        )
        code_grad = code_grad + sparsity_coeff * row_scale * row_norms
        rows_t, code_t, preact_grad = barrier(rows.T, code_rows.T, (code_grad * slope).astype(bf16))
        grads.append(
            (
                jnp.dot(rows_t, preact_grad, preferred_element_type=f32),
                jnp.dot(code_t, delta_rows, preferred_element_type=f32),
            )
        )
    (grad_enc, grad_dec), (more_enc, more_dec) = grads
    grad_dec = (
        grad_dec
        + sparsity_coeff
        * row_scale
        * totals[:, None]
        * dec_weight.astype(f32)
        / row_norms[:, None]
    )
    grad_enc, grad_dec = barrier(grad_enc, grad_dec)
    return ((grad_enc + more_enc).astype(bf16), (grad_dec + more_dec).astype(bf16))


def solution(mesh):
    torus = Mesh(mesh.devices.reshape(4, 2, 2, 4, 2), MESH)
    dp, tensor = ("z", "yh", "core"), ("x", "yl")
    latents = dp + tensor
    in_specs = (P(dp, tensor), P(None, latents), P(latents), P(latents), P(latents, None), P())
    out_specs = (P(None, latents), P(latents, None))
    return jax.shard_map(
        on_device, mesh=torus, in_specs=in_specs, out_specs=out_specs, check_vma=False
    )
```

time: 1180 us -> 223 us (0.19)
  waiting for transfers between devices: 1070 us -> 7.72 us
  blocking collectives: 25 us -> 156 us
  matrix products: 61.9 us -> 41.3 us
  between operations: 13.8 us -> 1.06 us
    reduce_scatter x1 -> x0, waiting for transfers between devices: 657 us -> none  [on_device(): lax.psum_scatter(jnp.dot(code_half, dec_weight, preferred_element_type=jn...]
    all_gather x2 -> x0, waiting for transfers between devices: 412 us -> none  [the longest x1 326 us: on_device(): delta_all = lax.all_gather(delta_half, ('dp', 'tensor'), axis=0, tiled=True)]
    all_to_all x0 -> x7, blocking collectives: none -> 156 us  [the longest x6 145 us: trade(): return lax.all_to_all(blocks, MESH, 0, 0, axis_index_groups=cubes(pairing))]
    all_gather x1 -> x0, blocking collectives: 25 us -> none  [on_device(): wide_rows = lax.all_gather(activations, 'tensor', axis=1, tiled=True)]
    dot_general x4 -> x14, matrix products: 61.9 us -> 41.3 us  [the longest x2 13 us: on_device(): jnp.dot(code_t, delta_rows, preferred_element_type=f32)]
  transfers between devices with their start and end apart: 3 -> 5, of which waited for: 3 -> 4; matrix products, arithmetic and copies ran while one was open for 0% -> 10% of each run, Pallas kernels for 0% -> 0%
where the time goes in v1:
time: 223 us
  blocking collectives  156 us (70%)
  matrix products  41.3 us (19%)
  starting transfers between devices  9.03 us (4%)
  waiting for transfers between devices  7.72 us (3%)
  other arithmetic  6.25 us (3%)
    all_to_all x6, blocking collectives, trade(): return lax.all_to_all(blocks, MESH, 0, 0, axis_index_groups=cubes(pairing))  145 us
    dot_general x2, matrix products, on_device(): jnp.dot(code_t, delta_rows, preferred_element_type=f32)  13 us
    all_to_all x1, blocking collectives, on_device(): lax.all_to_all(activations, ('x', 'yl'), split_axis=0, concat_axis=1, til...  11 us
    dot_general x2, matrix products, on_device(): lax.dot_general(delta_rows, dec_weight, (((1,), (1,)), ((), ())), preferr...  10.2 us
    ppermute x5, starting transfers between devices, swap(): return lax.ppermute(block, 'core', [(0, 1), (1, 0)])  9.03 us
    ppermute x5, waiting for transfers between devices, swap(): return lax.ppermute(block, 'core', [(0, 1), (1, 0)])  7.72 us
    dot_general x2, matrix products, on_device(): jnp.dot(rows_t, preact_grad, preferred_element_type=f32)  7.01 us
    dot_general x2, matrix products, encode(): jnp.dot(rows, enc_weight, preferred_element_type=f32) + enc_bias  5.18 us
  transfers between devices with their start and end apart: 5, of which 4 were waited for; matrix products, arithmetic and copies ran while one was open for 10% of the time, Pallas kernels for 0%

profile of v1, /device:TPU:1, one launch (start us, length us, event | category | flops | bytes accessed | tf_op | source)
XLA Modules:
  0.0 222.6 jit_solution(6513377568857615431)
XLA Ops:
  0.6 11.0 %all_to_all.43 = bf16[8,8,576]{2,1,0:T(8,128)(2,1)S(1)} all-to-all(bf16[8,8,576]{2,1,0:T(8,128)(2,1)} %bitcast.55), channel_id=1, replica_groups=mesh['z'=4,'yh'=2,'core'=2,'x'=4,'yl'=2] {'x','yl'}, dimensions={0} | all-to-all | bytes 147456 | tf_op jit(solution)/shard_map/all_to_all | solution.py:62
  11.7 0.1 reshape.47
  11.8 0.7 subtract_convert_fusion
  12.6 18.4 %all_to_all.44 = bf16[8,8,4608]{2,1,0:T(8,128)(2,1)S(1)} all-to-all(bf16[8,8,4608]{2,1,0:T(8,128)(2,1)S(1)} %broadcast_in_dim.8), channel_id=1, replica_groups={{0,2,1,3,32,34,33,35},{4,6,5,7,36,38,37,39},{16,18,17,19,48,50,49,51},{..., dimensions={0} | all-to-all | bytes 1179648 | tf_op jit(solution)/shard_map/all_to_all | solution.py:33
  31.0 0.4 broadcast_in_dim.9
  31.4 0.0 slice-start.11
  31.4 0.0 copy-start.6
  31.4 32.8 %all_to_all.45 = bf16[8,64,4608]{2,1,0:T(8,128)(2,1)S(1)} all-to-all(bf16[8,64,4608]{2,1,0:T(8,128)(2,1)S(1)} %broadcast_in_dim.9), channel_id=1, replica_groups={{0,6,17,23,96,102,113,119},{2,4,19,21,98,100,115,117},{1,7,16,22,97,103..., dimensions={0} | all-to-all | bytes 9437184 | tf_op jit(solution)/shard_map/all_to_all | solution.py:33
  64.2 3.5 %collective-permute-start = (bf16[512,4608]{1,0:T(8,128)(2,1)S(1)}, bf16[512,4608]{1,0:T(8,128)(2,1)S(1)}, u32[]{:S(2)}, u32[]{:S(2)}) collective-permute-start(bf16[512,4608]{1,0:T(8,128)(2,1)S(1)} %bitcast.35), channel_id=1, source_target_pairs={{0,8},{8,0},{1,9},{9,1},{2,10},{10,2},{3,11},{11,3},{4,12},{12,4},... | collective-permute-start | bytes 14155784 | tf_op jit(solution)/shard_map/ppermute | solution.py:37
  67.7 0.0 slice-start.4
  67.7 2.6 %convolution_add_fusion.3 = f32[512,512]{1,0:T(8,128)S(1)} fusion(bf16[512,4608]{1,0:T(8,128)(2,1)S(1)} %bitcast.36, bf16[4608,512]{1,0:T(8,128)(2,1)S(1)} %bitcast.57, f32[512]{0:T(512)S(1)} %copy-done.6), kind=kOutput, calls=%fused_computation.28 | convolution fusion | flops 2416181248 | bytes 10487808 | tf_op jit(solution)/shard_map/dot_general | solution.py:69
  70.3 0.0 slice-start.5
  70.3 4.9 %collective-permute-done = bf16[512,4608]{1,0:T(8,128)(2,1)S(1)} collective-permute-done((bf16[512,4608]{1,0:T(8,128)(2,1)S(1)}, bf16[512,4608]{1,0:T(8,128)(2,1)S(1)}, u32[]{:S(2)}, u32[]{:S(2)}) %collective-permute-start) | collective-permute-done | bytes 4718624 | tf_op jit(solution)/shard_map/ppermute | solution.py:37
  75.2 2.6 %convolution_add_fusion.2 = f32[512,512]{1,0:T(8,128)S(1)} fusion(bf16[512,4608]{1,0:T(8,128)(2,1)S(1)} %collective-permute-done, bf16[4608,512]{1,0:T(8,128)(2,1)S(1)} %bitcast.57, f32[512]{0:T(512)S(1)} %copy-done.6), kind=kOutput, calls=%fused_computation.27 | convolution fusion | flops 2416181248 | bytes 10487808 | tf_op jit(solution)/shard_map/dot_general | solution.py:69
  77.8 0.9 fusion.24
  78.8 1.0 convolution_convert_fusion.2
  79.8 0.5 collective-permute-start.1
  80.3 1.0 convolution_convert_fusion.1
  81.3 0.2 collective-permute-start.2
  81.5 1.0 convolution_convert_fusion
  82.5 0.5 collective-permute-start.3
  82.9 0.4 collective-permute-done.1
  83.3 1.0 add_convert_fusion.4
  84.3 1.2 collective-permute-done.2
  85.6 1.0 add_convert_fusion.3
  86.6 1.2 collective-permute-done.3
  87.8 1.0 add_convert_fusion.2
  88.8 0.4 pad_maximum_fusion
  89.2 33.3 %all_to_all.46 = bf16[8,64,4608]{2,1,0:T(8,128)(2,1)} all-to-all(bf16[8,64,4608]{2,1,0:T(8,128)(2,1)S(1)} %bitcast.40), channel_id=1, replica_groups={{0,6,17,23,96,102,113,119},{2,4,19,21,98,100,115,117},{1,7,16,22,97,103..., dimensions={0} | all-to-all | bytes 9437184 | tf_op jit(solution)/shard_map/all_to_all | solution.py:33
  122.5 3.1 %reduce_sum.50 = bf16[64,4608]{1,0:T(8,128)(2,1)S(1)} reduce(bf16[8,64,4608]{2,1,0:T(8,128)(2,1)} %all_to_all.46, bf16[]{:T(256)} %constant.15.clone.1), dimensions={0}, to_apply=%region_2.0 | reduce | flops 2064384 | bytes 5308418 | tf_op jit(solution)/shard_map/reduce_sum | solution.py:56
  125.6 13.6 %all_to_all.47 = bf16[8,8,4608]{2,1,0:T(8,128)(2,1)S(1)} all-to-all(bf16[8,8,4608]{2,1,0:T(8,128)(2,1)S(1)} %bitcast.50), channel_id=1, replica_groups={{0,2,1,3,32,34,33,35},{4,6,5,7,36,38,37,39},{16,18,17,19,48,50,49,51},{..., dimensions={0} | all-to-all | bytes 1179648 | tf_op jit(solution)/shard_map/all_to_all | solution.py:33
  139.2 0.1 convert_reduce_fusion
  139.3 13.6 %all_to_all.48 = bf16[8,8,4608]{2,1,0:T(8,128)(2,1)S(1)} all-to-all(bf16[8,8,4608]{2,1,0:T(8,128)(2,1)S(1)} %broadcast_in_dim.10), channel_id=1, replica_groups={{0,2,1,3,32,34,33,35},{4,6,5,7,36,38,37,39},{16,18,17,19,48,50,49,51},{..., dimensions={0} | all-to-all | bytes 1179648 | tf_op jit(solution)/shard_map/all_to_all | solution.py:33
  152.9 0.4 broadcast_in_dim.11
  153.3 0.0 slice-start.7
  153.3 33.6 %all_to_all.49 = bf16[8,64,4608]{2,1,0:T(8,128)(2,1)} all-to-all(bf16[8,64,4608]{2,1,0:T(8,128)(2,1)S(1)} %broadcast_in_dim.11), channel_id=1, replica_groups={{0,6,17,23,96,102,113,119},{2,4,19,21,98,100,115,117},{1,7,16,22,97,103..., dimensions={0} | all-to-all | bytes 9437184 | tf_op jit(solution)/shard_map/all_to_all | solution.py:33
  186.9 4.4 %collective-permute-start.4 = (bf16[512,4608]{1,0:T(8,128)(2,1)}, bf16[512,4608]{1,0:T(8,128)(2,1)}, u32[]{:S(2)}, u32[]{:S(2)}) collective-permute-start(bf16[512,4608]{1,0:T(8,128)(2,1)} %bitcast.9), channel_id=1, source_target_pairs={{0,8},{8,0},{1,9},{9,1},{2,10},{10,2},{3,11},{11,3},{4,12},{12,4},... | collective-permute-start | bytes 14155784 | tf_op jit(solution)/shard_map/ppermute | solution.py:37
  191.3 1.0 fusion
  192.3 0.0 slice-start.1
  192.3 5.2 %fusion.20 = bf16[512,512]{1,0:T(8,128)(2,1)S(1)} fusion(f32[512,512]{1,0:T(8,128)S(1)} %get-tuple-element.18, bf16[512,4608]{1,0:T(8,128)(2,1)} %bitcast.9, bf16[512,4608]{1,0:T(8,128)(2,1)S(1)} %bitcast.47, f32[512]{0:T(512)S(1)} %get-tuple-element.37), kind=kOutput, calls=%fused_computation.29 | convolution fusion | flops 2416705536 | bytes 11012096 | tf_op jit(solution)/shard_map/dot_general | solution.py:90
  197.5 0.0 slice-start.8
  197.6 2.6 %fusion.28 = f32[4608,512]{1,0:T(8,128)S(1)} fusion(bf16[4608,512]{0,1:T(8,128)(2,1)S(1)} %bitcast.39, bf16[512,512]{1,0:T(8,128)(2,1)S(1)} %fusion.20), kind=kOutput, calls=%fused_computation.48 | convolution fusion | flops 2415919104 | bytes 14680064 | tf_op jit(solution)/shard_map/dot_general | solution.py:97
  200.2 0.0 slice-start.9
  200.2 0.0 slice-start.3
  200.3 6.4 %fusion.2 = f32[512,4608]{1,0:T(8,128)S(1)} fusion(bf16[512,4608]{1,0:T(8,128)(2,1)} %param.10, bf16[512,512]{0,1:T(8,128)(2,1)S(1)} %bitcast.54, bf16[512,4608]{1,0:T(8,128)(2,1)} %bitcast.9, f32[512]{0:T(512)S(1)} %get-tuple-element.36, f32[512]{0:T(512)S(1)} %add_multiply_fusion), kind=kOutput, calls=%fused_computation.4 | convolution fusion | flops 2425356288 | bytes 19402752 | tf_op jit(solution)/shard_map/dot_general | solution.py:98
  206.7 5.0 %fusion.21 = bf16[512,512]{1,0:T(8,128)(2,1)S(1)} fusion(f32[512,512]{1,0:T(8,128)S(1)} %get-tuple-element.25, bf16[512,4608]{1,0:T(8,128)(2,1)} %collective-permute-done.4, bf16[512,4608]{1,0:T(8,128)(2,1)S(1)} %bitcast.49, f32[512]{0:T(512)S(1)} %get-tuple-element.37), kind=kOutput, calls=%fused_computation.30 | convolution fusion | flops 2416705536 | bytes 11012096 | tf_op jit(solution)/shard_map/dot_general | solution.py:90
  211.7 4.4 %add_convert_fusion.1 = bf16[4608,512]{1,0:T(8,128)(2,1)} fusion(f32[4608,512]{1,0:T(8,128)S(1)} %fusion.28, bf16[4608,512]{0,1:T(8,128)(2,1)S(1)} %bitcast.43, bf16[512,512]{1,0:T(8,128)(2,1)S(1)} %fusion.21), kind=kOutput, calls=%fused_computation.6 | convolution fusion | flops 2420637696 | bytes 19398656 | tf_op jit(solution)/shard_map/dot_general | solution.py:97
  216.0 6.6 %add_convert_fusion = bf16[512,4608]{1,0:T(8,128)(2,1)} fusion(f32[512,4608]{1,0:T(8,128)S(1)} %fusion.2, bf16[512,512]{0,1:T(8,128)(2,1)S(1)} %bitcast.53, bf16[512,4608]{1,0:T(8,128)(2,1)} %collective-permute-done.4), kind=kOutput, calls=%fused_computation.5 | convolution fusion | flops 2420637696 | bytes 19398656 | tf_op jit(solution)/shard_map/dot_general | solution.py:98
  (43 shorter events, 0.2 us)
Async XLA Ops:
  31.0 36.7 %slice-start.10 = ((s8[4718592]{0:T(1024)(128)(4,1)}), s8[4194304]{0:T(1024)(128)(4,1)S(1)}, s32[]{:S(2)}) async-start(s8[4718592]{0:T(1024)(128)(4,1)} %bitcast.56), calls=%async_computation.17 | async-start | bytes 8388608
  31.4 36.3 %slice-start.11 = ((s8[4718592]{0:T(1024)(128)(4,1)}), s8[524288]{0:T(1024)(128)(4,1)S(1)}, s32[]{:S(2)}) async-start(s8[4718592]{0:T(1024)(128)(4,1)} %bitcast.56), calls=%async_computation.18 | async-start | bytes 1048576
  31.4 36.3 %copy-start.6 = (f32[512]{0:T(512)S(1)}, f32[512]{0:T(512)}, u32[]{:S(2)}) copy-start(f32[512]{0:T(512)} %param.8) | copy-start | bytes 6148
  64.2 6.2 %copy-start = (bf16[8,64,4608]{2,1,0:T(8,128)(2,1)}, bf16[8,64,4608]{2,1,0:T(8,128)(2,1)S(1)}, u32[]{:S(2)}) copy-start(bf16[8,64,4608]{2,1,0:T(8,128)(2,1)S(1)} %all_to_all.45) | copy-start | bytes 14155780
  64.2 11.1 %collective-permute-start = (bf16[512,4608]{1,0:T(8,128)(2,1)S(1)}, bf16[512,4608]{1,0:T(8,128)(2,1)S(1)}, u32[]{:S(2)}, u32[]{:S(2)}) collective-permute-start(bf16[512,4608]{1,0:T(8,128)(2,1)S(1)} %bitcast.35), channel_id=1, source_target_pairs={{0,8},{8,0},{1,9},{9,1},{2,10},{10,2},{3,11},{11,3},{4,12},{12,4},... | collective-permute-start | bytes 14155784 | tf_op jit(solution)/shard_map/ppermute | solution.py:37
  67.7 11.1 %slice-start.4 = ((s8[4718592]{0:T(1024)(128)(4,1)}), s8[4194304]{0:T(1024)(128)(4,1)S(1)}, s32[]{:S(2)}) async-start(s8[4718592]{0:T(1024)(128)(4,1)} %bitcast.44), calls=%async_computation.11 | async-start | bytes 8388608
  70.3 7.5 %copy-start.5 = (f32[512]{0:T(512)S(1)}, f32[512]{0:T(512)}, u32[]{:S(2)}) copy-start(f32[512]{0:T(512)} %param.9) | copy-start | bytes 6148
  70.3 8.5 %slice-start.5 = ((s8[4718592]{0:T(1024)(128)(4,1)}), s8[524288]{0:T(1024)(128)(4,1)S(1)}, s32[]{:S(2)}) async-start(s8[4718592]{0:T(1024)(128)(4,1)} %bitcast.44), calls=%async_computation.12 | async-start | bytes 1048576
  75.2 2.6 %copy-start.1 = (bf16[512,4608]{1,0:T(8,128)(2,1)}, bf16[512,4608]{1,0:T(8,128)(2,1)S(1)}, u32[]{:S(2)}) copy-start(bf16[512,4608]{1,0:T(8,128)(2,1)S(1)} %collective-permute-done) | copy-start | bytes 14155780
  78.8 9.0 %copy-start.2 = (bf16[512,512]{1,0:T(8,128)(2,1)}, bf16[512,512]{1,0:T(8,128)(2,1)S(1)}, u32[]{:S(2)}) copy-start(bf16[512,512]{1,0:T(8,128)(2,1)S(1)} %get-tuple-element.16) | copy-start | bytes 1572868
  79.8 3.5 %collective-permute-start.1 = (bf16[512,1536]{1,0:T(8,128)(2,1)S(1)}, bf16[512,1536]{1,0:T(8,128)(2,1)S(1)}, u32[]{:S(2)}, u32[]{:S(2)}) collective-permute-start(bf16[512,1536]{1,0:T(8,128)(2,1)S(1)} %convolution_convert_fusion.2), channel_id=1, source_target_pairs={{0,8},{8,0},{1,9},{9,1},{2,10},{10,2},{3,11},{11,3},{4,12},{12,4},... | collective-permute-start | bytes 4718600 | tf_op jit(solution)/shard_map/ppermute | solution.py:37
  81.3 4.3 %collective-permute-start.2 = (bf16[512,1536]{1,0:T(8,128)(2,1)S(1)}, bf16[512,1536]{1,0:T(8,128)(2,1)S(1)}, u32[]{:S(2)}, u32[]{:S(2)}) collective-permute-start(bf16[512,1536]{1,0:T(8,128)(2,1)S(1)} %convolution_convert_fusion.1), channel_id=1, source_target_pairs={{0,8},{8,0},{1,9},{9,1},{2,10},{10,2},{3,11},{11,3},{4,12},{12,4},... | collective-permute-start | bytes 4718600 | tf_op jit(solution)/shard_map/ppermute | solution.py:37
  82.5 5.3 %collective-permute-start.3 = (bf16[512,1536]{1,0:T(8,128)(2,1)S(1)}, bf16[512,1536]{1,0:T(8,128)(2,1)S(1)}, u32[]{:S(2)}, u32[]{:S(2)}) collective-permute-start(bf16[512,1536]{1,0:T(8,128)(2,1)S(1)} %convolution_convert_fusion), channel_id=1, source_target_pairs={{0,8},{8,0},{1,9},{9,1},{2,10},{10,2},{3,11},{11,3},{4,12},{12,4},... | collective-permute-start | bytes 4718600 | tf_op jit(solution)/shard_map/ppermute | solution.py:37
  122.5 16.8 %copy-start.4 = (f32[4608]{0:T(1024)S(1)}, f32[4608]{0:T(1024)}, u32[]{:S(2)}) copy-start(f32[4608]{0:T(1024)} %param.11) | copy-start | bytes 55300
  152.9 38.3 %slice-start.6 = ((s8[4718592]{0:T(1024)(128)(4,1)}), s8[4194304]{0:T(1024)(128)(4,1)S(1)}, s32[]{:S(2)}) async-start(s8[4718592]{0:T(1024)(128)(4,1)} %bitcast.46), calls=%async_computation.13 | async-start | bytes 8388608
  153.3 38.0 %slice-start.7 = ((s8[4718592]{0:T(1024)(128)(4,1)}), s8[524288]{0:T(1024)(128)(4,1)S(1)}, s32[]{:S(2)}) async-start(s8[4718592]{0:T(1024)(128)(4,1)} %bitcast.46), calls=%async_computation.14 | async-start | bytes 1048576
  186.9 19.8 %collective-permute-start.4 = (bf16[512,4608]{1,0:T(8,128)(2,1)}, bf16[512,4608]{1,0:T(8,128)(2,1)}, u32[]{:S(2)}, u32[]{:S(2)}) collective-permute-start(bf16[512,4608]{1,0:T(8,128)(2,1)} %bitcast.9), channel_id=1, source_target_pairs={{0,8},{8,0},{1,9},{9,1},{2,10},{10,2},{3,11},{11,3},{4,12},{12,4},... | collective-permute-start | bytes 14155784 | tf_op jit(solution)/shard_map/ppermute | solution.py:37
  191.3 6.2 %slice-start = ((s8[4718592]{0:T(1024)(128)(4,1)}), s8[4194304]{0:T(1024)(128)(4,1)S(1)}, s32[]{:S(2)}) async-start(s8[4718592]{0:T(1024)(128)(4,1)} %bitcast.37), calls=%async_computation.7 | async-start | bytes 8388608
  192.3 5.2 %slice-start.1 = ((s8[4718592]{0:T(1024)(128)(4,1)}), s8[524288]{0:T(1024)(128)(4,1)S(1)}, s32[]{:S(2)}) async-start(s8[4718592]{0:T(1024)(128)(4,1)} %bitcast.37), calls=%async_computation.8 | async-start | bytes 1048576
  197.5 2.7 %copy-start.3 = (bf16[512,512]{1,0:T(8,128)(2,1)S(1)}, bf16[512,512]{1,0:T(8,128)(2,1)}, u32[]{:S(2)}) copy-start(bf16[512,512]{1,0:T(8,128)(2,1)} %copy-done.2) | copy-start | bytes 1572868
  197.5 9.1 %slice-start.8 = ((s8[4718592]{0:T(1024)(128)(4,1)}), s8[524288]{0:T(1024)(128)(4,1)S(1)}, s32[]{:S(2)}) async-start(s8[4718592]{0:T(1024)(128)(4,1)} %bitcast.48), calls=%async_computation.15 | async-start | bytes 1048576
  197.6 14.1 %slice-start.2 = ((s8[4718592]{0:T(1024)(128)(4,1)}), s8[4194304]{0:T(1024)(128)(4,1)S(1)}, s32[]{:S(2)}) async-start(s8[4718592]{0:T(1024)(128)(4,1)} %bitcast.41), calls=%async_computation.9 | async-start | bytes 8388608
  200.2 6.4 %slice-start.9 = ((s8[4718592]{0:T(1024)(128)(4,1)}), s8[4194304]{0:T(1024)(128)(4,1)S(1)}, s32[]{:S(2)}) async-start(s8[4718592]{0:T(1024)(128)(4,1)} %bitcast.48), calls=%async_computation.16 | async-start | bytes 8388608
  200.2 11.4 %slice-start.3 = ((s8[4718592]{0:T(1024)(128)(4,1)}), s8[524288]{0:T(1024)(128)(4,1)S(1)}, s32[]{:S(2)}) async-start(s8[4718592]{0:T(1024)(128)(4,1)} %bitcast.41), calls=%async_computation.10 | async-start | bytes 1048576

commit v2 on v1

v2 whole, which is shorter than its diff:
```python
import math

import jax
import jax.numpy as jnp
from jax import lax
from jax.sharding import Mesh, PartitionSpec as P

band_width = 0.1
sparsity_coeff = 0.5

bf16, f32 = jnp.bfloat16, jnp.float32
MESH = ("z", "yh", "core", "x", "yl")


def device(z, y, x, core):
    return (((z * 2 + y // 2) * 2 + core) * 4 + x) * 2 + y % 2


def receive(block, axes, pairing):
    pairs = []
    for z in range(4):
        for y in range(4):
            for x in range(4):
                for core in range(2):
                    partner = {"z": z, "y": y, "x": x}
                    for axis in axes:
                        partner[axis] ^= (1, 3)[(pairing + core) % 2]
                    pairs.append((device(core=core, **partner), device(z, y, x, core)))
    return lax.ppermute(block, MESH, pairs)


def cubes(pairing):
    groups = []
    for core in range(2):
        step = (1, 3)[(pairing + core) % 2]
        corners = (0, 1 if step == 3 else 2)
        pairs = [(corner, corner ^ step) for corner in corners]
        for zs in pairs:
            for ys in pairs:
                for xs in pairs:
                    groups.append([device(z, y, x, core) for z in zs for y in ys for x in xs])
    return groups


def trade(blocks, pairing):
    return lax.all_to_all(blocks, MESH, 0, 0, axis_index_groups=cubes(pairing))


def swap(block):
    return lax.ppermute(block, "core", [(0, 1), (1, 0)])


def barrier(*arrays):
    return lax.optimization_barrier(arrays)


def add(*blocks):
    return sum(block.astype(f32) for block in blocks)


def flat(block):
    return block.reshape(-1, block.shape[-1])


def gather(own, work):
    copies, = barrier(jnp.broadcast_to(own, (8, *own.shape)))
    block, = barrier(trade(copies, 0))
    x, y, z, xyz = (receive(block, corner, 1) for corner in ("x", "y", "z", "xyz"))
    near, = barrier(jnp.concatenate([block, x, y, z]))
    xy, yz, zx = receive(y, "x", 1), receive(z, "y", 1), receive(x, "z", 1)
    near, = barrier(jnp.concatenate([near, swap(near)]))
    near = flat(near)
    done = work(near)
    xy, yz, zx, xyz, _ = barrier(xy, yz, zx, xyz, done)
    distant, = barrier(jnp.concatenate([xy, yz, zx, xyz]))
    return near, done, flat(distant), flat(swap(distant))


def scatter(near, distant, work):
    xy, yz, zx, xyz = jnp.split(distant.reshape(32, 8, -1), 4)
    own, x, y, z = jnp.split(near.reshape(32, 8, -1), 4)
    y_more, z_more, x_more = receive(xy, "x", 1), receive(yz, "y", 1), receive(zx, "z", 1)
    xyz = receive(xyz, "xyz", 1)
    x, y, z = (add(*pair).astype(bf16) for pair in ((x, x_more), (y, y_more), (z, z_more)))
    x, y, z = receive(x, "x", 1), receive(y, "y", 1), receive(z, "z", 1)
    x, y, z, xyz, done = barrier(x, y, z, xyz, work)
    blocks = trade(add(own, xyz, x, y, z).astype(bf16), 0)
    return jnp.sum(blocks.astype(f32), axis=0), done


def on_device(activations, enc_weight, enc_bias, thresholds, dec_weight, dec_bias):
    row_scale = 1.0 / math.sqrt(1024)
    own_rows = lax.all_to_all(activations, ("x", "yl"), split_axis=0, concat_axis=1, tiled=True)
    own_rows = own_rows.astype(f32)
    row_norms = jnp.sqrt(jnp.sum(jnp.square(dec_weight.astype(f32)), axis=1) + 1e-06)
    own_centered, = barrier((own_rows - dec_bias).astype(bf16))

    def encode(rows):
        pre_act, = barrier(jnp.dot(rows, enc_weight, preferred_element_type=f32) + enc_bias)
        gating = jax.nn.sigmoid((pre_act - thresholds) / band_width)
        code_values = pre_act * gating
        slopes = gating + pre_act * gating * (1.0 - gating) / band_width
        return barrier(code_values.astype(bf16), slopes, jnp.sum(code_values, axis=0))

    near, encoded, mine, theirs = gather(own_centered, encode)
    code_near, slopes_near, totals_near = encoded
    code_mine, slopes_mine, totals_mine = encode(mine)
    code_theirs, slopes_theirs, totals_theirs = encode(theirs)
    totals = totals_near + totals_mine + totals_theirs

    code_mine_all, code_theirs_all = barrier(
        jnp.concatenate([code_mine, code_near[:256]]),
        jnp.concatenate([code_theirs, code_near[256:]]),
    )
    recon_theirs = jnp.dot(code_theirs_all, dec_weight, preferred_element_type=f32).astype(bf16)
    recon_theirs = swap(recon_theirs[:256]), swap(recon_theirs[256:])
    recon_mine, = barrier(
        jnp.dot(code_mine_all, dec_weight, preferred_element_type=f32).astype(bf16)
    )
    recon_distant, = barrier(add(recon_mine[:256], recon_theirs[0]).astype(bf16))
    recon_mine, recon_distant = barrier(recon_mine, recon_distant)
    recon_near = add(recon_mine[256:], recon_theirs[1]).astype(bf16)
    near_t, code_near_t, distant_t, code_distant_t = (
        near.T,
        code_near.T,
        jnp.concatenate([mine, theirs]).T,
        jnp.concatenate([code_mine, code_theirs]).T,
    )
    slopes_distant = jnp.concatenate([slopes_mine, slopes_theirs])
    recon, (near_t, code_near_t, distant_t, code_distant_t, slopes_distant) = scatter(
        recon_near, recon_distant, (near_t, code_near_t, distant_t, code_distant_t, slopes_distant)
    )
    recon_error = recon + dec_bias - own_rows
    own_delta, = barrier((recon_error * row_scale).astype(bf16))

    def preact_grad(delta, slopes):
        code_grad = lax.dot_general(
            delta, dec_weight, (((1,), (1,)), ((), ())), preferred_element_type=f32
        )
        return barrier(
            ((code_grad + sparsity_coeff * row_scale * row_norms) * slopes).astype(bf16)
        )[0]

    def near_grad(delta):
        return jnp.dot(near_t, preact_grad(delta, slopes_near), preferred_element_type=f32)

    delta_near, grad_enc, mine, theirs = gather(own_delta, near_grad)
    grad_dec = jnp.dot(code_near_t, delta_near, preferred_element_type=f32)
    grad_dec = (
        grad_dec
        + sparsity_coeff
        * row_scale
        * totals[:, None]
        * dec_weight.astype(f32)
        / row_norms[:, None]
    )
    grad_dec, = barrier(grad_dec)
    theirs, _ = barrier(theirs, grad_dec)
    delta, = barrier(jnp.concatenate([mine, theirs]))
    preact = preact_grad(delta, slopes_distant)
    grad_enc = grad_enc + jnp.dot(distant_t, preact, preferred_element_type=f32)
    grad_dec = grad_dec + jnp.dot(code_distant_t, delta, preferred_element_type=f32)
    return (grad_enc.astype(bf16), grad_dec.astype(bf16))


def solution(mesh):
    torus = Mesh(mesh.devices.reshape(4, 2, 2, 4, 2), MESH)
    dp, tensor = ("z", "yh", "core"), ("x", "yl")
    latents = dp + tensor
    in_specs = (P(dp, tensor), P(None, latents), P(latents), P(latents), P(latents, None), P())
    out_specs = (P(None, latents), P(latents, None))
    return jax.shard_map(
        on_device, mesh=torus, in_specs=in_specs, out_specs=out_specs, check_vma=False
    )
```

time: 223 us -> 204 us (0.915)
  blocking collectives: 156 us -> 59.3 us
  waiting for transfers between devices: 7.72 us -> 53.3 us
  starting transfers between devices: 9.03 us -> 30.4 us
  other arithmetic: 6.25 us -> 17.4 us
  matrix products: 41.3 us -> 38.9 us
  local copies, waits for them, and re-layouts: 1.06 us -> 3.37 us
    all_to_all x6 -> x3, blocking collectives: 145 us -> 48.3 us  [trade(): return lax.all_to_all(blocks, MESH, 0, 0, axis_index_groups=cubes(pairing))]
    ppermute x0 -> x21, waiting for transfers between devices: none -> 50.1 us  [receive(): return lax.ppermute(block, MESH, pairs)]
    ppermute x0 -> x21, starting transfers between devices: none -> 12.1 us  [receive(): return lax.ppermute(block, MESH, pairs)]
    ppermute x5 -> x6, starting transfers between devices: 9.03 us -> 18.3 us  [swap(): return lax.ppermute(block, 'core', [(0, 1), (1, 0)])]
    concatenate x1 -> x8, other arithmetic: 0.36 us -> 6.36 us  [the longest x2 2.19 us: gather(): distant, = barrier(jnp.concatenate([xy, yz, zx, xyz]))]
    ppermute x5 -> x6, waiting for transfers between devices: 7.72 us -> 3.12 us  [swap(): return lax.ppermute(block, 'core', [(0, 1), (1, 0)])]
    convert_element_type x0 -> x5, other arithmetic: none -> 3.23 us  [the longest x1 1.43 us: scatter(): blocks = trade(add(own, xyz, x, y, z).astype(bf16), 0)]
    reduce_sum x2 -> x1, other arithmetic: 3.15 us -> 0.08 us  [scatter(): return (jnp.sum(blocks.astype(f32), axis=0), done)]
  transfers between devices with their start and end apart: 5 -> 27, of which waited for: 4 -> 15; matrix products, arithmetic and copies ran while one was open for 10% -> 13% of each run, Pallas kernels for 0% -> 0%
where the time goes in v2:
time: 204 us
  blocking collectives  59.3 us (29%)
  waiting for transfers between devices  53.3 us (26%)
  matrix products  38.9 us (19%)
  starting transfers between devices  30.4 us (15%)
  other arithmetic  17.4 us (9%)
  local copies, waits for them, and re-layouts  3.37 us (2%)
    ppermute x21, waiting for transfers between devices, receive(): return lax.ppermute(block, MESH, pairs)  50.1 us
    all_to_all x3, blocking collectives, trade(): return lax.all_to_all(blocks, MESH, 0, 0, axis_index_groups=cubes(pairing))  48.3 us
    ppermute x6, starting transfers between devices, swap(): return lax.ppermute(block, 'core', [(0, 1), (1, 0)])  18.3 us
    ppermute x21, starting transfers between devices, receive(): return lax.ppermute(block, MESH, pairs)  12.1 us
    all_to_all x1, blocking collectives, on_device(): lax.all_to_all(activations, ('x', 'yl'), split_axis=0, concat_axis=1, til...  11 us
    dot_general x2, matrix products, preact_grad(): lax.dot_general(delta, dec_weight, (((1,), (1,)), ((), ())), preferred_el...  8.58 us
    dot_general x1, matrix products, on_device(): jnp.dot(code_distant_t, delta, preferred_element_type=f32)  6.75 us
    dot_general x1, matrix products, on_device(): grad_dec = jnp.dot(code_near_t, delta_near, preferred_element_type=f32)  5.42 us
  transfers between devices with their start and end apart: 27, of which 15 were waited for; matrix products, arithmetic and copies ran while one was open for 13% of the time, Pallas kernels for 0%

profile of v2, /device:TPU:1, one launch (start us, length us, event | category | flops | bytes accessed | tf_op | source)
XLA Modules:
  0.0 203.8 jit_solution(11104397638127938675)
XLA Ops:
  0.6 11.0 %all_to_all.28 = bf16[8,8,576]{2,1,0:T(8,128)(2,1)S(1)} all-to-all(bf16[8,8,576]{2,1,0:T(8,128)(2,1)} %bitcast.89), channel_id=1, replica_groups=mesh['z'=4,'yh'=2,'core'=2,'x'=4,'yl'=2] {'x','yl'}, dimensions={0} | all-to-all | bytes 147456 | tf_op jit(solution)/shard_map/all_to_all | solution.py:93
  11.8 0.8 subtract_convert_fusion
  12.6 18.4 %all_to_all.29 = bf16[8,8,4608]{2,1,0:T(8,128)(2,1)S(1)} all-to-all(bf16[8,8,4608]{2,1,0:T(8,128)(2,1)S(1)} %broadcast_in_dim.4), channel_id=1, replica_groups={{0,2,1,3,32,34,33,35},{4,6,5,7,36,38,37,39},{16,18,17,19,48,50,49,51},{..., dimensions={0} | all-to-all | bytes 1179648 | tf_op jit(solution)/shard_map/all_to_all | solution.py:46
  31.0 9.0 %collective-permute-done.4 = bf16[8,8,4608]{2,1,0:T(8,128)(2,1)S(1)} collective-permute-done((bf16[8,8,4608]{2,1,0:T(8,128)(2,1)S(1)}, bf16[8,8,4608]{2,1,0:T(8,128)(2,1)S(1)}, u32[]{:S(2)}, u32[]{:S(2)}) %collective-permute-start.4) | collective-permute-done | bytes 589856 | tf_op jit(solution)/shard_map/ppermute | solution.py:29
  40.4 1.7 collective-permute-start.7
  42.9 2.1 %collective-permute-start.3 = (bf16[8,8,4608]{2,1,0:T(8,128)(2,1)S(1)}, bf16[8,8,4608]{2,1,0:T(8,128)(2,1)S(1)}, u32[]{:S(2)}, u32[]{:S(2)}) collective-permute-start(bf16[8,8,4608]{2,1,0:T(8,128)(2,1)S(1)} %collective-permute-done.2), channel_id=1, source_target_pairs={{17,0},{9,8},{19,2},{11,10},{21,4},{13,12},{23,6},{15,14},{16,1},{... | collective-permute-start | bytes 1769480 | tf_op jit(solution)/shard_map/ppermute | solution.py:29
  45.1 0.9 collective-permute-start.1
  46.7 2.6 %fusion.8 = f32[512,512]{1,0:T(8,128)S(1)} fusion(bf16[4608,512]{1,0:T(8,128)(2,1)S(1)} %bitcast.91, bf16[64,8,4608]{2,1,0:T(8,128)(2,1)S(1)} %pad_maximum_fusion, f32[512]{0:T(512)S(1)} %copy-done.15), kind=kOutput, calls=%fused_computation.24 | convolution fusion | flops 2416181248 | bytes 10487808 | tf_op jit(solution)/shard_map/dot_general | solution.py:99
  49.4 1.4 fusion.37
  50.8 2.2 %collective-permute-done.6 = bf16[8,8,4608]{2,1,0:T(8,128)(2,1)S(1)} collective-permute-done((bf16[8,8,4608]{2,1,0:T(8,128)(2,1)S(1)}, bf16[8,8,4608]{2,1,0:T(8,128)(2,1)S(1)}, u32[]{:S(2)}, u32[]{:S(2)}) %collective-permute-start.6) | collective-permute-done | bytes 589856 | tf_op jit(solution)/shard_map/ppermute | solution.py:29
  53.0 5.0 %collective-permute-done.5 = bf16[8,8,4608]{2,1,0:T(8,128)(2,1)S(1)} collective-permute-done((bf16[8,8,4608]{2,1,0:T(8,128)(2,1)S(1)}, bf16[8,8,4608]{2,1,0:T(8,128)(2,1)S(1)}, u32[]{:S(2)}, u32[]{:S(2)}) %collective-permute-start.5) | collective-permute-done | bytes 589856 | tf_op jit(solution)/shard_map/ppermute | solution.py:29
  58.0 0.7 collective-permute-done.3
  59.0 4.5 %collective-permute-start.8 = (bf16[32,8,4608]{2,1,0:T(8,128)(2,1)S(1)}, bf16[32,8,4608]{2,1,0:T(8,128)(2,1)S(1)}, u32[]{:S(2)}, u32[]{:S(2)}) collective-permute-start(bf16[32,8,4608]{2,1,0:T(8,128)(2,1)S(1)} %pad_maximum_fusion.4), channel_id=1, source_target_pairs={{0,8},{8,0},{1,9},{9,1},{2,10},{10,2},{3,11},{11,3},{4,12},{12,4},... | collective-permute-start | bytes 7077896 | tf_op jit(solution)/shard_map/ppermute | solution.py:50
  63.4 1.4 convolution_add_fusion.2
  64.9 2.7 %collective-permute-done.8 = bf16[32,8,4608]{2,1,0:T(8,128)(2,1)S(1)} collective-permute-done((bf16[32,8,4608]{2,1,0:T(8,128)(2,1)S(1)}, bf16[32,8,4608]{2,1,0:T(8,128)(2,1)S(1)}, u32[]{:S(2)}, u32[]{:S(2)}) %collective-permute-start.8) | collective-permute-done | bytes 2359328 | tf_op jit(solution)/shard_map/ppermute | solution.py:50
  67.6 1.4 convolution_add_fusion.1
  69.0 1.1 fusion.33
  70.0 0.9 fusion.28
  70.9 2.8 %convolution_convert_fusion = bf16[512,4608]{1,0:T(8,128)(2,1)S(1)} fusion(bf16[512,512]{1,0:T(8,128)(2,1)S(1)} %get-tuple-element.43, bf16[512,4608]{1,0:T(8,128)(2,1)S(1)} %bitcast.83), kind=kOutput, calls=%fused_computation.7 | convolution fusion | flops 2418278400 | bytes 9961472 | tf_op jit(solution)/shard_map/dot_general | solution.py:115
  74.5 2.8 %convolution_convert_fusion.1 = bf16[512,4608]{1,0:T(8,128)(2,1)S(1)} fusion(bf16[512,512]{1,0:T(8,128)(2,1)S(1)} %get-tuple-element.42, bf16[512,4608]{1,0:T(8,128)(2,1)S(1)} %bitcast.83), kind=kOutput, calls=%fused_computation.8 | convolution fusion | flops 2418278400 | bytes 9961472 | tf_op jit(solution)/shard_map/dot_general | solution.py:118
  77.6 1.0 pad_maximum_fusion.7
  79.8 1.1 collective-permute-start.13
  80.9 2.6 %collective-permute-start.11 = (bf16[8,8,4608]{2,1,0:T(8,128)(2,1)S(1)}, bf16[8,8,4608]{2,1,0:T(8,128)(2,1)S(1)}, u32[]{:S(2)}, u32[]{:S(2)}) collective-permute-start(bf16[8,8,4608]{2,1,0:T(8,128)(2,1)S(1)} %get-tuple-element.71), channel_id=1, source_target_pairs={{96,0},{40,8},{98,2},{42,10},{100,4},{44,12},{102,6},{46,14},{97,1... | collective-permute-start | bytes 1769480 | tf_op jit(solution)/shard_map/ppermute | solution.py:29
  84.1 10.5 %collective-permute-done.15 = bf16[8,8,4608]{2,1,0:T(8,128)(2,1)S(1)} collective-permute-done((bf16[8,8,4608]{2,1,0:T(8,128)(2,1)S(1)}, bf16[8,8,4608]{2,1,0:T(8,128)(2,1)S(1)}, u32[]{:S(2)}, u32[]{:S(2)}) %collective-permute-start.15) | collective-permute-done | bytes 589856 | tf_op jit(solution)/shard_map/ppermute | solution.py:29
  94.6 2.4 %collective-permute-done.11 = bf16[8,8,4608]{2,1,0:T(8,128)(2,1)S(1)} collective-permute-done((bf16[8,8,4608]{2,1,0:T(8,128)(2,1)S(1)}, bf16[8,8,4608]{2,1,0:T(8,128)(2,1)S(1)}, u32[]{:S(2)}, u32[]{:S(2)}) %collective-permute-start.11) | collective-permute-done | bytes 589856 | tf_op jit(solution)/shard_map/ppermute | solution.py:29
  97.8 2.0 maximum_bitcast_fusion
  99.8 6.4 %collective-permute-done.16 = bf16[8,8,4608]{2,1,0:T(8,128)(2,1)S(1)} collective-permute-done((bf16[8,8,4608]{2,1,0:T(8,128)(2,1)S(1)}, bf16[8,8,4608]{2,1,0:T(8,128)(2,1)S(1)}, u32[]{:S(2)}, u32[]{:S(2)}) %collective-permute-start.16) | collective-permute-done | bytes 589856 | tf_op jit(solution)/shard_map/ppermute | solution.py:29
  106.8 1.4 fusion.23
  108.2 16.3 %all_to_all.30 = bf16[8,8,4608]{2,1,0:T(8,128)(2,1)S(1)} all-to-all(bf16[8,8,4608]{2,1,0:T(8,128)(2,1)S(1)} %fusion.23), channel_id=1, replica_groups={{0,2,1,3,32,34,33,35},{4,6,5,7,36,38,37,39},{16,18,17,19,48,50,49,51},{..., dimensions={0} | all-to-all | bytes 1179648 | tf_op jit(solution)/shard_map/all_to_all | solution.py:46
  124.7 13.6 %all_to_all.31 = bf16[8,8,4608]{2,1,0:T(8,128)(2,1)S(1)} all-to-all(bf16[8,8,4608]{2,1,0:T(8,128)(2,1)S(1)} %broadcast_in_dim.5), channel_id=1, replica_groups={{0,2,1,3,32,34,33,35},{4,6,5,7,36,38,37,39},{16,18,17,19,48,50,49,51},{..., dimensions={0} | all-to-all | bytes 1179648 | tf_op jit(solution)/shard_map/all_to_all | solution.py:46
  138.3 9.1 %collective-permute-done.20 = bf16[8,8,4608]{2,1,0:T(8,128)(2,1)} collective-permute-done((bf16[8,8,4608]{2,1,0:T(8,128)(2,1)S(1)}, bf16[8,8,4608]{2,1,0:T(8,128)(2,1)}, u32[]{:S(2)}, u32[]{:S(2)}) %collective-permute-start.20) | collective-permute-done | bytes 589856 | tf_op jit(solution)/shard_map/ppermute | solution.py:29
  147.4 1.7 pad_maximum_fusion.5
  149.1 6.8 %collective-permute-start.21 = (bf16[32,8,4608]{2,1,0:T(8,128)(2,1)S(1)}, bf16[32,8,4608]{2,1,0:T(8,128)(2,1)S(1)}, u32[]{:S(2)}, u32[]{:S(2)}) collective-permute-start(bf16[32,8,4608]{2,1,0:T(8,128)(2,1)S(1)} %pad_maximum_fusion.5), channel_id=1, source_target_pairs={{0,8},{8,0},{1,9},{9,1},{2,10},{10,2},{3,11},{11,3},{4,12},{12,4},... | collective-permute-start | bytes 7077896 | tf_op jit(solution)/shard_map/ppermute | solution.py:50
  156.0 1.0 fusion
  157.6 1.3 collective-permute-start.25
  159.5 1.1 collective-permute-start.22
  160.6 0.9 collective-permute-start.24
  161.9 2.2 %copy-done = bf16[64,8,4608]{2,1,0:T(8,128)(2,1)} copy-done((bf16[64,8,4608]{2,1,0:T(8,128)(2,1)}, bf16[64,8,4608]{2,1,0:T(8,128)(2,1)S(1)}, u32[]{:S(2)}) %copy-start) | copy-done | bytes 4718616
  164.0 3.9 %fusion.17 = bf16[512,512]{1,0:T(8,128)(2,1)S(1)} fusion(f32[512,512]{1,0:T(8,128)} %get-tuple-element.34, bf16[512,4608]{1,0:T(8,128)(2,1)S(1)} %bitcast.83, bf16[64,8,4608]{2,1,0:T(8,128)(2,1)S(1)} %pad_maximum_fusion.1, f32[512]{0:T(512)} %get-tuple-element.88), kind=kOutput, calls=%fused_computation.28 | convolution fusion | flops 2416705536 | bytes 11012096 | tf_op jit(solution)/shard_map/dot_general | solution.py:137
  168.0 2.6 %fusion.41 = f32[4608,512]{1,0:T(8,128)S(1)} fusion(bf16[4608,512]{0,1:T(8,128)(2,1)S(1)} %bitcast.79, bf16[512,512]{1,0:T(8,128)(2,1)S(1)} %fusion.17), kind=kOutput, calls=%fused_computation.82 | convolution fusion | flops 2415919104 | bytes 14680064 | tf_op jit(solution)/shard_map/dot_general | solution.py:145
  170.7 3.6 %collective-permute-done.23 = bf16[8,8,4608]{2,1,0:T(8,128)(2,1)} collective-permute-done((bf16[8,8,4608]{2,1,0:T(8,128)(2,1)}, bf16[8,8,4608]{2,1,0:T(8,128)(2,1)}, u32[]{:S(2)}, u32[]{:S(2)}) %collective-permute-start.23) | collective-permute-done | bytes 589856 | tf_op jit(solution)/shard_map/ppermute | solution.py:29
  174.3 0.7 collective-permute-done.24
  174.9 1.9 pad_maximum_fusion.6
  176.8 4.6 %collective-permute-start.26 = (bf16[32,8,4608]{2,1,0:T(8,128)(2,1)S(1)}, bf16[32,8,4608]{2,1,0:T(8,128)(2,1)S(1)}, u32[]{:S(2)}, u32[]{:S(2)}) collective-permute-start(bf16[32,8,4608]{2,1,0:T(8,128)(2,1)S(1)} %pad_maximum_fusion.6), channel_id=1, source_target_pairs={{0,8},{8,0},{1,9},{9,1},{2,10},{10,2},{3,11},{11,3},{4,12},{12,4},... | collective-permute-start | bytes 7077896 | tf_op jit(solution)/shard_map/ppermute | solution.py:50
  181.5 5.4 %fusion.2 = f32[512,4608]{1,0:T(8,128)} fusion(bf16[512,4608]{1,0:T(8,128)(2,1)S(1)} %bitcast.85, bf16[512,512]{0,1:T(8,128)(2,1)S(1)} %bitcast.88, bf16[64,8,4608]{2,1,0:T(8,128)(2,1)S(1)} %copy-done.1, f32[512]{0:T(512)S(1)} %copy-done.14, f32[512]{0:T(512)S(1)} %add_multiply_fusion), kind=kOutput, calls=%fused_computation.4 | convolution fusion | flops 2425356288 | bytes 19402752 | tf_op jit(solution)/shard_map/dot_general | solution.py:148
  187.6 4.7 %convolution_add_fusion = f32[512,512]{1,0:T(8,128)S(1)} fusion(bf16[512,4608]{1,0:T(8,128)(2,1)S(1)} %pad_maximum_fusion.2, bf16[512,4608]{1,0:T(8,128)(2,1)} %param.10, f32[512]{0:T(512)S(1)} %copy-done.13), kind=kOutput, calls=%fused_computation.27 | convolution fusion | flops 2416181248 | bytes 10487808 | tf_op jit(solution)/shard_map/dot_general | solution.py:137
  192.3 6.8 %add_convert_fusion = bf16[512,4608]{1,0:T(8,128)(2,1)} fusion(f32[512,4608]{1,0:T(8,128)} %fusion.2, bf16[512,512]{0,1:T(8,128)(2,1)S(1)} %copy-done.4, bf16[512,4608]{1,0:T(8,128)(2,1)S(1)} %pad_maximum_fusion.2), kind=kOutput, calls=%fused_computation.5 | convolution fusion | flops 2420637696 | bytes 19398656 | tf_op jit(solution)/shard_map/dot_general | solution.py:162
  199.3 4.5 %add_convert_fusion.1 = bf16[4608,512]{1,0:T(8,128)(2,1)} fusion(f32[4608,512]{1,0:T(8,128)S(1)} %fusion.41, bf16[4608,512]{0,1:T(8,128)(2,1)S(1)} %maximum_bitcast_fusion, bf16[512,512]{1,0:T(8,128)(2,1)S(1)} %multiply_convert_fusion), kind=kOutput, calls=%fused_computation.6 | convolution fusion | flops 2420637696 | bytes 19398656 | tf_op jit(solution)/shard_map/dot_general | solution.py:161
  (99 shorter events, 9.3 us)
Async XLA Ops:
  11.8 34.9 %copy-start.7 = (f32[8,4608]{1,0:T(8,128)}, f32[8,4608]{1,0:T(8,128)S(1)}, u32[]{:S(2)}) copy-start(f32[8,4608]{1,0:T(8,128)S(1)} %reshape.65) | copy-start | bytes 442372
  31.0 9.0 %collective-permute-start.4 = (bf16[8,8,4608]{2,1,0:T(8,128)(2,1)S(1)}, bf16[8,8,4608]{2,1,0:T(8,128)(2,1)S(1)}, u32[]{:S(2)}, u32[]{:S(2)}) collective-permute-start(bf16[8,8,4608]{2,1,0:T(8,128)(2,1)S(1)} %all_to_all.29), channel_id=1, source_target_pairs={{6,0},{10,8},{4,2},{8,10},{2,4},{14,12},{0,6},{12,14},{7,1},{11,9}... | collective-permute-start | bytes 1769480 | tf_op jit(solution)/shard_map/ppermute | solution.py:29
  31.0 9.0 %collective-permute-start.2 = (bf16[8,8,4608]{2,1,0:T(8,128)(2,1)S(1)}, bf16[8,8,4608]{2,1,0:T(8,128)(2,1)S(1)}, u32[]{:S(2)}, u32[]{:S(2)}) collective-permute-start(bf16[8,8,4608]{2,1,0:T(8,128)(2,1)S(1)} %all_to_all.29), channel_id=1, source_target_pairs={{96,0},{40,8},{98,2},{42,10},{100,4},{44,12},{102,6},{46,14},{97,1... | collective-permute-start | bytes 1769480 | tf_op jit(solution)/shard_map/ppermute | solution.py:29
  31.0 9.0 %collective-permute-start = (bf16[8,8,4608]{2,1,0:T(8,128)(2,1)S(1)}, bf16[8,8,4608]{2,1,0:T(8,128)(2,1)S(1)}, u32[]{:S(2)}, u32[]{:S(2)}) collective-permute-start(bf16[8,8,4608]{2,1,0:T(8,128)(2,1)S(1)} %all_to_all.29), channel_id=1, source_target_pairs={{17,0},{9,8},{19,2},{11,10},{21,4},{13,12},{23,6},{15,14},{16,1},{... | collective-permute-start | bytes 1769480 | tf_op jit(solution)/shard_map/ppermute | solution.py:29
  40.1 6.6 %slice-start.4 = ((s8[4718592]{0:T(1024)(128)(4,1)}), s8[4194304]{0:T(1024)(128)(4,1)S(1)}, s32[]{:S(2)}) async-start(s8[4718592]{0:T(1024)(128)(4,1)} %bitcast.90), calls=%async_computation.8 | async-start | bytes 8388608
  40.4 6.3 %slice-start.5 = ((s8[4718592]{0:T(1024)(128)(4,1)}), s8[524288]{0:T(1024)(128)(4,1)S(1)}, s32[]{:S(2)}) async-start(s8[4718592]{0:T(1024)(128)(4,1)} %bitcast.90), calls=%async_computation.9 | async-start | bytes 1048576
  40.4 6.3 %copy-start.15 = (f32[512]{0:T(512)S(1)}, f32[512]{0:T(512)}, u32[]{:S(2)}) copy-start(f32[512]{0:T(512)} %param.8) | copy-start | bytes 6148
  40.4 5.9 %collective-permute-start.7 = (bf16[32,8,4608]{2,1,0:T(8,128)(2,1)S(1)}, bf16[32,8,4608]{2,1,0:T(8,128)(2,1)S(1)}, u32[]{:S(2)}, u32[]{:S(2)}) collective-permute-start(bf16[32,8,4608]{2,1,0:T(8,128)(2,1)S(1)} %pad_maximum_fusion.3), channel_id=1, source_target_pairs={{0,8},{8,0},{1,9},{9,1},{2,10},{10,2},{3,11},{11,3},{4,12},{12,4},... | collective-permute-start | bytes 7077896 | tf_op jit(solution)/shard_map/ppermute | solution.py:50
  42.1 10.9 %collective-permute-start.6 = (bf16[8,8,4608]{2,1,0:T(8,128)(2,1)S(1)}, bf16[8,8,4608]{2,1,0:T(8,128)(2,1)S(1)}, u32[]{:S(2)}, u32[]{:S(2)}) collective-permute-start(bf16[8,8,4608]{2,1,0:T(8,128)(2,1)S(1)} %all_to_all.29), channel_id=1, source_target_pairs={{119,0},{43,8},{117,2},{41,10},{115,4},{47,12},{113,6},{45,14},{11... | collective-permute-start | bytes 1769480 | tf_op jit(solution)/shard_map/ppermute | solution.py:29
  42.6 15.3 %collective-permute-start.5 = (bf16[8,8,4608]{2,1,0:T(8,128)(2,1)S(1)}, bf16[8,8,4608]{2,1,0:T(8,128)(2,1)S(1)}, u32[]{:S(2)}, u32[]{:S(2)}) collective-permute-start(bf16[8,8,4608]{2,1,0:T(8,128)(2,1)S(1)} %collective-permute-done.4), channel_id=1, source_target_pairs={{96,0},{40,8},{98,2},{42,10},{100,4},{44,12},{102,6},{46,14},{97,1... | collective-permute-start | bytes 1769480 | tf_op jit(solution)/shard_map/ppermute | solution.py:29
  42.9 15.7 %collective-permute-start.3 = (bf16[8,8,4608]{2,1,0:T(8,128)(2,1)S(1)}, bf16[8,8,4608]{2,1,0:T(8,128)(2,1)S(1)}, u32[]{:S(2)}, u32[]{:S(2)}) collective-permute-start(bf16[8,8,4608]{2,1,0:T(8,128)(2,1)S(1)} %collective-permute-done.2), channel_id=1, source_target_pairs={{17,0},{9,8},{19,2},{11,10},{21,4},{13,12},{23,6},{15,14},{16,1},{... | collective-permute-start | bytes 1769480 | tf_op jit(solution)/shard_map/ppermute | solution.py:29
  45.1 13.6 %collective-permute-start.1 = (bf16[8,8,4608]{2,1,0:T(8,128)(2,1)S(1)}, bf16[8,8,4608]{2,1,0:T(8,128)(2,1)S(1)}, u32[]{:S(2)}, u32[]{:S(2)}) collective-permute-start(bf16[8,8,4608]{2,1,0:T(8,128)(2,1)S(1)} %collective-permute-done), channel_id=1, source_target_pairs={{6,0},{10,8},{4,2},{8,10},{2,4},{14,12},{0,6},{12,14},{7,1},{11,9}... | collective-permute-start | bytes 1769480 | tf_op jit(solution)/shard_map/ppermute | solution.py:29
  46.7 2.6 %copy-start.10 = (f32[512]{0:T(512)S(1)}, f32[512]{0:T(512)}, u32[]{:S(2)}) copy-start(f32[512]{0:T(512)} %param.9) | copy-start | bytes 6148
  50.8 14.0 %copy-start.5 = (bf16[512,512]{1,0:T(8,128)(2,1)}, bf16[512,512]{1,0:T(8,128)(2,1)S(1)}, u32[]{:S(2)}) copy-start(bf16[512,512]{1,0:T(8,128)(2,1)S(1)} %get-tuple-element.33) | copy-start | bytes 1572868
  59.0 8.6 %collective-permute-start.8 = (bf16[32,8,4608]{2,1,0:T(8,128)(2,1)S(1)}, bf16[32,8,4608]{2,1,0:T(8,128)(2,1)S(1)}, u32[]{:S(2)}, u32[]{:S(2)}) collective-permute-start(bf16[32,8,4608]{2,1,0:T(8,128)(2,1)S(1)} %pad_maximum_fusion.4), channel_id=1, source_target_pairs={{0,8},{8,0},{1,9},{9,1},{2,10},{10,2},{3,11},{11,3},{4,12},{12,4},... | collective-permute-start | bytes 7077896 | tf_op jit(solution)/shard_map/ppermute | solution.py:50
  64.8 6.1 %slice-start = ((s8[4718592]{0:T(1024)(128)(4,1)}), s8[4194304]{0:T(1024)(128)(4,1)S(1)}, s32[]{:S(2)}) async-start(s8[4718592]{0:T(1024)(128)(4,1)} %bitcast.82), calls=%async_computation.4 | async-start | bytes 8388608
  64.9 6.1 %slice-start.1 = ((s8[4718592]{0:T(1024)(128)(4,1)}), s8[524288]{0:T(1024)(128)(4,1)S(1)}, s32[]{:S(2)}) async-start(s8[4718592]{0:T(1024)(128)(4,1)} %bitcast.82), calls=%async_computation.5 | async-start | bytes 1048576
  67.6 6.2 %copy-start.3 = (bf16[32,8,4608]{2,1,0:T(8,128)(2,1)}, bf16[32,8,4608]{2,1,0:T(8,128)(2,1)S(1)}, u32[]{:S(2)}) copy-start(bf16[32,8,4608]{2,1,0:T(8,128)(2,1)S(1)} %collective-permute-done.8) | copy-start | bytes 7077892
  74.1 4.6 %collective-permute-start.9 = (bf16[256,4608]{1,0:T(8,128)(2,1)S(1)}, bf16[256,4608]{1,0:T(8,128)(2,1)S(1)}, u32[]{:S(2)}, u32[]{:S(2)}) collective-permute-start(bf16[256,4608]{1,0:T(8,128)(2,1)S(1)} %get-tuple-element.67), channel_id=1, source_target_pairs={{0,8},{8,0},{1,9},{9,1},{2,10},{10,2},{3,11},{11,3},{4,12},{12,4},... | collective-permute-start | bytes 7077896 | tf_op jit(solution)/shard_map/ppermute | solution.py:50
  77.4 6.2 %collective-permute-start.10 = (bf16[256,4608]{1,0:T(8,128)(2,1)S(1)}, bf16[256,4608]{1,0:T(8,128)(2,1)S(1)}, u32[]{:S(2)}, u32[]{:S(2)}) collective-permute-start(bf16[256,4608]{1,0:T(8,128)(2,1)S(1)} %get-tuple-element.66), channel_id=1, source_target_pairs={{0,8},{8,0},{1,9},{9,1},{2,10},{10,2},{3,11},{11,3},{4,12},{12,4},... | collective-permute-start | bytes 7077896 | tf_op jit(solution)/shard_map/ppermute | solution.py:50
  79.4 20.3 %collective-permute-start.17 = (bf16[8,8,4608]{2,1,0:T(8,128)(2,1)S(1)}, bf16[8,8,4608]{2,1,0:T(8,128)(2,1)}, u32[]{:S(2)}, u32[]{:S(2)}) collective-permute-start(bf16[8,8,4608]{2,1,0:T(8,128)(2,1)S(1)} %get-tuple-element.68), channel_id=1, source_target_pairs={{119,0},{43,8},{117,2},{41,10},{115,4},{47,12},{113,6},{45,14},{11... | collective-permute-start | bytes 1769480 | tf_op jit(solution)/shard_map/ppermute | solution.py:29
  79.7 14.9 %collective-permute-start.15 = (bf16[8,8,4608]{2,1,0:T(8,128)(2,1)S(1)}, bf16[8,8,4608]{2,1,0:T(8,128)(2,1)S(1)}, u32[]{:S(2)}, u32[]{:S(2)}) collective-permute-start(bf16[8,8,4608]{2,1,0:T(8,128)(2,1)S(1)} %get-tuple-element.69), channel_id=1, source_target_pairs={{17,0},{9,8},{19,2},{11,10},{21,4},{13,12},{23,6},{15,14},{16,1},{... | collective-permute-start | bytes 1769480 | tf_op jit(solution)/shard_map/ppermute | solution.py:29
  79.8 14.8 %collective-permute-start.13 = (bf16[8,8,4608]{2,1,0:T(8,128)(2,1)S(1)}, bf16[8,8,4608]{2,1,0:T(8,128)(2,1)S(1)}, u32[]{:S(2)}, u32[]{:S(2)}) collective-permute-start(bf16[8,8,4608]{2,1,0:T(8,128)(2,1)S(1)} %get-tuple-element.70), channel_id=1, source_target_pairs={{6,0},{10,8},{4,2},{8,10},{2,4},{14,12},{0,6},{12,14},{7,1},{11,9}... | collective-permute-start | bytes 1769480 | tf_op jit(solution)/shard_map/ppermute | solution.py:29
  80.9 16.1 %collective-permute-start.11 = (bf16[8,8,4608]{2,1,0:T(8,128)(2,1)S(1)}, bf16[8,8,4608]{2,1,0:T(8,128)(2,1)S(1)}, u32[]{:S(2)}, u32[]{:S(2)}) collective-permute-start(bf16[8,8,4608]{2,1,0:T(8,128)(2,1)S(1)} %get-tuple-element.71), channel_id=1, source_target_pairs={{96,0},{40,8},{98,2},{42,10},{100,4},{44,12},{102,6},{46,14},{97,1... | collective-permute-start | bytes 1769480 | tf_op jit(solution)/shard_map/ppermute | solution.py:29
  97.4 8.8 %collective-permute-start.16 = (bf16[8,8,4608]{2,1,0:T(8,128)(2,1)S(1)}, bf16[8,8,4608]{2,1,0:T(8,128)(2,1)S(1)}, u32[]{:S(2)}, u32[]{:S(2)}) collective-permute-start(bf16[8,8,4608]{2,1,0:T(8,128)(2,1)S(1)} %get-tuple-element.72), channel_id=1, source_target_pairs={{96,0},{40,8},{98,2},{42,10},{100,4},{44,12},{102,6},{46,14},{97,1... | collective-permute-start | bytes 1769480 | tf_op jit(solution)/shard_map/ppermute | solution.py:29
  97.5 8.8 %collective-permute-start.14 = (bf16[8,8,4608]{2,1,0:T(8,128)(2,1)S(1)}, bf16[8,8,4608]{2,1,0:T(8,128)(2,1)S(1)}, u32[]{:S(2)}, u32[]{:S(2)}) collective-permute-start(bf16[8,8,4608]{2,1,0:T(8,128)(2,1)S(1)} %get-tuple-element.73), channel_id=1, source_target_pairs={{17,0},{9,8},{19,2},{11,10},{21,4},{13,12},{23,6},{15,14},{16,1},{... | collective-permute-start | bytes 1769480 | tf_op jit(solution)/shard_map/ppermute | solution.py:29
  97.8 9.0 %collective-permute-start.12 = (bf16[8,8,4608]{2,1,0:T(8,128)(2,1)S(1)}, bf16[8,8,4608]{2,1,0:T(8,128)(2,1)S(1)}, u32[]{:S(2)}, u32[]{:S(2)}) collective-permute-start(bf16[8,8,4608]{2,1,0:T(8,128)(2,1)S(1)} %get-tuple-element.74), channel_id=1, source_target_pairs={{6,0},{10,8},{4,2},{8,10},{2,4},{14,12},{0,6},{12,14},{7,1},{11,9}... | collective-permute-start | bytes 1769480 | tf_op jit(solution)/shard_map/ppermute | solution.py:29
  99.8 24.8 %copy-start.8 = (f32[8,4608]{1,0:T(8,128)S(1)}, f32[8,4608]{1,0:T(8,128)}, u32[]{:S(2)}) copy-start(f32[8,4608]{1,0:T(8,128)} %copy-done.7) | copy-start | bytes 442372
  99.8 24.8 %copy-start.9 = (f32[4608]{0:T(1024)S(1)}, f32[4608]{0:T(1024)}, u32[]{:S(2)}) copy-start(f32[4608]{0:T(1024)} %param.11) | copy-start | bytes 55300
  138.3 9.1 %collective-permute-start.20 = (bf16[8,8,4608]{2,1,0:T(8,128)(2,1)S(1)}, bf16[8,8,4608]{2,1,0:T(8,128)(2,1)}, u32[]{:S(2)}, u32[]{:S(2)}) collective-permute-start(bf16[8,8,4608]{2,1,0:T(8,128)(2,1)S(1)} %all_to_all.31), channel_id=1, source_target_pairs={{96,0},{40,8},{98,2},{42,10},{100,4},{44,12},{102,6},{46,14},{97,1... | collective-permute-start | bytes 1769480 | tf_op jit(solution)/shard_map/ppermute | solution.py:29
  138.3 9.1 %collective-permute-start.19 = (bf16[8,8,4608]{2,1,0:T(8,128)(2,1)S(1)}, bf16[8,8,4608]{2,1,0:T(8,128)(2,1)}, u32[]{:S(2)}, u32[]{:S(2)}) collective-permute-start(bf16[8,8,4608]{2,1,0:T(8,128)(2,1)S(1)} %all_to_all.31), channel_id=1, source_target_pairs={{17,0},{9,8},{19,2},{11,10},{21,4},{13,12},{23,6},{15,14},{16,1},{... | collective-permute-start | bytes 1769480 | tf_op jit(solution)/shard_map/ppermute | solution.py:29
  138.3 9.1 %collective-permute-start.18 = (bf16[8,8,4608]{2,1,0:T(8,128)(2,1)S(1)}, bf16[8,8,4608]{2,1,0:T(8,128)(2,1)}, u32[]{:S(2)}, u32[]{:S(2)}) collective-permute-start(bf16[8,8,4608]{2,1,0:T(8,128)(2,1)S(1)} %all_to_all.31), channel_id=1, source_target_pairs={{6,0},{10,8},{4,2},{8,10},{2,4},{14,12},{0,6},{12,14},{7,1},{11,9}... | collective-permute-start | bytes 1769480 | tf_op jit(solution)/shard_map/ppermute | solution.py:29
  149.1 12.3 %collective-permute-start.21 = (bf16[32,8,4608]{2,1,0:T(8,128)(2,1)S(1)}, bf16[32,8,4608]{2,1,0:T(8,128)(2,1)S(1)}, u32[]{:S(2)}, u32[]{:S(2)}) collective-permute-start(bf16[32,8,4608]{2,1,0:T(8,128)(2,1)S(1)} %pad_maximum_fusion.5), channel_id=1, source_target_pairs={{0,8},{8,0},{1,9},{9,1},{2,10},{10,2},{3,11},{11,3},{4,12},{12,4},... | collective-permute-start | bytes 7077896 | tf_op jit(solution)/shard_map/ppermute | solution.py:50
  157.6 13.1 %collective-permute-start.25 = (bf16[8,8,4608]{2,1,0:T(8,128)(2,1)S(1)}, bf16[8,8,4608]{2,1,0:T(8,128)(2,1)}, u32[]{:S(2)}, u32[]{:S(2)}) collective-permute-start(bf16[8,8,4608]{2,1,0:T(8,128)(2,1)S(1)} %all_to_all.31), channel_id=1, source_target_pairs={{119,0},{43,8},{117,2},{41,10},{115,4},{47,12},{113,6},{45,14},{11... | collective-permute-start | bytes 1769480 | tf_op jit(solution)/shard_map/ppermute | solution.py:29
  158.9 15.4 %collective-permute-start.23 = (bf16[8,8,4608]{2,1,0:T(8,128)(2,1)}, bf16[8,8,4608]{2,1,0:T(8,128)(2,1)}, u32[]{:S(2)}, u32[]{:S(2)}) collective-permute-start(bf16[8,8,4608]{2,1,0:T(8,128)(2,1)} %collective-permute-done.20), channel_id=1, source_target_pairs={{17,0},{9,8},{19,2},{11,10},{21,4},{13,12},{23,6},{15,14},{16,1},{... | collective-permute-start | bytes 1769480 | tf_op jit(solution)/shard_map/ppermute | solution.py:29
  159.5 14.8 %collective-permute-start.22 = (bf16[8,8,4608]{2,1,0:T(8,128)(2,1)}, bf16[8,8,4608]{2,1,0:T(8,128)(2,1)}, u32[]{:S(2)}, u32[]{:S(2)}) collective-permute-start(bf16[8,8,4608]{2,1,0:T(8,128)(2,1)} %collective-permute-done.19), channel_id=1, source_target_pairs={{6,0},{10,8},{4,2},{8,10},{2,4},{14,12},{0,6},{12,14},{7,1},{11,9}... | collective-permute-start | bytes 1769480 | tf_op jit(solution)/shard_map/ppermute | solution.py:29
  160.6 14.4 %collective-permute-start.24 = (bf16[8,8,4608]{2,1,0:T(8,128)(2,1)}, bf16[8,8,4608]{2,1,0:T(8,128)(2,1)}, u32[]{:S(2)}, u32[]{:S(2)}) collective-permute-start(bf16[8,8,4608]{2,1,0:T(8,128)(2,1)} %collective-permute-done.18), channel_id=1, source_target_pairs={{96,0},{40,8},{98,2},{42,10},{100,4},{44,12},{102,6},{46,14},{97,1... | collective-permute-start | bytes 1769480 | tf_op jit(solution)/shard_map/ppermute | solution.py:29
  161.8 2.2 %copy-start = (bf16[64,8,4608]{2,1,0:T(8,128)(2,1)}, bf16[64,8,4608]{2,1,0:T(8,128)(2,1)S(1)}, u32[]{:S(2)}) copy-start(bf16[64,8,4608]{2,1,0:T(8,128)(2,1)S(1)} %pad_maximum_fusion.1) | copy-start | bytes 14155780
  164.0 17.4 %slice-start.2 = ((s8[4718592]{0:T(1024)(128)(4,1)}), s8[524288]{0:T(1024)(128)(4,1)S(1)}, s32[]{:S(2)}) async-start(s8[4718592]{0:T(1024)(128)(4,1)} %bitcast.84), calls=%async_computation.6 | async-start | bytes 1048576
  167.9 13.5 %copy-start.11 = (f32[512]{0:T(512)S(1)}, f32[512]{0:T(512)}, u32[]{:S(2)}) copy-start(f32[512]{0:T(512)} %get-tuple-element.60) | copy-start | bytes 6148
  168.0 13.5 %copy-start.12 = (f32[512]{0:T(512)S(1)}, f32[512]{0:T(512)}, u32[]{:S(2)}) copy-start(f32[512]{0:T(512)} %get-tuple-element.59) | copy-start | bytes 6148
  168.0 13.5 %slice-start.3 = ((s8[4718592]{0:T(1024)(128)(4,1)}), s8[4194304]{0:T(1024)(128)(4,1)S(1)}, s32[]{:S(2)}) async-start(s8[4718592]{0:T(1024)(128)(4,1)} %bitcast.84), calls=%async_computation.7 | async-start | bytes 8388608
  168.0 13.5 %copy-start.6 = (bf16[512,512]{1,0:T(8,128)(2,1)S(1)}, bf16[512,512]{1,0:T(8,128)(2,1)}, u32[]{:S(2)}) copy-start(bf16[512,512]{1,0:T(8,128)(2,1)} %copy-done.5) | copy-start | bytes 1572868
  170.6 10.8 %copy-start.1 = (bf16[64,8,4608]{2,1,0:T(8,128)(2,1)S(1)}, bf16[64,8,4608]{2,1,0:T(8,128)(2,1)}, u32[]{:S(2)}) copy-start(bf16[64,8,4608]{2,1,0:T(8,128)(2,1)} %copy-done) | copy-start | bytes 14155780
  170.7 10.8 %copy-start.14 = (f32[512]{0:T(512)S(1)}, f32[512]{0:T(512)}, u32[]{:S(2)}) copy-start(f32[512]{0:T(512)} %get-tuple-element.87) | copy-start | bytes 6148
  176.8 10.1 %collective-permute-start.26 = (bf16[32,8,4608]{2,1,0:T(8,128)(2,1)S(1)}, bf16[32,8,4608]{2,1,0:T(8,128)(2,1)S(1)}, u32[]{:S(2)}, u32[]{:S(2)}) collective-permute-start(bf16[32,8,4608]{2,1,0:T(8,128)(2,1)S(1)} %pad_maximum_fusion.6), channel_id=1, source_target_pairs={{0,8},{8,0},{1,9},{9,1},{2,10},{10,2},{3,11},{11,3},{4,12},{12,4},... | collective-permute-start | bytes 7077896 | tf_op jit(solution)/shard_map/ppermute | solution.py:50
  187.6 4.7 %copy-start.4 = (bf16[512,512]{0,1:T(8,128)(2,1)S(1)}, bf16[512,512]{0,1:T(8,128)(2,1)}, u32[]{:S(2)}) copy-start(bf16[512,512]{0,1:T(8,128)(2,1)} %get-tuple-element.63) | copy-start | bytes 1572868
  192.3 6.8 %copy-start.2 = (f32[512,512]{1,0:T(8,128)S(1)}, f32[512,512]{1,0:T(8,128)}, u32[]{:S(2)}) copy-start(f32[512,512]{1,0:T(8,128)} %pad_maximum_fusion.7) | copy-start | bytes 3145732
  (1 other events, 0.7 us)

commit v3 on v2

--- a/solution.py
+++ b/solution.py
@@ -82,8 +82,9 @@
     y_more, z_more, x_more = receive(xy, "x", 1), receive(yz, "y", 1), receive(zx, "z", 1)
     xyz = receive(xyz, "xyz", 1)
     x, y, z = (add(*pair).astype(bf16) for pair in ((x, x_more), (y, y_more), (z, z_more)))
+    done = work(x_more)
     x, y, z = receive(x, "x", 1), receive(y, "y", 1), receive(z, "z", 1)
-    x, y, z, xyz, done = barrier(x, y, z, xyz, work)
+    x, y, z, xyz, done = barrier(x, y, z, xyz, done)
     blocks = trade(add(own, xyz, x, y, z).astype(bf16), 0)
     return jnp.sum(blocks.astype(f32), axis=0), done
 
@@ -92,7 +93,6 @@
     row_scale = 1.0 / math.sqrt(1024)
     own_rows = lax.all_to_all(activations, ("x", "yl"), split_axis=0, concat_axis=1, tiled=True)
     own_rows = own_rows.astype(f32)
-    row_norms = jnp.sqrt(jnp.sum(jnp.square(dec_weight.astype(f32)), axis=1) + 1e-06)
     own_centered, = barrier((own_rows - dec_bias).astype(bf16))
 
     def encode(rows):
@@ -105,6 +105,7 @@
     near, encoded, mine, theirs = gather(own_centered, encode)
     code_near, slopes_near, totals_near = encoded
     code_mine, slopes_mine, totals_mine = encode(mine)
+    theirs, _ = barrier(theirs, code_mine)
     code_theirs, slopes_theirs, totals_theirs = encode(theirs)
     totals = totals_near + totals_mine + totals_theirs
 
@@ -120,16 +121,26 @@
     recon_distant, = barrier(add(recon_mine[:256], recon_theirs[0]).astype(bf16))
     recon_mine, recon_distant = barrier(recon_mine, recon_distant)
     recon_near = add(recon_mine[256:], recon_theirs[1]).astype(bf16)
-    near_t, code_near_t, distant_t, code_distant_t = (
-        near.T,
-        code_near.T,
-        jnp.concatenate([mine, theirs]).T,
-        jnp.concatenate([code_mine, code_theirs]).T,
-    )
-    slopes_distant = jnp.concatenate([slopes_mine, slopes_theirs])
-    recon, (near_t, code_near_t, distant_t, code_distant_t, slopes_distant) = scatter(
-        recon_near, recon_distant, (near_t, code_near_t, distant_t, code_distant_t, slopes_distant)
-    )
+
+    def side_work(received):
+        *rest, dec, _ = barrier(
+            near, code_near, mine, theirs, code_mine, code_theirs, slopes_mine, slopes_theirs,
+            dec_weight, received,
+        )
+        near_rows, code_rows, mine_rows, their_rows, mine_code, their_code, *slopes = rest
+        row_norms = jnp.sqrt(jnp.sum(jnp.square(dec.astype(f32)), axis=1) + 1e-06)
+        return (
+            near_rows.T,
+            code_rows.T,
+            jnp.concatenate([mine_rows, their_rows]).T,
+            jnp.concatenate([mine_code, their_code]).T,
+            jnp.concatenate(slopes),
+            sparsity_coeff * row_scale * row_norms,
+            sparsity_coeff * row_scale * totals / row_norms,
+        )
+
+    recon, work = scatter(recon_near, recon_distant, side_work)
+    near_t, code_near_t, distant_t, code_distant_t, slopes_distant, norm_grad, norm_scale = work
     recon_error = recon + dec_bias - own_rows
     own_delta, = barrier((recon_error * row_scale).astype(bf16))
 
@@ -138,22 +149,16 @@
             delta, dec_weight, (((1,), (1,)), ((), ())), preferred_element_type=f32
         )
         return barrier(
-            ((code_grad + sparsity_coeff * row_scale * row_norms) * slopes).astype(bf16)
+            ((code_grad + norm_grad) * slopes).astype(bf16)
         )[0]
 
     def near_grad(delta):
-        return jnp.dot(near_t, preact_grad(delta, slopes_near), preferred_element_type=f32)
+        preact = preact_grad(delta, slopes_near)
+        return jnp.dot(near_t, preact, preferred_element_type=f32).astype(bf16)
 
     delta_near, grad_enc, mine, theirs = gather(own_delta, near_grad)
     grad_dec = jnp.dot(code_near_t, delta_near, preferred_element_type=f32)
-    grad_dec = (
-        grad_dec
-        + sparsity_coeff
-        * row_scale
-        * totals[:, None]
-        * dec_weight.astype(f32)
-        / row_norms[:, None]
-    )
+    grad_dec = (grad_dec + norm_scale[:, None] * dec_weight.astype(f32)).astype(bf16)
     grad_dec, = barrier(grad_dec)
     theirs, _ = barrier(theirs, grad_dec)
     delta, = barrier(jnp.concatenate([mine, theirs]))

time: 204 us -> 197 us (0.966)
  starting transfers between devices: 30.4 us -> 37.7 us
  matrix products: 38.9 us -> 32.4 us
  other arithmetic: 17.4 us -> 14.8 us
  blocking collectives: 59.3 us -> 56.8 us
    ppermute x6, starting transfers between devices: 18.3 us -> 23.5 us  [swap(): return lax.ppermute(block, 'core', [(0, 1), (1, 0)])]
    ppermute x21, waiting for transfers between devices: 50.1 us -> 46.1 us  [receive(): return lax.ppermute(block, MESH, pairs)]
    dot_general x2, matrix products: 8.58 us -> 5.25 us  [preact_grad(): lax.dot_general(delta, dec_weight, (((1,), (1,)), ((), ())), preferred_el...]
    all_to_all x3, blocking collectives: 48.3 us -> 45.8 us  [trade(): return lax.all_to_all(blocks, MESH, 0, 0, axis_index_groups=cubes(pairing))]
    dot_general x1, matrix products: 6.75 us -> 4.34 us  [on_device(): jnp.dot(code_distant_t, delta, preferred_element_type=f32)]
    dot_general x1, matrix products: 5.42 us -> 3.07 us  [on_device(): grad_dec = jnp.dot(code_near_t, delta_near, preferred_element_type=f32)]
    ppermute x6, waiting for transfers between devices: 3.12 us -> 5.33 us  [swap(): return lax.ppermute(block, 'core', [(0, 1), (1, 0)])]
  transfers between devices with their start and end apart: 27 -> 27, of which waited for: 15 -> 19; matrix products, arithmetic and copies ran while one was open for 13% -> 14% of each run, Pallas kernels for 0% -> 0%
where the time goes in v3:
time: 197 us; the launch traced here: 196 us
  blocking collectives  56.8 us (29%)
  waiting for transfers between devices  51.4 us (26%)
  starting transfers between devices  37.7 us (19%)
  matrix products  32.4 us (16%)
  other arithmetic  14.8 us (8%)
  local copies, waits for them, and re-layouts  2.33 us (1%)
    ppermute x21, waiting for transfers between devices, receive(): return lax.ppermute(block, MESH, pairs)  46.1 us
    all_to_all x3, blocking collectives, trade(): return lax.all_to_all(blocks, MESH, 0, 0, axis_index_groups=cubes(pairing))  45.8 us
    ppermute x6, starting transfers between devices, swap(): return lax.ppermute(block, 'core', [(0, 1), (1, 0)])  23.5 us
    ppermute x21, starting transfers between devices, receive(): return lax.ppermute(block, MESH, pairs)  14.1 us
    all_to_all x1, blocking collectives, on_device(): lax.all_to_all(activations, ('x', 'yl'), split_axis=0, concat_axis=1, til...  11 us
    dot_general x3, matrix products, encode(): jnp.dot(rows, enc_weight, preferred_element_type=f32) + enc_bias  5.34 us
    ppermute x6, waiting for transfers between devices, swap(): return lax.ppermute(block, 'core', [(0, 1), (1, 0)])  5.33 us
    dot_general x2, matrix products, preact_grad(): lax.dot_general(delta, dec_weight, (((1,), (1,)), ((), ())), preferred_el...  5.25 us
  transfers between devices with their start and end apart: 27, of which 19 were waited for; matrix products, arithmetic and copies ran while one was open for 14% of the time, Pallas kernels for 0%

profile of v3, /device:TPU:1, one launch (start us, length us, event | category | flops | bytes accessed | tf_op | source)
XLA Modules:
  0.0 196.5 jit_solution(6038243372648228687)
XLA Ops:
  0.6 11.0 %all_to_all.28 = bf16[8,8,576]{2,1,0:T(8,128)(2,1)S(1)} all-to-all(bf16[8,8,576]{2,1,0:T(8,128)(2,1)} %bitcast.86), channel_id=1, replica_groups=mesh['z'=4,'yh'=2,'core'=2,'x'=4,'yl'=2] {'x','yl'}, dimensions={0} | all-to-all | bytes 147456 | tf_op jit(solution)/shard_map/all_to_all | solution.py:94
  12.6 18.4 %all_to_all.29 = bf16[8,8,4608]{2,1,0:T(8,128)(2,1)S(1)} all-to-all(bf16[8,8,4608]{2,1,0:T(8,128)(2,1)S(1)} %broadcast_in_dim.4), channel_id=1, replica_groups={{0,2,1,3,32,34,33,35},{4,6,5,7,36,38,37,39},{16,18,17,19,48,50,49,51},{..., dimensions={0} | all-to-all | bytes 1179648 | tf_op jit(solution)/shard_map/all_to_all | solution.py:46
  31.0 9.0 %collective-permute-done = bf16[8,8,4608]{2,1,0:T(8,128)(2,1)S(1)} collective-permute-done((bf16[8,8,4608]{2,1,0:T(8,128)(2,1)S(1)}, bf16[8,8,4608]{2,1,0:T(8,128)(2,1)S(1)}, u32[]{:S(2)}, u32[]{:S(2)}) %collective-permute-start) | collective-permute-done | bytes 589856 | tf_op jit(solution)/shard_map/ppermute | solution.py:29
  40.4 2.6 %collective-permute-start.7 = (bf16[32,8,4608]{2,1,0:T(8,128)(2,1)S(1)}, bf16[32,8,4608]{2,1,0:T(8,128)(2,1)S(1)}, u32[]{:S(2)}, u32[]{:S(2)}) collective-permute-start(bf16[32,8,4608]{2,1,0:T(8,128)(2,1)S(1)} %pad_maximum_fusion.3), channel_id=1, source_target_pairs={{0,8},{8,0},{1,9},{9,1},{2,10},{10,2},{3,11},{11,3},{4,12},{12,4},... | collective-permute-start | bytes 7077896 | tf_op jit(solution)/shard_map/ppermute | solution.py:50
  43.0 2.1 %collective-permute-start.1 = (bf16[8,8,4608]{2,1,0:T(8,128)(2,1)S(1)}, bf16[8,8,4608]{2,1,0:T(8,128)(2,1)S(1)}, u32[]{:S(2)}, u32[]{:S(2)}) collective-permute-start(bf16[8,8,4608]{2,1,0:T(8,128)(2,1)S(1)} %collective-permute-done), channel_id=1, source_target_pairs={{6,0},{10,8},{4,2},{8,10},{2,4},{14,12},{0,6},{12,14},{7,1},{11,9}... | collective-permute-start | bytes 1769480 | tf_op jit(solution)/shard_map/ppermute | solution.py:29
  45.0 0.8 collective-permute-start.3
  45.8 1.0 collective-permute-start.5
  47.6 2.6 %convolution_add_fusion.1 = f32[512,512]{1,0:T(8,128)S(1)} fusion(bf16[4608,512]{1,0:T(8,128)(2,1)S(1)} %bitcast.88, f32[512]{0:T(512)S(1)} %copy-done.7, bf16[64,8,4608]{2,1,0:T(8,128)(2,1)S(1)} %pad_maximum_fusion), kind=kOutput, calls=%fused_computation.24 | convolution fusion | flops 2416181248 | bytes 10487808 | tf_op jit(solution)/shard_map/dot_general | solution.py:99
  50.2 1.4 fusion.31
  51.6 2.2 %collective-permute-done.6 = bf16[8,8,4608]{2,1,0:T(8,128)(2,1)S(1)} collective-permute-done((bf16[8,8,4608]{2,1,0:T(8,128)(2,1)S(1)}, bf16[8,8,4608]{2,1,0:T(8,128)(2,1)S(1)}, u32[]{:S(2)}, u32[]{:S(2)}) %collective-permute-start.6) | collective-permute-done | bytes 589856 | tf_op jit(solution)/shard_map/ppermute | solution.py:29
  53.8 5.1 %collective-permute-done.1 = bf16[8,8,4608]{2,1,0:T(8,128)(2,1)S(1)} collective-permute-done((bf16[8,8,4608]{2,1,0:T(8,128)(2,1)S(1)}, bf16[8,8,4608]{2,1,0:T(8,128)(2,1)S(1)}, u32[]{:S(2)}, u32[]{:S(2)}) %collective-permute-start.1) | collective-permute-done | bytes 589856 | tf_op jit(solution)/shard_map/ppermute | solution.py:29
  60.4 4.6 %collective-permute-start.8 = (bf16[32,8,4608]{2,1,0:T(8,128)(2,1)S(1)}, bf16[32,8,4608]{2,1,0:T(8,128)(2,1)S(1)}, u32[]{:S(2)}, u32[]{:S(2)}) collective-permute-start(bf16[32,8,4608]{2,1,0:T(8,128)(2,1)S(1)} %pad_maximum_fusion.4), channel_id=1, source_target_pairs={{0,8},{8,0},{1,9},{9,1},{2,10},{10,2},{3,11},{11,3},{4,12},{12,4},... | collective-permute-start | bytes 7077896 | tf_op jit(solution)/shard_map/ppermute | solution.py:50
  65.1 1.4 convolution_add_fusion.3
  66.8 2.5 %collective-permute-done.8 = bf16[32,8,4608]{2,1,0:T(8,128)(2,1)S(1)} collective-permute-done((bf16[32,8,4608]{2,1,0:T(8,128)(2,1)S(1)}, bf16[32,8,4608]{2,1,0:T(8,128)(2,1)S(1)}, u32[]{:S(2)}, u32[]{:S(2)}) %collective-permute-start.8) | collective-permute-done | bytes 2359328 | tf_op jit(solution)/shard_map/ppermute | solution.py:50
  69.2 1.4 convolution_add_fusion.2
  71.0 2.8 %convolution_convert_fusion.1 = bf16[512,4608]{1,0:T(8,128)(2,1)S(1)} fusion(bf16[512,512]{1,0:T(8,128)(2,1)S(1)} %get-tuple-element.56, bf16[512,4608]{1,0:T(8,128)(2,1)S(1)} %bitcast.76), kind=kOutput, calls=%fused_computation.5 | convolution fusion | flops 2418278400 | bytes 9961472 | tf_op jit(solution)/shard_map/dot_general | solution.py:116
  74.6 2.8 %convolution_convert_fusion.2 = bf16[512,4608]{1,0:T(8,128)(2,1)S(1)} fusion(bf16[512,512]{1,0:T(8,128)(2,1)S(1)} %get-tuple-element.55, bf16[512,4608]{1,0:T(8,128)(2,1)S(1)} %bitcast.76), kind=kOutput, calls=%fused_computation.6 | convolution fusion | flops 2418278400 | bytes 9961472 | tf_op jit(solution)/shard_map/dot_general | solution.py:119
  77.6 1.1 collective-permute-done.9
  79.3 1.0 slice_bitcast_fusion.4
  80.3 3.8 %collective-permute-start.17 = (bf16[8,8,4608]{2,1,0:T(8,128)(2,1)}, bf16[8,8,4608]{2,1,0:T(8,128)(2,1)}, u32[]{:S(2)}, u32[]{:S(2)}) collective-permute-start(bf16[8,8,4608]{2,1,0:T(8,128)(2,1)} %get-tuple-element.90), channel_id=1, source_target_pairs={{119,0},{43,8},{117,2},{41,10},{115,4},{47,12},{113,6},{45,14},{11... | collective-permute-start | bytes 1769480 | tf_op jit(solution)/shard_map/ppermute | solution.py:29
  84.7 4.6 %collective-permute-done.11 = bf16[8,8,4608]{2,1,0:T(8,128)(2,1)S(1)} collective-permute-done((bf16[8,8,4608]{2,1,0:T(8,128)(2,1)S(1)}, bf16[8,8,4608]{2,1,0:T(8,128)(2,1)S(1)}, u32[]{:S(2)}, u32[]{:S(2)}) %collective-permute-start.11) | collective-permute-done | bytes 589856 | tf_op jit(solution)/shard_map/ppermute | solution.py:29
  89.3 1.0 multiply_reduce_fusion
  90.3 5.4 %collective-permute-done.15 = bf16[8,8,4608]{2,1,0:T(8,128)(2,1)S(1)} collective-permute-done((bf16[8,8,4608]{2,1,0:T(8,128)(2,1)S(1)}, bf16[8,8,4608]{2,1,0:T(8,128)(2,1)S(1)}, u32[]{:S(2)}, u32[]{:S(2)}) %collective-permute-start.15) | collective-permute-done | bytes 589856 | tf_op jit(solution)/shard_map/ppermute | solution.py:29
  96.2 1.5 collective-permute-start.12
  97.7 1.1 collective-permute-start.16
  98.8 1.1 pad_maximum_fusion.7
  99.9 0.8 maximum_bitcast_fusion.1
  100.7 2.5 %maximum_bitcast_fusion = bf16[4608,512]{0,1:T(8,128)(2,1)} fusion(bf16[256,4608]{1,0:T(8,128)(2,1)S(1)} %bitcast.84, bf16[256,4608]{1,0:T(8,128)(2,1)S(1)} %bitcast.77), kind=kLoop, calls=%fused_computation.8 | loop fusion | flops 9437184 | bytes 9437184 | tf_op jit(solution)/shard_map/transpose | solution.py:135
  103.2 2.1 %collective-permute-done.12 = bf16[8,8,4608]{2,1,0:T(8,128)(2,1)S(1)} collective-permute-done((bf16[8,8,4608]{2,1,0:T(8,128)(2,1)S(1)}, bf16[8,8,4608]{2,1,0:T(8,128)(2,1)S(1)}, u32[]{:S(2)}, u32[]{:S(2)}) %collective-permute-start.12) | collective-permute-done | bytes 589856 | tf_op jit(solution)/shard_map/ppermute | solution.py:29
  105.3 1.5 collective-permute-done.14
  106.8 1.4 fusion.17
  108.2 13.8 %all_to_all.30 = bf16[8,8,4608]{2,1,0:T(8,128)(2,1)S(1)} all-to-all(bf16[8,8,4608]{2,1,0:T(8,128)(2,1)S(1)} %fusion.17), channel_id=1, replica_groups={{0,2,1,3,32,34,33,35},{4,6,5,7,36,38,37,39},{16,18,17,19,48,50,49,51},{..., dimensions={0} | all-to-all | bytes 1179648 | tf_op jit(solution)/shard_map/all_to_all | solution.py:46
  122.2 13.6 %all_to_all.31 = bf16[8,8,4608]{2,1,0:T(8,128)(2,1)S(1)} all-to-all(bf16[8,8,4608]{2,1,0:T(8,128)(2,1)S(1)} %broadcast_in_dim.5), channel_id=1, replica_groups={{0,2,1,3,32,34,33,35},{4,6,5,7,36,38,37,39},{16,18,17,19,48,50,49,51},{..., dimensions={0} | all-to-all | bytes 1179648 | tf_op jit(solution)/shard_map/all_to_all | solution.py:46
  135.8 8.7 %collective-permute-done.18 = bf16[8,8,4608]{2,1,0:T(8,128)(2,1)S(1)} collective-permute-done((bf16[8,8,4608]{2,1,0:T(8,128)(2,1)S(1)}, bf16[8,8,4608]{2,1,0:T(8,128)(2,1)S(1)}, u32[]{:S(2)}, u32[]{:S(2)}) %collective-permute-start.18) | collective-permute-done | bytes 589856 | tf_op jit(solution)/shard_map/ppermute | solution.py:29
  145.3 10.2 %collective-permute-start.21 = (bf16[32,8,4608]{2,1,0:T(8,128)(2,1)S(1)}, bf16[32,8,4608]{2,1,0:T(8,128)(2,1)S(1)}, u32[]{:S(2)}, u32[]{:S(2)}) collective-permute-start(bf16[32,8,4608]{2,1,0:T(8,128)(2,1)S(1)} %pad_maximum_fusion.5), channel_id=1, source_target_pairs={{0,8},{8,0},{1,9},{9,1},{2,10},{10,2},{3,11},{11,3},{4,12},{12,4},... | collective-permute-start | bytes 7077896 | tf_op jit(solution)/shard_map/ppermute | solution.py:50
  156.2 1.3 collective-permute-start.22
  157.5 0.8 collective-permute-start.23
  158.3 1.1 collective-permute-start.24
  160.1 2.6 %fusion.11 = bf16[512,512]{1,0:T(8,128)(2,1)S(1)} fusion(f32[512,512]{1,0:T(8,128)S(1)} %copy-done.3, bf16[512,4608]{1,0:T(8,128)(2,1)S(1)} %bitcast.76, bf16[64,8,4608]{2,1,0:T(8,128)(2,1)S(1)} %pad_maximum_fusion.1, f32[512]{0:T(512)S(1)} %get-tuple-element.77), kind=kOutput, calls=%fused_computation.26 | convolution fusion | flops 2416705536 | bytes 11012096 | tf_op jit(solution)/shard_map/dot_general | solution.py:148
  162.8 4.3 %convolution_convert_fusion = bf16[4608,512]{1,0:T(8,128)(2,1)} fusion(bf16[4608,512]{0,1:T(8,128)(2,1)S(1)} %bitcast.80, bf16[512,512]{1,0:T(8,128)(2,1)S(1)} %fusion.11), kind=kOutput, calls=%fused_computation.4 | convolution fusion | flops 2418278400 | bytes 9961472 | tf_op jit(solution)/shard_map/dot_general | solution.py:157
  167.1 4.5 %collective-permute-done.22 = bf16[8,8,4608]{2,1,0:T(8,128)(2,1)S(1)} collective-permute-done((bf16[8,8,4608]{2,1,0:T(8,128)(2,1)S(1)}, bf16[8,8,4608]{2,1,0:T(8,128)(2,1)S(1)}, u32[]{:S(2)}, u32[]{:S(2)}) %collective-permute-start.22) | collective-permute-done | bytes 589856 | tf_op jit(solution)/shard_map/ppermute | solution.py:29
  172.8 1.5 pad_maximum_fusion.6
  174.3 5.4 %collective-permute-start.26 = (bf16[32,8,4608]{2,1,0:T(8,128)(2,1)S(1)}, bf16[32,8,4608]{2,1,0:T(8,128)(2,1)S(1)}, u32[]{:S(2)}, u32[]{:S(2)}) collective-permute-start(bf16[32,8,4608]{2,1,0:T(8,128)(2,1)S(1)} %pad_maximum_fusion.6), channel_id=1, source_target_pairs={{0,8},{8,0},{1,9},{9,1},{2,10},{10,2},{3,11},{11,3},{4,12},{12,4},... | collective-permute-start | bytes 7077896 | tf_op jit(solution)/shard_map/ppermute | solution.py:50
  179.8 3.1 %add_convert_fusion.2 = bf16[512,4608]{1,0:T(8,128)(2,1)S(1)} fusion(bf16[512,4608]{1,0:T(8,128)(2,1)S(1)} %bitcast.76, bf16[512,512]{0,1:T(8,128)(2,1)S(1)} %bitcast.79, bf16[64,8,4608]{2,1,0:T(8,128)(2,1)S(1)} %pad_maximum_fusion.1, f32[512]{0:T(512)S(1)} %get-tuple-element.84), kind=kOutput, calls=%fused_computation.2 | convolution fusion | flops 2425356288 | bytes 14682112 | tf_op jit(solution)/shard_map/dot_general | solution.py:160
  182.9 1.1 collective-permute-done.26
  185.0 4.3 %add_convert_fusion = bf16[512,4608]{1,0:T(8,128)(2,1)} fusion(bf16[512,4608]{1,0:T(8,128)(2,1)S(1)} %add_convert_fusion.2, bf16[512,512]{0,1:T(8,128)(2,1)S(1)} %copy-done, bf16[512,4608]{1,0:T(8,128)(2,1)S(1)} %pad_maximum_fusion.2), kind=kOutput, calls=%fused_computation | convolution fusion | flops 2422996992 | bytes 14680064 | tf_op jit(solution)/shard_map/dot_general | solution.py:167
  189.3 2.6 %fusion.10 = bf16[512,512]{1,0:T(8,128)(2,1)S(1)} fusion(f32[512,512]{1,0:T(8,128)S(1)} %copy-done.4, bf16[512,4608]{1,0:T(8,128)(2,1)S(1)} %pad_maximum_fusion.2, bf16[512,4608]{1,0:T(8,128)(2,1)S(1)} %bitcast.76, f32[512]{0:T(512)S(1)} %get-tuple-element.77), kind=kOutput, calls=%fused_computation.25 | convolution fusion | flops 2416705536 | bytes 11012096 | tf_op jit(solution)/shard_map/dot_general | solution.py:148
  192.0 4.5 %add_convert_fusion.1 = bf16[4608,512]{1,0:T(8,128)(2,1)} fusion(bf16[4608,512]{1,0:T(8,128)(2,1)S(1)} %bitcast.92, bf16[4608,512]{0,1:T(8,128)(2,1)S(1)} %bitcast.82, bf16[512,512]{1,0:T(8,128)(2,1)S(1)} %fusion.10), kind=kOutput, calls=%fused_computation.1 | convolution fusion | flops 2422996992 | bytes 14680064 | tf_op jit(solution)/shard_map/dot_general | solution.py:166
  (93 shorter events, 11.3 us)
Async XLA Ops:
  11.8 35.0 %copy-start.1 = (f32[8,4608]{1,0:T(8,128)}, f32[8,4608]{1,0:T(8,128)S(1)}, u32[]{:S(2)}) copy-start(f32[8,4608]{1,0:T(8,128)S(1)} %reshape.56) | copy-start | bytes 442372
  31.0 9.0 %collective-permute-start = (bf16[8,8,4608]{2,1,0:T(8,128)(2,1)S(1)}, bf16[8,8,4608]{2,1,0:T(8,128)(2,1)S(1)}, u32[]{:S(2)}, u32[]{:S(2)}) collective-permute-start(bf16[8,8,4608]{2,1,0:T(8,128)(2,1)S(1)} %all_to_all.29), channel_id=1, source_target_pairs={{17,0},{9,8},{19,2},{11,10},{21,4},{13,12},{23,6},{15,14},{16,1},{... | collective-permute-start | bytes 1769480 | tf_op jit(solution)/shard_map/ppermute | solution.py:29
  31.0 9.0 %collective-permute-start.2 = (bf16[8,8,4608]{2,1,0:T(8,128)(2,1)S(1)}, bf16[8,8,4608]{2,1,0:T(8,128)(2,1)S(1)}, u32[]{:S(2)}, u32[]{:S(2)}) collective-permute-start(bf16[8,8,4608]{2,1,0:T(8,128)(2,1)S(1)} %all_to_all.29), channel_id=1, source_target_pairs={{96,0},{40,8},{98,2},{42,10},{100,4},{44,12},{102,6},{46,14},{97,1... | collective-permute-start | bytes 1769480 | tf_op jit(solution)/shard_map/ppermute | solution.py:29
  31.0 9.0 %collective-permute-start.4 = (bf16[8,8,4608]{2,1,0:T(8,128)(2,1)S(1)}, bf16[8,8,4608]{2,1,0:T(8,128)(2,1)S(1)}, u32[]{:S(2)}, u32[]{:S(2)}) collective-permute-start(bf16[8,8,4608]{2,1,0:T(8,128)(2,1)S(1)} %all_to_all.29), channel_id=1, source_target_pairs={{6,0},{10,8},{4,2},{8,10},{2,4},{14,12},{0,6},{12,14},{7,1},{11,9}... | collective-permute-start | bytes 1769480 | tf_op jit(solution)/shard_map/ppermute | solution.py:29
  40.1 7.5 %slice-start.4 = ((s8[4718592]{0:T(1024)(128)(4,1)}), s8[4194304]{0:T(1024)(128)(4,1)S(1)}, s32[]{:S(2)}) async-start(s8[4718592]{0:T(1024)(128)(4,1)} %bitcast.87), calls=%async_computation.8 | async-start | bytes 8388608
  40.4 7.2 %slice-start.5 = ((s8[4718592]{0:T(1024)(128)(4,1)}), s8[524288]{0:T(1024)(128)(4,1)S(1)}, s32[]{:S(2)}) async-start(s8[4718592]{0:T(1024)(128)(4,1)} %bitcast.87), calls=%async_computation.9 | async-start | bytes 1048576
  40.4 7.2 %copy-start.7 = (f32[512]{0:T(512)S(1)}, f32[512]{0:T(512)}, u32[]{:S(2)}) copy-start(f32[512]{0:T(512)} %param.8) | copy-start | bytes 6148
  40.4 6.7 %collective-permute-start.7 = (bf16[32,8,4608]{2,1,0:T(8,128)(2,1)S(1)}, bf16[32,8,4608]{2,1,0:T(8,128)(2,1)S(1)}, u32[]{:S(2)}, u32[]{:S(2)}) collective-permute-start(bf16[32,8,4608]{2,1,0:T(8,128)(2,1)S(1)} %pad_maximum_fusion.3), channel_id=1, source_target_pairs={{0,8},{8,0},{1,9},{9,1},{2,10},{10,2},{3,11},{11,3},{4,12},{12,4},... | collective-permute-start | bytes 7077896 | tf_op jit(solution)/shard_map/ppermute | solution.py:50
  43.0 10.9 %collective-permute-start.6 = (bf16[8,8,4608]{2,1,0:T(8,128)(2,1)S(1)}, bf16[8,8,4608]{2,1,0:T(8,128)(2,1)S(1)}, u32[]{:S(2)}, u32[]{:S(2)}) collective-permute-start(bf16[8,8,4608]{2,1,0:T(8,128)(2,1)S(1)} %all_to_all.29), channel_id=1, source_target_pairs={{119,0},{43,8},{117,2},{41,10},{115,4},{47,12},{113,6},{45,14},{11... | collective-permute-start | bytes 1769480 | tf_op jit(solution)/shard_map/ppermute | solution.py:29
  43.0 16.0 %collective-permute-start.1 = (bf16[8,8,4608]{2,1,0:T(8,128)(2,1)S(1)}, bf16[8,8,4608]{2,1,0:T(8,128)(2,1)S(1)}, u32[]{:S(2)}, u32[]{:S(2)}) collective-permute-start(bf16[8,8,4608]{2,1,0:T(8,128)(2,1)S(1)} %collective-permute-done), channel_id=1, source_target_pairs={{6,0},{10,8},{4,2},{8,10},{2,4},{14,12},{0,6},{12,14},{7,1},{11,9}... | collective-permute-start | bytes 1769480 | tf_op jit(solution)/shard_map/ppermute | solution.py:29
  45.0 14.4 %collective-permute-start.3 = (bf16[8,8,4608]{2,1,0:T(8,128)(2,1)S(1)}, bf16[8,8,4608]{2,1,0:T(8,128)(2,1)S(1)}, u32[]{:S(2)}, u32[]{:S(2)}) collective-permute-start(bf16[8,8,4608]{2,1,0:T(8,128)(2,1)S(1)} %collective-permute-done.2), channel_id=1, source_target_pairs={{17,0},{9,8},{19,2},{11,10},{21,4},{13,12},{23,6},{15,14},{16,1},{... | collective-permute-start | bytes 1769480 | tf_op jit(solution)/shard_map/ppermute | solution.py:29
  45.8 14.3 %collective-permute-start.5 = (bf16[8,8,4608]{2,1,0:T(8,128)(2,1)S(1)}, bf16[8,8,4608]{2,1,0:T(8,128)(2,1)S(1)}, u32[]{:S(2)}, u32[]{:S(2)}) collective-permute-start(bf16[8,8,4608]{2,1,0:T(8,128)(2,1)S(1)} %collective-permute-done.4), channel_id=1, source_target_pairs={{96,0},{40,8},{98,2},{42,10},{100,4},{44,12},{102,6},{46,14},{97,1... | collective-permute-start | bytes 1769480 | tf_op jit(solution)/shard_map/ppermute | solution.py:29
  47.6 2.6 %copy-start.6 = (f32[512]{0:T(512)S(1)}, f32[512]{0:T(512)}, u32[]{:S(2)}) copy-start(f32[512]{0:T(512)} %param.9) | copy-start | bytes 6148
  60.1 9.1 %slice-start.6 = ((s8[4718592]{0:T(1024)(128)(4,1)}), s8[524288]{0:T(1024)(128)(4,1)S(1)}, s32[]{:S(2)}) async-start(s8[4718592]{0:T(1024)(128)(4,1)} %bitcast.89), calls=%async_computation.10 | async-start | bytes 1048576
  60.4 8.8 %slice-start.7 = ((s8[4718592]{0:T(1024)(128)(4,1)}), s8[4194304]{0:T(1024)(128)(4,1)S(1)}, s32[]{:S(2)}) async-start(s8[4718592]{0:T(1024)(128)(4,1)} %bitcast.89), calls=%async_computation.11 | async-start | bytes 8388608
  60.4 8.8 %collective-permute-start.8 = (bf16[32,8,4608]{2,1,0:T(8,128)(2,1)S(1)}, bf16[32,8,4608]{2,1,0:T(8,128)(2,1)S(1)}, u32[]{:S(2)}, u32[]{:S(2)}) collective-permute-start(bf16[32,8,4608]{2,1,0:T(8,128)(2,1)S(1)} %pad_maximum_fusion.4), channel_id=1, source_target_pairs={{0,8},{8,0},{1,9},{9,1},{2,10},{10,2},{3,11},{11,3},{4,12},{12,4},... | collective-permute-start | bytes 7077896 | tf_op jit(solution)/shard_map/ppermute | solution.py:50
  66.7 4.3 %slice-start = ((s8[4718592]{0:T(1024)(128)(4,1)}), s8[4194304]{0:T(1024)(128)(4,1)S(1)}, s32[]{:S(2)}) async-start(s8[4718592]{0:T(1024)(128)(4,1)} %bitcast.75), calls=%async_computation.4 | async-start | bytes 8388608
  69.2 1.7 slice-start.1
  74.1 4.6 %collective-permute-start.9 = (bf16[256,4608]{1,0:T(8,128)(2,1)S(1)}, bf16[256,4608]{1,0:T(8,128)(2,1)S(1)}, u32[]{:S(2)}, u32[]{:S(2)}) collective-permute-start(bf16[256,4608]{1,0:T(8,128)(2,1)S(1)} %get-tuple-element.89), channel_id=1, source_target_pairs={{0,8},{8,0},{1,9},{9,1},{2,10},{10,2},{3,11},{11,3},{4,12},{12,4},... | collective-permute-start | bytes 7077896 | tf_op jit(solution)/shard_map/ppermute | solution.py:50
  77.4 6.7 %collective-permute-start.10 = (bf16[256,4608]{1,0:T(8,128)(2,1)S(1)}, bf16[256,4608]{1,0:T(8,128)(2,1)S(1)}, u32[]{:S(2)}, u32[]{:S(2)}) collective-permute-start(bf16[256,4608]{1,0:T(8,128)(2,1)S(1)} %get-tuple-element.88), channel_id=1, source_target_pairs={{0,8},{8,0},{1,9},{9,1},{2,10},{10,2},{3,11},{11,3},{4,12},{12,4},... | collective-permute-start | bytes 7077896 | tf_op jit(solution)/shard_map/ppermute | solution.py:50
  80.3 9.0 %collective-permute-start.11 = (bf16[8,8,4608]{2,1,0:T(8,128)(2,1)S(1)}, bf16[8,8,4608]{2,1,0:T(8,128)(2,1)S(1)}, u32[]{:S(2)}, u32[]{:S(2)}) collective-permute-start(bf16[8,8,4608]{2,1,0:T(8,128)(2,1)S(1)} %get-tuple-element.93), channel_id=1, source_target_pairs={{96,0},{40,8},{98,2},{42,10},{100,4},{44,12},{102,6},{46,14},{97,1... | collective-permute-start | bytes 1769480 | tf_op jit(solution)/shard_map/ppermute | solution.py:29
  80.3 10.0 %collective-permute-start.13 = (bf16[8,8,4608]{2,1,0:T(8,128)(2,1)S(1)}, bf16[8,8,4608]{2,1,0:T(8,128)(2,1)S(1)}, u32[]{:S(2)}, u32[]{:S(2)}) collective-permute-start(bf16[8,8,4608]{2,1,0:T(8,128)(2,1)S(1)} %get-tuple-element.92), channel_id=1, source_target_pairs={{6,0},{10,8},{4,2},{8,10},{2,4},{14,12},{0,6},{12,14},{7,1},{11,9}... | collective-permute-start | bytes 1769480 | tf_op jit(solution)/shard_map/ppermute | solution.py:29
  80.3 15.5 %collective-permute-start.15 = (bf16[8,8,4608]{2,1,0:T(8,128)(2,1)S(1)}, bf16[8,8,4608]{2,1,0:T(8,128)(2,1)S(1)}, u32[]{:S(2)}, u32[]{:S(2)}) collective-permute-start(bf16[8,8,4608]{2,1,0:T(8,128)(2,1)S(1)} %get-tuple-element.91), channel_id=1, source_target_pairs={{17,0},{9,8},{19,2},{11,10},{21,4},{13,12},{23,6},{15,14},{16,1},{... | collective-permute-start | bytes 1769480 | tf_op jit(solution)/shard_map/ppermute | solution.py:29
  80.3 22.8 %collective-permute-start.17 = (bf16[8,8,4608]{2,1,0:T(8,128)(2,1)}, bf16[8,8,4608]{2,1,0:T(8,128)(2,1)}, u32[]{:S(2)}, u32[]{:S(2)}) collective-permute-start(bf16[8,8,4608]{2,1,0:T(8,128)(2,1)} %get-tuple-element.90), channel_id=1, source_target_pairs={{119,0},{43,8},{117,2},{41,10},{115,4},{47,12},{113,6},{45,14},{11... | collective-permute-start | bytes 1769480 | tf_op jit(solution)/shard_map/ppermute | solution.py:29
  96.2 9.1 %collective-permute-start.12 = (bf16[8,8,4608]{2,1,0:T(8,128)(2,1)S(1)}, bf16[8,8,4608]{2,1,0:T(8,128)(2,1)S(1)}, u32[]{:S(2)}, u32[]{:S(2)}) collective-permute-start(bf16[8,8,4608]{2,1,0:T(8,128)(2,1)S(1)} %get-tuple-element.96), channel_id=1, source_target_pairs={{6,0},{10,8},{4,2},{8,10},{2,4},{14,12},{0,6},{12,14},{7,1},{11,9}... | collective-permute-start | bytes 1769480 | tf_op jit(solution)/shard_map/ppermute | solution.py:29
  97.7 9.0 %collective-permute-start.14 = (bf16[8,8,4608]{2,1,0:T(8,128)(2,1)S(1)}, bf16[8,8,4608]{2,1,0:T(8,128)(2,1)S(1)}, u32[]{:S(2)}, u32[]{:S(2)}) collective-permute-start(bf16[8,8,4608]{2,1,0:T(8,128)(2,1)S(1)} %get-tuple-element.95), channel_id=1, source_target_pairs={{17,0},{9,8},{19,2},{11,10},{21,4},{13,12},{23,6},{15,14},{16,1},{... | collective-permute-start | bytes 1769480 | tf_op jit(solution)/shard_map/ppermute | solution.py:29
  97.7 9.0 %collective-permute-start.16 = (bf16[8,8,4608]{2,1,0:T(8,128)(2,1)S(1)}, bf16[8,8,4608]{2,1,0:T(8,128)(2,1)S(1)}, u32[]{:S(2)}, u32[]{:S(2)}) collective-permute-start(bf16[8,8,4608]{2,1,0:T(8,128)(2,1)S(1)} %get-tuple-element.94), channel_id=1, source_target_pairs={{96,0},{40,8},{98,2},{42,10},{100,4},{44,12},{102,6},{46,14},{97,1... | collective-permute-start | bytes 1769480 | tf_op jit(solution)/shard_map/ppermute | solution.py:29
  103.2 18.9 %copy-start.2 = (f32[8,4608]{1,0:T(8,128)S(1)}, f32[8,4608]{1,0:T(8,128)}, u32[]{:S(2)}) copy-start(f32[8,4608]{1,0:T(8,128)} %copy-done.1) | copy-start | bytes 442372
  103.2 19.0 %copy-start.5 = (f32[4608]{0:T(1024)S(1)}, f32[4608]{0:T(1024)}, u32[]{:S(2)}) copy-start(f32[4608]{0:T(1024)} %param.11) | copy-start | bytes 55300
  135.8 8.7 %collective-permute-start.18 = (bf16[8,8,4608]{2,1,0:T(8,128)(2,1)S(1)}, bf16[8,8,4608]{2,1,0:T(8,128)(2,1)S(1)}, u32[]{:S(2)}, u32[]{:S(2)}) collective-permute-start(bf16[8,8,4608]{2,1,0:T(8,128)(2,1)S(1)} %all_to_all.31), channel_id=1, source_target_pairs={{6,0},{10,8},{4,2},{8,10},{2,4},{14,12},{0,6},{12,14},{7,1},{11,9}... | collective-permute-start | bytes 1769480 | tf_op jit(solution)/shard_map/ppermute | solution.py:29
  135.8 8.7 %collective-permute-start.19 = (bf16[8,8,4608]{2,1,0:T(8,128)(2,1)S(1)}, bf16[8,8,4608]{2,1,0:T(8,128)(2,1)S(1)}, u32[]{:S(2)}, u32[]{:S(2)}) collective-permute-start(bf16[8,8,4608]{2,1,0:T(8,128)(2,1)S(1)} %all_to_all.31), channel_id=1, source_target_pairs={{17,0},{9,8},{19,2},{11,10},{21,4},{13,12},{23,6},{15,14},{16,1},{... | collective-permute-start | bytes 1769480 | tf_op jit(solution)/shard_map/ppermute | solution.py:29
  135.8 9.2 %collective-permute-start.20 = (bf16[8,8,4608]{2,1,0:T(8,128)(2,1)S(1)}, bf16[8,8,4608]{2,1,0:T(8,128)(2,1)S(1)}, u32[]{:S(2)}, u32[]{:S(2)}) collective-permute-start(bf16[8,8,4608]{2,1,0:T(8,128)(2,1)S(1)} %all_to_all.31), channel_id=1, source_target_pairs={{96,0},{40,8},{98,2},{42,10},{100,4},{44,12},{102,6},{46,14},{97,1... | collective-permute-start | bytes 1769480 | tf_op jit(solution)/shard_map/ppermute | solution.py:29
  145.3 14.8 %copy-start.3 = (f32[512,512]{1,0:T(8,128)S(1)}, f32[512,512]{1,0:T(8,128)}, u32[]{:S(2)}) copy-start(f32[512,512]{1,0:T(8,128)} %get-tuple-element.46) | copy-start | bytes 3145732
  145.3 14.4 %collective-permute-start.21 = (bf16[32,8,4608]{2,1,0:T(8,128)(2,1)S(1)}, bf16[32,8,4608]{2,1,0:T(8,128)(2,1)S(1)}, u32[]{:S(2)}, u32[]{:S(2)}) collective-permute-start(bf16[32,8,4608]{2,1,0:T(8,128)(2,1)S(1)} %pad_maximum_fusion.5), channel_id=1, source_target_pairs={{0,8},{8,0},{1,9},{9,1},{2,10},{10,2},{3,11},{11,3},{4,12},{12,4},... | collective-permute-start | bytes 7077896 | tf_op jit(solution)/shard_map/ppermute | solution.py:50
  155.5 11.5 %collective-permute-start.25 = (bf16[8,8,4608]{2,1,0:T(8,128)(2,1)S(1)}, bf16[8,8,4608]{2,1,0:T(8,128)(2,1)S(1)}, u32[]{:S(2)}, u32[]{:S(2)}) collective-permute-start(bf16[8,8,4608]{2,1,0:T(8,128)(2,1)S(1)} %all_to_all.31), channel_id=1, source_target_pairs={{119,0},{43,8},{117,2},{41,10},{115,4},{47,12},{113,6},{45,14},{11... | collective-permute-start | bytes 1769480 | tf_op jit(solution)/shard_map/ppermute | solution.py:29
  156.2 15.3 %collective-permute-start.22 = (bf16[8,8,4608]{2,1,0:T(8,128)(2,1)S(1)}, bf16[8,8,4608]{2,1,0:T(8,128)(2,1)S(1)}, u32[]{:S(2)}, u32[]{:S(2)}) collective-permute-start(bf16[8,8,4608]{2,1,0:T(8,128)(2,1)S(1)} %collective-permute-done.19), channel_id=1, source_target_pairs={{6,0},{10,8},{4,2},{8,10},{2,4},{14,12},{0,6},{12,14},{7,1},{11,9}... | collective-permute-start | bytes 1769480 | tf_op jit(solution)/shard_map/ppermute | solution.py:29
  157.5 14.5 %collective-permute-start.23 = (bf16[8,8,4608]{2,1,0:T(8,128)(2,1)S(1)}, bf16[8,8,4608]{2,1,0:T(8,128)(2,1)}, u32[]{:S(2)}, u32[]{:S(2)}) collective-permute-start(bf16[8,8,4608]{2,1,0:T(8,128)(2,1)S(1)} %collective-permute-done.20), channel_id=1, source_target_pairs={{17,0},{9,8},{19,2},{11,10},{21,4},{13,12},{23,6},{15,14},{16,1},{... | collective-permute-start | bytes 1769480 | tf_op jit(solution)/shard_map/ppermute | solution.py:29
  158.3 14.5 %collective-permute-start.24 = (bf16[8,8,4608]{2,1,0:T(8,128)(2,1)S(1)}, bf16[8,8,4608]{2,1,0:T(8,128)(2,1)}, u32[]{:S(2)}, u32[]{:S(2)}) collective-permute-start(bf16[8,8,4608]{2,1,0:T(8,128)(2,1)S(1)} %collective-permute-done.18), channel_id=1, source_target_pairs={{96,0},{40,8},{98,2},{42,10},{100,4},{44,12},{102,6},{46,14},{97,1... | collective-permute-start | bytes 1769480 | tf_op jit(solution)/shard_map/ppermute | solution.py:29
  174.3 9.6 %collective-permute-start.26 = (bf16[32,8,4608]{2,1,0:T(8,128)(2,1)S(1)}, bf16[32,8,4608]{2,1,0:T(8,128)(2,1)S(1)}, u32[]{:S(2)}, u32[]{:S(2)}) collective-permute-start(bf16[32,8,4608]{2,1,0:T(8,128)(2,1)S(1)} %pad_maximum_fusion.6), channel_id=1, source_target_pairs={{0,8},{8,0},{1,9},{9,1},{2,10},{10,2},{3,11},{11,3},{4,12},{12,4},... | collective-permute-start | bytes 7077896 | tf_op jit(solution)/shard_map/ppermute | solution.py:50
  183.9 1.0 copy-start
  185.0 4.3 %copy-start.4 = (f32[512,512]{1,0:T(8,128)S(1)}, f32[512,512]{1,0:T(8,128)}, u32[]{:S(2)}) copy-start(f32[512,512]{1,0:T(8,128)} %pad_maximum_fusion.7) | copy-start | bytes 3145732
  185.0 7.0 %slice-start.2 = ((s8[4718592]{0:T(1024)(128)(4,1)}), s8[4194304]{0:T(1024)(128)(4,1)S(1)}, s32[]{:S(2)}) async-start(s8[4718592]{0:T(1024)(128)(4,1)} %bitcast.81), calls=%async_computation.6 | async-start | bytes 8388608
  185.0 7.0 %slice-start.8 = ((s8[4718592]{0:T(1024)(128)(4,1)}), s8[524288]{0:T(1024)(128)(4,1)S(1)}, s32[]{:S(2)}) async-start(s8[4718592]{0:T(1024)(128)(4,1)} %bitcast.91), calls=%async_computation.12 | async-start | bytes 1048576
  189.3 2.7 %slice-start.3 = ((s8[4718592]{0:T(1024)(128)(4,1)}), s8[524288]{0:T(1024)(128)(4,1)S(1)}, s32[]{:S(2)}) async-start(s8[4718592]{0:T(1024)(128)(4,1)} %bitcast.81), calls=%async_computation.7 | async-start | bytes 1048576
  189.3 2.7 %slice-start.9 = ((s8[4718592]{0:T(1024)(128)(4,1)}), s8[4194304]{0:T(1024)(128)(4,1)S(1)}, s32[]{:S(2)}) async-start(s8[4718592]{0:T(1024)(128)(4,1)} %bitcast.91), calls=%async_computation.13 | async-start | bytes 8388608

commit v4 on v3

--- a/solution.py
+++ b/solution.py
@@ -65,9 +65,10 @@
 def gather(own, work):
     copies, = barrier(jnp.broadcast_to(own, (8, *own.shape)))
     block, = barrier(trade(copies, 0))
-    x, y, z, xyz = (receive(block, corner, 1) for corner in ("x", "y", "z", "xyz"))
+    x, y, z = (receive(block, axis, 1) for axis in "xyz")
     near, = barrier(jnp.concatenate([block, x, y, z]))
     xy, yz, zx = receive(y, "x", 1), receive(z, "y", 1), receive(x, "z", 1)
+    xyz = receive(z, "xy", 1)
     near, = barrier(jnp.concatenate([near, swap(near)]))
     near = flat(near)
     done = work(near)
@@ -77,8 +78,7 @@
 
 
 def scatter(near, distant, work):
-    xy, yz, zx, xyz = jnp.split(distant.reshape(32, 8, -1), 4)
-    own, x, y, z = jnp.split(near.reshape(32, 8, -1), 4)
+    (own, x, y, z), (xy, yz, zx, xyz) = near, distant
     y_more, z_more, x_more = receive(xy, "x", 1), receive(yz, "y", 1), receive(zx, "z", 1)
     xyz = receive(xyz, "xyz", 1)
     x, y, z = (add(*pair).astype(bf16) for pair in ((x, x_more), (y, y_more), (z, z_more)))
@@ -109,18 +109,16 @@
     code_theirs, slopes_theirs, totals_theirs = encode(theirs)
     totals = totals_near + totals_mine + totals_theirs
 
-    code_mine_all, code_theirs_all = barrier(
-        jnp.concatenate([code_mine, code_near[:256]]),
-        jnp.concatenate([code_theirs, code_near[256:]]),
-    )
-    recon_theirs = jnp.dot(code_theirs_all, dec_weight, preferred_element_type=f32).astype(bf16)
-    recon_theirs = swap(recon_theirs[:256]), swap(recon_theirs[256:])
-    recon_mine, = barrier(
-        jnp.dot(code_mine_all, dec_weight, preferred_element_type=f32).astype(bf16)
-    )
-    recon_distant, = barrier(add(recon_mine[:256], recon_theirs[0]).astype(bf16))
-    recon_mine, recon_distant = barrier(recon_mine, recon_distant)
-    recon_near = add(recon_mine[256:], recon_theirs[1]).astype(bf16)
+    def decode(mine, theirs):
+        theirs, mine = (
+            barrier(jnp.dot(rows, dec_weight, preferred_element_type=f32).astype(bf16))[0]
+            for rows in (theirs, mine)
+        )
+        pairs = zip(*(jnp.split(rows.reshape(32, 8, -1), 4) for rows in (mine, swap(theirs))))
+        return barrier(*(add(*pair).astype(bf16) for pair in pairs))
+
+    recon_near = decode(code_near[:256], code_near[256:])
+    recon_distant = decode(code_mine, code_theirs)
 
     def side_work(received):
         *rest, dec, _ = barrier(
@@ -134,13 +132,14 @@
             code_rows.T,
             jnp.concatenate([mine_rows, their_rows]).T,
             jnp.concatenate([mine_code, their_code]).T,
-            jnp.concatenate(slopes),
+            *slopes,
             sparsity_coeff * row_scale * row_norms,
             sparsity_coeff * row_scale * totals / row_norms,
         )
 
     recon, work = scatter(recon_near, recon_distant, side_work)
-    near_t, code_near_t, distant_t, code_distant_t, slopes_distant, norm_grad, norm_scale = work
+    near_t, code_near_t, distant_t, code_distant_t, slopes_mine, slopes_theirs, *norms = work
+    norm_grad, norm_scale = norms
     recon_error = recon + dec_bias - own_rows
     own_delta, = barrier((recon_error * row_scale).astype(bf16))
 
@@ -160,9 +159,10 @@
     grad_dec = jnp.dot(code_near_t, delta_near, preferred_element_type=f32)
     grad_dec = (grad_dec + norm_scale[:, None] * dec_weight.astype(f32)).astype(bf16)
     grad_dec, = barrier(grad_dec)
+    preact_mine = preact_grad(mine, slopes_mine)
     theirs, _ = barrier(theirs, grad_dec)
     delta, = barrier(jnp.concatenate([mine, theirs]))
-    preact = preact_grad(delta, slopes_distant)
+    preact, = barrier(jnp.concatenate([preact_mine, preact_grad(theirs, slopes_theirs)]))
     grad_enc = grad_enc + jnp.dot(distant_t, preact, preferred_element_type=f32)
     grad_dec = grad_dec + jnp.dot(code_distant_t, delta, preferred_element_type=f32)
     return (grad_enc.astype(bf16), grad_dec.astype(bf16))

time: 197 us -> 186 us (0.944)
  starting transfers between devices: 37.7 us -> 24.6 us
    ppermute x6, starting transfers between devices: 23.5 us -> 13.8 us  [swap(): return lax.ppermute(block, 'core', [(0, 1), (1, 0)])]
    ppermute x21, starting transfers between devices: 14.1 us -> 10.8 us  [receive(): return lax.ppermute(block, MESH, pairs)]
    transpose x1, other arithmetic: 2.45 us -> 0.31 us  [side_work(): jnp.concatenate([mine_rows, their_rows])]
    dot_general x2 -> x3, matrix products: 5.25 us -> 6.68 us  [preact_grad(): lax.dot_general(delta, dec_weight, (((1,), (1,)), ((), ())), preferred_el...]
    dot_general x2 -> x4, matrix products: 5.66 us -> 5.55 us  [decode(): jnp.dot(rows, dec_weight, preferred_element_type=f32).astype(bf16)]
  transfers between devices with their start and end apart: 27 -> 27, of which waited for: 19 -> 15; matrix products, arithmetic and copies ran while one was open for 14% -> 16% of each run, Pallas kernels for 0% -> 0%
where the time goes in v4:
time: 186 us; the launch traced here: 185 us
  blocking collectives  57.2 us (31%)
  waiting for transfers between devices  52.8 us (28%)
  matrix products  33.7 us (18%)
  starting transfers between devices  24.6 us (13%)
  other arithmetic  14.8 us (8%)
    ppermute x21, waiting for transfers between devices, receive(): return lax.ppermute(block, MESH, pairs)  47.5 us
    all_to_all x3, blocking collectives, trade(): return lax.all_to_all(blocks, MESH, 0, 0, axis_index_groups=cubes(pairing))  46.2 us
    ppermute x6, starting transfers between devices, swap(): return lax.ppermute(block, 'core', [(0, 1), (1, 0)])  13.8 us
    all_to_all x1, blocking collectives, on_device(): lax.all_to_all(activations, ('x', 'yl'), split_axis=0, concat_axis=1, til...  11 us
    ppermute x21, starting transfers between devices, receive(): return lax.ppermute(block, MESH, pairs)  10.8 us
    dot_general x3, matrix products, preact_grad(): lax.dot_general(delta, dec_weight, (((1,), (1,)), ((), ())), preferred_el...  6.68 us
    dot_general x4, matrix products, decode(): jnp.dot(rows, dec_weight, preferred_element_type=f32).astype(bf16)  5.55 us
    dot_general x3, matrix products, encode(): jnp.dot(rows, enc_weight, preferred_element_type=f32) + enc_bias  5.38 us
  transfers between devices with their start and end apart: 27, of which 15 were waited for; matrix products, arithmetic and copies ran while one was open for 16% of the time, Pallas kernels for 0%

profile of v4, /device:TPU:1, one launch (start us, length us, event | category | flops | bytes accessed | tf_op | source)
XLA Modules:
  0.0 185.2 jit_solution(2344537399491145544)
XLA Ops:
  0.6 11.0 %all_to_all.28 = bf16[8,8,576]{2,1,0:T(8,128)(2,1)S(1)} all-to-all(bf16[8,8,576]{2,1,0:T(8,128)(2,1)} %bitcast.78), channel_id=1, replica_groups=mesh['z'=4,'yh'=2,'core'=2,'x'=4,'yl'=2] {'x','yl'}, dimensions={0} | all-to-all | bytes 147456 | tf_op jit(solution)/shard_map/all_to_all | solution.py:94
  12.6 18.5 %all_to_all.29 = bf16[8,8,4608]{2,1,0:T(8,128)(2,1)S(1)} all-to-all(bf16[8,8,4608]{2,1,0:T(8,128)(2,1)S(1)} %broadcast_in_dim.4), channel_id=1, replica_groups={{0,2,1,3,32,34,33,35},{4,6,5,7,36,38,37,39},{16,18,17,19,48,50,49,51},{..., dimensions={0} | all-to-all | bytes 1179648 | tf_op jit(solution)/shard_map/all_to_all | solution.py:46
  31.1 9.0 %collective-permute-done.2 = bf16[8,8,4608]{2,1,0:T(8,128)(2,1)S(1)} collective-permute-done((bf16[8,8,4608]{2,1,0:T(8,128)(2,1)S(1)}, bf16[8,8,4608]{2,1,0:T(8,128)(2,1)S(1)}, u32[]{:S(2)}, u32[]{:S(2)}) %collective-permute-start.2) | collective-permute-done | bytes 589856 | tf_op jit(solution)/shard_map/ppermute | solution.py:29
  40.5 2.4 %collective-permute-start.3 = (bf16[32,8,4608]{2,1,0:T(8,128)(2,1)S(1)}, bf16[32,8,4608]{2,1,0:T(8,128)(2,1)S(1)}, u32[]{:S(2)}, u32[]{:S(2)}) collective-permute-start(bf16[32,8,4608]{2,1,0:T(8,128)(2,1)S(1)} %pad_maximum_fusion.3), channel_id=1, source_target_pairs={{0,8},{8,0},{1,9},{9,1},{2,10},{10,2},{3,11},{11,3},{4,12},{12,4},... | collective-permute-start | bytes 7077896 | tf_op jit(solution)/shard_map/ppermute | solution.py:50
  43.5 2.1 %collective-permute-start.5 = (bf16[8,8,4608]{2,1,0:T(8,128)(2,1)S(1)}, bf16[8,8,4608]{2,1,0:T(8,128)(2,1)S(1)}, u32[]{:S(2)}, u32[]{:S(2)}) collective-permute-start(bf16[8,8,4608]{2,1,0:T(8,128)(2,1)S(1)} %collective-permute-done.1), channel_id=1, source_target_pairs={{6,0},{10,8},{4,2},{8,10},{2,4},{14,12},{0,6},{12,14},{7,1},{11,9}... | collective-permute-start | bytes 1769480 | tf_op jit(solution)/shard_map/ppermute | solution.py:29
  46.1 1.0 collective-permute-done.3
  47.6 2.6 %convolution_add_fusion = f32[512,512]{1,0:T(8,128)S(1)} fusion(bf16[4608,512]{1,0:T(8,128)(2,1)S(1)} %bitcast.80, f32[512]{0:T(512)S(1)} %copy-done.9, bf16[64,8,4608]{2,1,0:T(8,128)(2,1)S(1)} %pad_maximum_fusion), kind=kOutput, calls=%fused_computation.22 | convolution fusion | flops 2416181248 | bytes 10487808 | tf_op jit(solution)/shard_map/dot_general | solution.py:99
  50.2 1.4 fusion.37
  51.7 1.3 collective-permute-done.8
  52.9 5.4 %collective-permute-done.6 = bf16[8,8,4608]{2,1,0:T(8,128)(2,1)S(1)} collective-permute-done((bf16[8,8,4608]{2,1,0:T(8,128)(2,1)S(1)}, bf16[8,8,4608]{2,1,0:T(8,128)(2,1)S(1)}, u32[]{:S(2)}, u32[]{:S(2)}) %collective-permute-start.6) | collective-permute-done | bytes 589856 | tf_op jit(solution)/shard_map/ppermute | solution.py:29
  59.0 3.7 %collective-permute-start.9 = (bf16[32,8,4608]{2,1,0:T(8,128)(2,1)S(1)}, bf16[32,8,4608]{2,1,0:T(8,128)(2,1)S(1)}, u32[]{:S(2)}, u32[]{:S(2)}) collective-permute-start(bf16[32,8,4608]{2,1,0:T(8,128)(2,1)S(1)} %pad_maximum_fusion.4), channel_id=1, source_target_pairs={{0,8},{8,0},{1,9},{9,1},{2,10},{10,2},{3,11},{11,3},{4,12},{12,4},... | collective-permute-start | bytes 7077896 | tf_op jit(solution)/shard_map/ppermute | solution.py:50
  62.7 1.4 convolution_add_fusion.4
  64.1 1.1 fusion.35
  65.2 1.7 collective-permute-done.9
  66.9 1.4 convolution_add_fusion.3
  68.3 1.0 fusion.33
  69.3 1.4 convolution_convert_fusion.1
  71.1 1.4 convolution_convert_fusion.3
  72.9 1.4 convolution_convert_fusion.2
  74.3 1.4 convolution_convert_fusion.4
  77.0 1.7 collective-permute-done.4
  79.6 2.8 %collective-permute-start.17 = (bf16[8,8,4608]{2,1,0:T(8,128)(2,1)S(1)}, bf16[8,8,4608]{2,1,0:T(8,128)(2,1)S(1)}, u32[]{:S(2)}, u32[]{:S(2)}) collective-permute-start(bf16[8,8,4608]{2,1,0:T(8,128)(2,1)S(1)} %get-tuple-element.66), channel_id=1, source_target_pairs={{119,0},{43,8},{117,2},{41,10},{115,4},{47,12},{113,6},{45,14},{11... | collective-permute-start | bytes 1769480 | tf_op jit(solution)/shard_map/ppermute | solution.py:29
  82.5 3.0 %collective-permute-done.11 = bf16[8,8,4608]{2,1,0:T(8,128)(2,1)S(1)} collective-permute-done((bf16[8,8,4608]{2,1,0:T(8,128)(2,1)S(1)}, bf16[8,8,4608]{2,1,0:T(8,128)(2,1)S(1)}, u32[]{:S(2)}, u32[]{:S(2)}) %collective-permute-start.11) | collective-permute-done | bytes 589856 | tf_op jit(solution)/shard_map/ppermute | solution.py:29
  85.6 2.9 %collective-permute-done.13 = bf16[8,8,4608]{2,1,0:T(8,128)(2,1)S(1)} collective-permute-done((bf16[8,8,4608]{2,1,0:T(8,128)(2,1)S(1)}, bf16[8,8,4608]{2,1,0:T(8,128)(2,1)S(1)}, u32[]{:S(2)}, u32[]{:S(2)}) %collective-permute-start.13) | collective-permute-done | bytes 589856 | tf_op jit(solution)/shard_map/ppermute | solution.py:29
  88.8 1.0 multiply_reduce_fusion
  89.8 5.2 %collective-permute-done.15 = bf16[8,8,4608]{2,1,0:T(8,128)(2,1)S(1)} collective-permute-done((bf16[8,8,4608]{2,1,0:T(8,128)(2,1)S(1)}, bf16[8,8,4608]{2,1,0:T(8,128)(2,1)S(1)}, u32[]{:S(2)}, u32[]{:S(2)}) %collective-permute-start.15) | collective-permute-done | bytes 589856 | tf_op jit(solution)/shard_map/ppermute | solution.py:29
  94.9 1.0 add_convert_fusion.4
  97.6 3.6 %collective-permute-done.12 = bf16[8,8,4608]{2,1,0:T(8,128)(2,1)S(1)} collective-permute-done((bf16[8,8,4608]{2,1,0:T(8,128)(2,1)S(1)}, bf16[8,8,4608]{2,1,0:T(8,128)(2,1)S(1)}, u32[]{:S(2)}, u32[]{:S(2)}) %collective-permute-start.12) | collective-permute-done | bytes 589856 | tf_op jit(solution)/shard_map/ppermute | solution.py:29
  101.3 3.9 %collective-permute-done.16 = bf16[8,8,4608]{2,1,0:T(8,128)(2,1)S(1)} collective-permute-done((bf16[8,8,4608]{2,1,0:T(8,128)(2,1)}, bf16[8,8,4608]{2,1,0:T(8,128)(2,1)S(1)}, u32[]{:S(2)}, u32[]{:S(2)}) %collective-permute-start.16) | collective-permute-done | bytes 589856 | tf_op jit(solution)/shard_map/ppermute | solution.py:29
  105.5 14.1 %all_to_all.30 = bf16[8,8,4608]{2,1,0:T(8,128)(2,1)S(1)} all-to-all(bf16[8,8,4608]{2,1,0:T(8,128)(2,1)S(1)} %add_convert_fusion.3), channel_id=1, replica_groups={{0,2,1,3,32,34,33,35},{4,6,5,7,36,38,37,39},{16,18,17,19,48,50,49,51},{..., dimensions={0} | all-to-all | bytes 1179648 | tf_op jit(solution)/shard_map/all_to_all | solution.py:46
  119.8 13.6 %all_to_all.31 = bf16[8,8,4608]{2,1,0:T(8,128)(2,1)S(1)} all-to-all(bf16[8,8,4608]{2,1,0:T(8,128)(2,1)S(1)} %broadcast_in_dim.5), channel_id=1, replica_groups={{0,2,1,3,32,34,33,35},{4,6,5,7,36,38,37,39},{16,18,17,19,48,50,49,51},{..., dimensions={0} | all-to-all | bytes 1179648 | tf_op jit(solution)/shard_map/all_to_all | solution.py:46
  133.4 9.1 %collective-permute-done.20 = bf16[8,8,4608]{2,1,0:T(8,128)(2,1)} collective-permute-done((bf16[8,8,4608]{2,1,0:T(8,128)(2,1)S(1)}, bf16[8,8,4608]{2,1,0:T(8,128)(2,1)}, u32[]{:S(2)}, u32[]{:S(2)}) %collective-permute-start.20) | collective-permute-done | bytes 589856 | tf_op jit(solution)/shard_map/ppermute | solution.py:29
  142.5 1.7 pad_maximum_fusion.5
  144.3 2.8 %collective-permute-start.21 = (bf16[32,8,4608]{2,1,0:T(8,128)(2,1)S(1)}, bf16[32,8,4608]{2,1,0:T(8,128)(2,1)S(1)}, u32[]{:S(2)}, u32[]{:S(2)}) collective-permute-start(bf16[32,8,4608]{2,1,0:T(8,128)(2,1)S(1)} %pad_maximum_fusion.5), channel_id=1, source_target_pairs={{0,8},{8,0},{1,9},{9,1},{2,10},{10,2},{3,11},{11,3},{4,12},{12,4},... | collective-permute-start | bytes 7077896 | tf_op jit(solution)/shard_map/ppermute | solution.py:50
  147.0 0.9 collective-permute-start.25
  147.9 0.9 collective-permute-start.23
  148.8 0.9 collective-permute-start.22
  150.3 0.9 collective-permute-done.21
  151.6 3.9 %fusion.9 = bf16[512,512]{1,0:T(8,128)(2,1)S(1)} fusion(f32[512,512]{1,0:T(8,128)} %get-tuple-element.52, bf16[512,4608]{1,0:T(8,128)(2,1)S(1)} %bitcast.69, bf16[64,8,4608]{2,1,0:T(8,128)(2,1)S(1)} %pad_maximum_fusion.1, f32[512]{0:T(512)S(1)} %get-tuple-element.86), kind=kOutput, calls=%fused_computation.23 | convolution fusion | flops 2416705536 | bytes 11012096 | tf_op jit(solution)/shard_map/dot_general | solution.py:147
  155.5 4.3 %convolution_convert_fusion = bf16[4608,512]{1,0:T(8,128)(2,1)} fusion(bf16[4608,512]{0,1:T(8,128)(2,1)S(1)} %bitcast.72, bf16[512,512]{1,0:T(8,128)(2,1)S(1)} %fusion.9), kind=kOutput, calls=%fused_computation.4 | convolution fusion | flops 2418278400 | bytes 9961472 | tf_op jit(solution)/shard_map/dot_general | solution.py:156
  159.8 3.8 %collective-permute-done.23 = bf16[8,8,4608]{2,1,0:T(8,128)(2,1)} collective-permute-done((bf16[8,8,4608]{2,1,0:T(8,128)(2,1)}, bf16[8,8,4608]{2,1,0:T(8,128)(2,1)}, u32[]{:S(2)}, u32[]{:S(2)}) %collective-permute-start.23) | collective-permute-done | bytes 589856 | tf_op jit(solution)/shard_map/ppermute | solution.py:29
  163.6 1.9 %pad_maximum_fusion.6 = bf16[32,8,4608]{2,1,0:T(8,128)(2,1)S(1)} fusion(bf16[8,8,4608]{2,1,0:T(8,128)(2,1)} %collective-permute-done.25, bf16[8,8,4608]{2,1,0:T(8,128)(2,1)} %collective-permute-done.24, bf16[8,8,4608]{2,1,0:T(8,128)(2,1)} %collective-permute-done.23, bf16[8,8,4608]{2,1,0:T(8,128)(2,1)} %collective-permute-done.22), kind=kLoop, calls=%fused_computation.19 | loop fusion | flops 3538944 | bytes 4718592 | tf_op jit(solution)/shard_map/concatenate | solution.py:76
  165.5 4.0 %collective-permute-start.26 = (bf16[32,8,4608]{2,1,0:T(8,128)(2,1)S(1)}, bf16[32,8,4608]{2,1,0:T(8,128)(2,1)S(1)}, u32[]{:S(2)}, u32[]{:S(2)}) collective-permute-start(bf16[32,8,4608]{2,1,0:T(8,128)(2,1)S(1)} %pad_maximum_fusion.6), channel_id=1, source_target_pairs={{0,8},{8,0},{1,9},{9,1},{2,10},{10,2},{3,11},{11,3},{4,12},{12,4},... | collective-permute-start | bytes 7077896 | tf_op jit(solution)/shard_map/ppermute | solution.py:50
  169.5 3.1 %add_convert_fusion.2 = bf16[512,4608]{1,0:T(8,128)(2,1)S(1)} fusion(bf16[512,4608]{1,0:T(8,128)(2,1)S(1)} %bitcast.69, bf16[512,512]{0,1:T(8,128)(2,1)S(1)} %bitcast.77, bf16[64,8,4608]{2,1,0:T(8,128)(2,1)S(1)} %pad_maximum_fusion.1, f32[512]{0:T(512)S(1)} %get-tuple-element.94), kind=kOutput, calls=%fused_computation.2 | convolution fusion | flops 2425356288 | bytes 14682112 | tf_op jit(solution)/shard_map/dot_general | solution.py:159
  172.6 1.4 fusion.14
  174.0 1.4 fusion.15
  176.5 4.3 %add_convert_fusion = bf16[512,4608]{1,0:T(8,128)(2,1)} fusion(bf16[512,4608]{1,0:T(8,128)(2,1)S(1)} %add_convert_fusion.2, bf16[512,512]{0,1:T(8,128)(2,1)S(1)} %copy-done.2, bf16[512,4608]{1,0:T(8,128)(2,1)S(1)} %pad_maximum_fusion.2), kind=kOutput, calls=%fused_computation | convolution fusion | flops 2422996992 | bytes 14680064 | tf_op jit(solution)/shard_map/dot_general | solution.py:167
  180.8 4.4 %add_convert_fusion.1 = bf16[4608,512]{1,0:T(8,128)(2,1)} fusion(bf16[4608,512]{1,0:T(8,128)(2,1)S(1)} %bitcast.84, bf16[4608,512]{0,1:T(8,128)(2,1)S(1)} %maximum_bitcast_fusion, bf16[512,512]{1,0:T(8,128)(2,1)S(1)} %pad_maximum_fusion.7), kind=kOutput, calls=%fused_computation.1 | convolution fusion | flops 2422996992 | bytes 14680064 | tf_op jit(solution)/shard_map/dot_general | solution.py:166
  (93 shorter events, 11.2 us)
Async XLA Ops:
  11.8 28.7 %copy-start.3 = (f32[8,4608]{1,0:T(8,128)}, f32[8,4608]{1,0:T(8,128)S(1)}, u32[]{:S(2)}) copy-start(f32[8,4608]{1,0:T(8,128)S(1)} %reshape.90) | copy-start | bytes 442372
  31.1 9.0 %collective-permute-start.2 = (bf16[8,8,4608]{2,1,0:T(8,128)(2,1)S(1)}, bf16[8,8,4608]{2,1,0:T(8,128)(2,1)S(1)}, u32[]{:S(2)}, u32[]{:S(2)}) collective-permute-start(bf16[8,8,4608]{2,1,0:T(8,128)(2,1)S(1)} %all_to_all.29), channel_id=1, source_target_pairs={{96,0},{40,8},{98,2},{42,10},{100,4},{44,12},{102,6},{46,14},{97,1... | collective-permute-start | bytes 1769480 | tf_op jit(solution)/shard_map/ppermute | solution.py:29
  31.1 9.0 %collective-permute-start.1 = (bf16[8,8,4608]{2,1,0:T(8,128)(2,1)S(1)}, bf16[8,8,4608]{2,1,0:T(8,128)(2,1)S(1)}, u32[]{:S(2)}, u32[]{:S(2)}) collective-permute-start(bf16[8,8,4608]{2,1,0:T(8,128)(2,1)S(1)} %all_to_all.29), channel_id=1, source_target_pairs={{17,0},{9,8},{19,2},{11,10},{21,4},{13,12},{23,6},{15,14},{16,1},{... | collective-permute-start | bytes 1769480 | tf_op jit(solution)/shard_map/ppermute | solution.py:29
  31.1 9.0 %collective-permute-start = (bf16[8,8,4608]{2,1,0:T(8,128)(2,1)S(1)}, bf16[8,8,4608]{2,1,0:T(8,128)(2,1)S(1)}, u32[]{:S(2)}, u32[]{:S(2)}) collective-permute-start(bf16[8,8,4608]{2,1,0:T(8,128)(2,1)S(1)} %all_to_all.29), channel_id=1, source_target_pairs={{6,0},{10,8},{4,2},{8,10},{2,4},{14,12},{0,6},{12,14},{7,1},{11,9}... | collective-permute-start | bytes 1769480 | tf_op jit(solution)/shard_map/ppermute | solution.py:29
  40.2 7.4 %slice-start.2 = ((s8[4718592]{0:T(1024)(128)(4,1)}), s8[4194304]{0:T(1024)(128)(4,1)S(1)}, s32[]{:S(2)}) async-start(s8[4718592]{0:T(1024)(128)(4,1)} %bitcast.79), calls=%async_computation.6 | async-start | bytes 8388608
  40.5 7.1 %slice-start.3 = ((s8[4718592]{0:T(1024)(128)(4,1)}), s8[524288]{0:T(1024)(128)(4,1)S(1)}, s32[]{:S(2)}) async-start(s8[4718592]{0:T(1024)(128)(4,1)} %bitcast.79), calls=%async_computation.7 | async-start | bytes 1048576
  40.5 7.1 %copy-start.9 = (f32[512]{0:T(512)S(1)}, f32[512]{0:T(512)}, u32[]{:S(2)}) copy-start(f32[512]{0:T(512)} %param.8) | copy-start | bytes 6148
  40.5 6.6 %collective-permute-start.3 = (bf16[32,8,4608]{2,1,0:T(8,128)(2,1)S(1)}, bf16[32,8,4608]{2,1,0:T(8,128)(2,1)S(1)}, u32[]{:S(2)}, u32[]{:S(2)}) collective-permute-start(bf16[32,8,4608]{2,1,0:T(8,128)(2,1)S(1)} %pad_maximum_fusion.3), channel_id=1, source_target_pairs={{0,8},{8,0},{1,9},{9,1},{2,10},{10,2},{3,11},{11,3},{4,12},{12,4},... | collective-permute-start | bytes 7077896 | tf_op jit(solution)/shard_map/ppermute | solution.py:50
  43.0 10.0 %collective-permute-start.8 = (bf16[8,8,4608]{2,1,0:T(8,128)(2,1)S(1)}, bf16[8,8,4608]{2,1,0:T(8,128)(2,1)S(1)}, u32[]{:S(2)}, u32[]{:S(2)}) collective-permute-start(bf16[8,8,4608]{2,1,0:T(8,128)(2,1)S(1)} %collective-permute-done.2), channel_id=1, source_target_pairs={{23,0},{11,8},{21,2},{9,10},{19,4},{15,12},{17,6},{13,14},{22,1},{... | collective-permute-start | bytes 1769480 | tf_op jit(solution)/shard_map/ppermute | solution.py:29
  43.0 15.3 %collective-permute-start.6 = (bf16[8,8,4608]{2,1,0:T(8,128)(2,1)S(1)}, bf16[8,8,4608]{2,1,0:T(8,128)(2,1)S(1)}, u32[]{:S(2)}, u32[]{:S(2)}) collective-permute-start(bf16[8,8,4608]{2,1,0:T(8,128)(2,1)S(1)} %collective-permute-done.2), channel_id=1, source_target_pairs={{17,0},{9,8},{19,2},{11,10},{21,4},{13,12},{23,6},{15,14},{16,1},{... | collective-permute-start | bytes 1769480 | tf_op jit(solution)/shard_map/ppermute | solution.py:29
  43.5 15.1 %collective-permute-start.5 = (bf16[8,8,4608]{2,1,0:T(8,128)(2,1)S(1)}, bf16[8,8,4608]{2,1,0:T(8,128)(2,1)S(1)}, u32[]{:S(2)}, u32[]{:S(2)}) collective-permute-start(bf16[8,8,4608]{2,1,0:T(8,128)(2,1)S(1)} %collective-permute-done.1), channel_id=1, source_target_pairs={{6,0},{10,8},{4,2},{8,10},{2,4},{14,12},{0,6},{12,14},{7,1},{11,9}... | collective-permute-start | bytes 1769480 | tf_op jit(solution)/shard_map/ppermute | solution.py:29
  45.6 13.0 %collective-permute-start.7 = (bf16[8,8,4608]{2,1,0:T(8,128)(2,1)S(1)}, bf16[8,8,4608]{2,1,0:T(8,128)(2,1)S(1)}, u32[]{:S(2)}, u32[]{:S(2)}) collective-permute-start(bf16[8,8,4608]{2,1,0:T(8,128)(2,1)S(1)} %collective-permute-done), channel_id=1, source_target_pairs={{96,0},{40,8},{98,2},{42,10},{100,4},{44,12},{102,6},{46,14},{97,1... | collective-permute-start | bytes 1769480 | tf_op jit(solution)/shard_map/ppermute | solution.py:29
  47.1 15.6 %slice-start.4 = ((s8[4718592]{0:T(1024)(128)(4,1)}), s8[4194304]{0:T(1024)(128)(4,1)S(1)}, s32[]{:S(2)}) async-start(s8[4718592]{0:T(1024)(128)(4,1)} %bitcast.81), calls=%async_computation.8 | async-start | bytes 8388608
  47.6 2.6 %copy-start.8 = (f32[512]{0:T(512)S(1)}, f32[512]{0:T(512)}, u32[]{:S(2)}) copy-start(f32[512]{0:T(512)} %param.9) | copy-start | bytes 6148
  47.6 15.1 %slice-start.5 = ((s8[4718592]{0:T(1024)(128)(4,1)}), s8[524288]{0:T(1024)(128)(4,1)S(1)}, s32[]{:S(2)}) async-start(s8[4718592]{0:T(1024)(128)(4,1)} %bitcast.81), calls=%async_computation.9 | async-start | bytes 1048576
  59.0 7.9 %collective-permute-start.9 = (bf16[32,8,4608]{2,1,0:T(8,128)(2,1)S(1)}, bf16[32,8,4608]{2,1,0:T(8,128)(2,1)S(1)}, u32[]{:S(2)}, u32[]{:S(2)}) collective-permute-start(bf16[32,8,4608]{2,1,0:T(8,128)(2,1)S(1)} %pad_maximum_fusion.4), channel_id=1, source_target_pairs={{0,8},{8,0},{1,9},{9,1},{2,10},{10,2},{3,11},{11,3},{4,12},{12,4},... | collective-permute-start | bytes 7077896 | tf_op jit(solution)/shard_map/ppermute | solution.py:50
  64.1 5.2 %slice-start = ((s8[4718592]{0:T(1024)(128)(4,1)}), s8[4194304]{0:T(1024)(128)(4,1)S(1)}, s32[]{:S(2)}) async-start(s8[4718592]{0:T(1024)(128)(4,1)} %bitcast.68), calls=%async_computation.4 | async-start | bytes 8388608
  66.9 1.4 copy-start
  66.9 2.4 %slice-start.1 = ((s8[4718592]{0:T(1024)(128)(4,1)}), s8[524288]{0:T(1024)(128)(4,1)S(1)}, s32[]{:S(2)}) async-start(s8[4718592]{0:T(1024)(128)(4,1)} %bitcast.68), calls=%async_computation.5 | async-start | bytes 1048576
  70.7 5.0 %collective-permute-start.10 = (bf16[256,4608]{1,0:T(8,128)(2,1)S(1)}, bf16[256,4608]{1,0:T(8,128)(2,1)S(1)}, u32[]{:S(2)}, u32[]{:S(2)}) collective-permute-start(bf16[256,4608]{1,0:T(8,128)(2,1)S(1)} %convolution_convert_fusion.1), channel_id=1, source_target_pairs={{0,8},{8,0},{1,9},{9,1},{2,10},{10,2},{3,11},{11,3},{4,12},{12,4},... | collective-permute-start | bytes 7077896 | tf_op jit(solution)/shard_map/ppermute | solution.py:50
  72.5 6.1 %collective-permute-start.4 = (bf16[256,4608]{1,0:T(8,128)(2,1)S(1)}, bf16[256,4608]{1,0:T(8,128)(2,1)S(1)}, u32[]{:S(2)}, u32[]{:S(2)}) collective-permute-start(bf16[256,4608]{1,0:T(8,128)(2,1)S(1)} %convolution_convert_fusion.3), channel_id=1, source_target_pairs={{0,8},{8,0},{1,9},{9,1},{2,10},{10,2},{3,11},{11,3},{4,12},{12,4},... | collective-permute-start | bytes 7077896 | tf_op jit(solution)/shard_map/ppermute | solution.py:50
  76.3 9.1 %collective-permute-start.11 = (bf16[8,8,4608]{2,1,0:T(8,128)(2,1)S(1)}, bf16[8,8,4608]{2,1,0:T(8,128)(2,1)S(1)}, u32[]{:S(2)}, u32[]{:S(2)}) collective-permute-start(bf16[8,8,4608]{2,1,0:T(8,128)(2,1)S(1)} %get-tuple-element.61), channel_id=1, source_target_pairs={{96,0},{40,8},{98,2},{42,10},{100,4},{44,12},{102,6},{46,14},{97,1... | collective-permute-start | bytes 1769480 | tf_op jit(solution)/shard_map/ppermute | solution.py:29
  79.4 9.1 %collective-permute-start.13 = (bf16[8,8,4608]{2,1,0:T(8,128)(2,1)S(1)}, bf16[8,8,4608]{2,1,0:T(8,128)(2,1)S(1)}, u32[]{:S(2)}, u32[]{:S(2)}) collective-permute-start(bf16[8,8,4608]{2,1,0:T(8,128)(2,1)S(1)} %get-tuple-element.63), channel_id=1, source_target_pairs={{6,0},{10,8},{4,2},{8,10},{2,4},{14,12},{0,6},{12,14},{7,1},{11,9}... | collective-permute-start | bytes 1769480 | tf_op jit(solution)/shard_map/ppermute | solution.py:29
  79.5 15.4 %collective-permute-start.15 = (bf16[8,8,4608]{2,1,0:T(8,128)(2,1)S(1)}, bf16[8,8,4608]{2,1,0:T(8,128)(2,1)S(1)}, u32[]{:S(2)}, u32[]{:S(2)}) collective-permute-start(bf16[8,8,4608]{2,1,0:T(8,128)(2,1)S(1)} %get-tuple-element.65), channel_id=1, source_target_pairs={{17,0},{9,8},{19,2},{11,10},{21,4},{13,12},{23,6},{15,14},{16,1},{... | collective-permute-start | bytes 1769480 | tf_op jit(solution)/shard_map/ppermute | solution.py:29
  79.6 18.0 %collective-permute-start.17 = (bf16[8,8,4608]{2,1,0:T(8,128)(2,1)S(1)}, bf16[8,8,4608]{2,1,0:T(8,128)(2,1)S(1)}, u32[]{:S(2)}, u32[]{:S(2)}) collective-permute-start(bf16[8,8,4608]{2,1,0:T(8,128)(2,1)S(1)} %get-tuple-element.66), channel_id=1, source_target_pairs={{119,0},{43,8},{117,2},{41,10},{115,4},{47,12},{113,6},{45,14},{11... | collective-permute-start | bytes 1769480 | tf_op jit(solution)/shard_map/ppermute | solution.py:29
  85.5 15.7 %collective-permute-start.12 = (bf16[8,8,4608]{2,1,0:T(8,128)(2,1)S(1)}, bf16[8,8,4608]{2,1,0:T(8,128)(2,1)S(1)}, u32[]{:S(2)}, u32[]{:S(2)}) collective-permute-start(bf16[8,8,4608]{2,1,0:T(8,128)(2,1)S(1)} %add_convert_fusion.6), channel_id=1, source_target_pairs={{6,0},{10,8},{4,2},{8,10},{2,4},{14,12},{0,6},{12,14},{7,1},{11,9}... | collective-permute-start | bytes 1769480 | tf_op jit(solution)/shard_map/ppermute | solution.py:29
  88.7 12.6 %collective-permute-start.14 = (bf16[8,8,4608]{2,1,0:T(8,128)(2,1)S(1)}, bf16[8,8,4608]{2,1,0:T(8,128)(2,1)S(1)}, u32[]{:S(2)}, u32[]{:S(2)}) collective-permute-start(bf16[8,8,4608]{2,1,0:T(8,128)(2,1)S(1)} %add_convert_fusion.5), channel_id=1, source_target_pairs={{17,0},{9,8},{19,2},{11,10},{21,4},{13,12},{23,6},{15,14},{16,1},{... | collective-permute-start | bytes 1769480 | tf_op jit(solution)/shard_map/ppermute | solution.py:29
  89.8 7.5 %copy-start.1 = (bf16[32,8,4608]{2,1,0:T(8,128)(2,1)S(1)}, bf16[32,8,4608]{2,1,0:T(8,128)(2,1)}, u32[]{:S(2)}) copy-start(bf16[32,8,4608]{2,1,0:T(8,128)(2,1)} %copy-done) | copy-start | bytes 7077892
  95.9 9.2 %collective-permute-start.16 = (bf16[8,8,4608]{2,1,0:T(8,128)(2,1)}, bf16[8,8,4608]{2,1,0:T(8,128)(2,1)S(1)}, u32[]{:S(2)}, u32[]{:S(2)}) collective-permute-start(bf16[8,8,4608]{2,1,0:T(8,128)(2,1)} %add_convert_fusion.4), channel_id=1, source_target_pairs={{96,0},{40,8},{98,2},{42,10},{100,4},{44,12},{102,6},{46,14},{97,1... | collective-permute-start | bytes 1769480 | tf_op jit(solution)/shard_map/ppermute | solution.py:29
  105.1 14.6 %copy-start.4 = (f32[8,4608]{1,0:T(8,128)S(1)}, f32[8,4608]{1,0:T(8,128)}, u32[]{:S(2)}) copy-start(f32[8,4608]{1,0:T(8,128)} %copy-done.3) | copy-start | bytes 442372
  105.1 14.6 %copy-start.7 = (f32[4608]{0:T(1024)S(1)}, f32[4608]{0:T(1024)}, u32[]{:S(2)}) copy-start(f32[4608]{0:T(1024)} %param.11) | copy-start | bytes 55300
  133.4 9.1 %collective-permute-start.20 = (bf16[8,8,4608]{2,1,0:T(8,128)(2,1)S(1)}, bf16[8,8,4608]{2,1,0:T(8,128)(2,1)}, u32[]{:S(2)}, u32[]{:S(2)}) collective-permute-start(bf16[8,8,4608]{2,1,0:T(8,128)(2,1)S(1)} %all_to_all.31), channel_id=1, source_target_pairs={{96,0},{40,8},{98,2},{42,10},{100,4},{44,12},{102,6},{46,14},{97,1... | collective-permute-start | bytes 1769480 | tf_op jit(solution)/shard_map/ppermute | solution.py:29
  133.4 9.1 %collective-permute-start.19 = (bf16[8,8,4608]{2,1,0:T(8,128)(2,1)S(1)}, bf16[8,8,4608]{2,1,0:T(8,128)(2,1)}, u32[]{:S(2)}, u32[]{:S(2)}) collective-permute-start(bf16[8,8,4608]{2,1,0:T(8,128)(2,1)S(1)} %all_to_all.31), channel_id=1, source_target_pairs={{17,0},{9,8},{19,2},{11,10},{21,4},{13,12},{23,6},{15,14},{16,1},{... | collective-permute-start | bytes 1769480 | tf_op jit(solution)/shard_map/ppermute | solution.py:29
  133.4 9.1 %collective-permute-start.18 = (bf16[8,8,4608]{2,1,0:T(8,128)(2,1)S(1)}, bf16[8,8,4608]{2,1,0:T(8,128)(2,1)}, u32[]{:S(2)}, u32[]{:S(2)}) collective-permute-start(bf16[8,8,4608]{2,1,0:T(8,128)(2,1)S(1)} %all_to_all.31), channel_id=1, source_target_pairs={{6,0},{10,8},{4,2},{8,10},{2,4},{14,12},{0,6},{12,14},{7,1},{11,9}... | collective-permute-start | bytes 1769480 | tf_op jit(solution)/shard_map/ppermute | solution.py:29
  144.3 6.9 %collective-permute-start.21 = (bf16[32,8,4608]{2,1,0:T(8,128)(2,1)S(1)}, bf16[32,8,4608]{2,1,0:T(8,128)(2,1)S(1)}, u32[]{:S(2)}, u32[]{:S(2)}) collective-permute-start(bf16[32,8,4608]{2,1,0:T(8,128)(2,1)S(1)} %pad_maximum_fusion.5), channel_id=1, source_target_pairs={{0,8},{8,0},{1,9},{9,1},{2,10},{10,2},{3,11},{11,3},{4,12},{12,4},... | collective-permute-start | bytes 7077896 | tf_op jit(solution)/shard_map/ppermute | solution.py:50
  147.0 12.7 %collective-permute-start.25 = (bf16[8,8,4608]{2,1,0:T(8,128)(2,1)}, bf16[8,8,4608]{2,1,0:T(8,128)(2,1)}, u32[]{:S(2)}, u32[]{:S(2)}) collective-permute-start(bf16[8,8,4608]{2,1,0:T(8,128)(2,1)} %collective-permute-done.20), channel_id=1, source_target_pairs={{23,0},{11,8},{21,2},{9,10},{19,4},{15,12},{17,6},{13,14},{22,1},{... | collective-permute-start | bytes 1769480 | tf_op jit(solution)/shard_map/ppermute | solution.py:29
  147.9 15.7 %collective-permute-start.23 = (bf16[8,8,4608]{2,1,0:T(8,128)(2,1)}, bf16[8,8,4608]{2,1,0:T(8,128)(2,1)}, u32[]{:S(2)}, u32[]{:S(2)}) collective-permute-start(bf16[8,8,4608]{2,1,0:T(8,128)(2,1)} %collective-permute-done.20), channel_id=1, source_target_pairs={{17,0},{9,8},{19,2},{11,10},{21,4},{13,12},{23,6},{15,14},{16,1},{... | collective-permute-start | bytes 1769480 | tf_op jit(solution)/shard_map/ppermute | solution.py:29
  148.8 14.8 %collective-permute-start.22 = (bf16[8,8,4608]{2,1,0:T(8,128)(2,1)}, bf16[8,8,4608]{2,1,0:T(8,128)(2,1)}, u32[]{:S(2)}, u32[]{:S(2)}) collective-permute-start(bf16[8,8,4608]{2,1,0:T(8,128)(2,1)} %collective-permute-done.19), channel_id=1, source_target_pairs={{6,0},{10,8},{4,2},{8,10},{2,4},{14,12},{0,6},{12,14},{7,1},{11,9}... | collective-permute-start | bytes 1769480 | tf_op jit(solution)/shard_map/ppermute | solution.py:29
  149.7 13.9 %collective-permute-start.24 = (bf16[8,8,4608]{2,1,0:T(8,128)(2,1)}, bf16[8,8,4608]{2,1,0:T(8,128)(2,1)}, u32[]{:S(2)}, u32[]{:S(2)}) collective-permute-start(bf16[8,8,4608]{2,1,0:T(8,128)(2,1)} %collective-permute-done.18), channel_id=1, source_target_pairs={{96,0},{40,8},{98,2},{42,10},{100,4},{44,12},{102,6},{46,14},{97,1... | collective-permute-start | bytes 1769480 | tf_op jit(solution)/shard_map/ppermute | solution.py:29
  165.5 7.1 %copy-start.5 = (f32[256,512]{1,0:T(8,128)S(1)}, f32[256,512]{1,0:T(8,128)}, u32[]{:S(2)}) copy-start(f32[256,512]{1,0:T(8,128)} %get-tuple-element.92) | copy-start | bytes 1572868
  165.5 8.5 %collective-permute-start.26 = (bf16[32,8,4608]{2,1,0:T(8,128)(2,1)S(1)}, bf16[32,8,4608]{2,1,0:T(8,128)(2,1)S(1)}, u32[]{:S(2)}, u32[]{:S(2)}) collective-permute-start(bf16[32,8,4608]{2,1,0:T(8,128)(2,1)S(1)} %pad_maximum_fusion.6), channel_id=1, source_target_pairs={{0,8},{8,0},{1,9},{9,1},{2,10},{10,2},{3,11},{11,3},{4,12},{12,4},... | collective-permute-start | bytes 7077896 | tf_op jit(solution)/shard_map/ppermute | solution.py:50
  172.6 1.4 copy-start.6
  175.4 1.0 copy-start.2
  175.8 5.1 %slice-start.6 = ((s8[4718592]{0:T(1024)(128)(4,1)}), s8[4194304]{0:T(1024)(128)(4,1)S(1)}, s32[]{:S(2)}) async-start(s8[4718592]{0:T(1024)(128)(4,1)} %bitcast.83), calls=%async_computation.10 | async-start | bytes 8388608
  176.5 4.3 %slice-start.7 = ((s8[4718592]{0:T(1024)(128)(4,1)}), s8[524288]{0:T(1024)(128)(4,1)S(1)}, s32[]{:S(2)}) async-start(s8[4718592]{0:T(1024)(128)(4,1)} %bitcast.83), calls=%async_computation.11 | async-start | bytes 1048576

commit v5 on v4

--- a/solution.py
+++ b/solution.py
@@ -100,25 +100,26 @@
         gating = jax.nn.sigmoid((pre_act - thresholds) / band_width)
         code_values = pre_act * gating
         slopes = gating + pre_act * gating * (1.0 - gating) / band_width
-        return barrier(code_values.astype(bf16), slopes, jnp.sum(code_values, axis=0))
+        return barrier(code_values.astype(bf16), slopes.astype(bf16), jnp.sum(code_values, axis=0))
 
     near, encoded, mine, theirs = gather(own_centered, encode)
     code_near, slopes_near, totals_near = encoded
-    code_mine, slopes_mine, totals_mine = encode(mine)
-    theirs, _ = barrier(theirs, code_mine)
-    code_theirs, slopes_theirs, totals_theirs = encode(theirs)
-    totals = totals_near + totals_mine + totals_theirs
+    def decode(code_rows):
+        return barrier(jnp.dot(code_rows, dec_weight, preferred_element_type=f32).astype(bf16))[0]
 
-    def decode(mine, theirs):
-        theirs, mine = (
-            barrier(jnp.dot(rows, dec_weight, preferred_element_type=f32).astype(bf16))[0]
-            for rows in (theirs, mine)
-        )
+    def sums(mine, theirs):
         pairs = zip(*(jnp.split(rows.reshape(32, 8, -1), 4) for rows in (mine, swap(theirs))))
         return barrier(*(add(*pair).astype(bf16) for pair in pairs))
 
-    recon_near = decode(code_near[:256], code_near[256:])
-    recon_distant = decode(code_mine, code_theirs)
+    recon_theirs = decode(code_near[256:])
+    code_mine, slopes_mine, totals_mine = encode(mine)
+    theirs, _, _ = barrier(theirs, code_mine, recon_theirs)
+    code_theirs, slopes_theirs, totals_theirs = encode(theirs)
+    totals = totals_near + totals_mine + totals_theirs
+    recon_distant = sums(decode(code_mine), decode(code_theirs))
+    recon_mine = decode(code_near[:256])
+    recon_theirs, _ = barrier(recon_theirs, recon_distant)
+    recon_near = sums(recon_mine, recon_theirs)
 
     def side_work(received):
         *rest, dec, _ = barrier(

time: 186 us -> 189 us (1.016)
  matrix products: 33.7 us -> 37.8 us
  waiting for transfers between devices: 52.8 us -> 50.5 us
  starting transfers between devices: 24.6 us -> 26.5 us
    dot_general x3, matrix products: 5.38 us -> 9.66 us  [encode(): jnp.dot(rows, enc_weight, preferred_element_type=f32) + enc_bias]
    ppermute x21, waiting for transfers between devices: 47.5 us -> 45.4 us  [receive(): return lax.ppermute(block, MESH, pairs)]
  transfers between devices with their start and end apart: 27 -> 27, of which waited for: 15 -> 13; matrix products, arithmetic and copies ran while one was open for 16% -> 16% of each run, Pallas kernels for 0% -> 0%
where the time goes in v5:
time: 189 us; the launch traced here: 188 us
  blocking collectives  57.3 us (30%)
  waiting for transfers between devices  50.5 us (27%)
  matrix products  37.8 us (20%)
  starting transfers between devices  26.5 us (14%)
  other arithmetic  14.5 us (8%)
    all_to_all x3, blocking collectives, trade(): return lax.all_to_all(blocks, MESH, 0, 0, axis_index_groups=cubes(pairing))  46.3 us
    ppermute x21, waiting for transfers between devices, receive(): return lax.ppermute(block, MESH, pairs)  45.4 us
    ppermute x6, starting transfers between devices, swap(): return lax.ppermute(block, 'core', [(0, 1), (1, 0)])  15.3 us
    ppermute x21, starting transfers between devices, receive(): return lax.ppermute(block, MESH, pairs)  11.2 us
    all_to_all x1, blocking collectives, on_device(): lax.all_to_all(activations, ('x', 'yl'), split_axis=0, concat_axis=1, til...  11 us
    dot_general x3, matrix products, encode(): jnp.dot(rows, enc_weight, preferred_element_type=f32) + enc_bias  9.66 us
    dot_general x3, matrix products, preact_grad(): lax.dot_general(delta, dec_weight, (((1,), (1,)), ((), ())), preferred_el...  6.49 us
    dot_general x4, matrix products, decode(): jnp.dot(code_rows, dec_weight, preferred_element_type=f32).astype(bf16)  5.54 us
  transfers between devices with their start and end apart: 27, of which 13 were waited for; matrix products, arithmetic and copies ran while one was open for 16% of the time, Pallas kernels for 0%

profile of v5, /device:TPU:1, one launch (start us, length us, event | category | flops | bytes accessed | tf_op | source)
XLA Modules:
  0.0 188.2 jit_solution(13246080621457862878)
XLA Ops:
  0.6 11.0 %all_to_all.28 = bf16[8,8,576]{2,1,0:T(8,128)(2,1)S(1)} all-to-all(bf16[8,8,576]{2,1,0:T(8,128)(2,1)} %bitcast.78), channel_id=1, replica_groups=mesh['z'=4,'yh'=2,'core'=2,'x'=4,'yl'=2] {'x','yl'}, dimensions={0} | all-to-all | bytes 147456 | tf_op jit(solution)/shard_map/all_to_all | solution.py:94
  11.8 0.8 subtract_convert_fusion
  12.6 18.5 %all_to_all.29 = bf16[8,8,4608]{2,1,0:T(8,128)(2,1)S(1)} all-to-all(bf16[8,8,4608]{2,1,0:T(8,128)(2,1)S(1)} %broadcast_in_dim.4), channel_id=1, replica_groups={{0,2,1,3,32,34,33,35},{4,6,5,7,36,38,37,39},{16,18,17,19,48,50,49,51},{..., dimensions={0} | all-to-all | bytes 1179648 | tf_op jit(solution)/shard_map/all_to_all | solution.py:46
  31.1 9.0 %collective-permute-done.2 = bf16[8,8,4608]{2,1,0:T(8,128)(2,1)S(1)} collective-permute-done((bf16[8,8,4608]{2,1,0:T(8,128)(2,1)S(1)}, bf16[8,8,4608]{2,1,0:T(8,128)(2,1)S(1)}, u32[]{:S(2)}, u32[]{:S(2)}) %collective-permute-start.2) | collective-permute-done | bytes 589856 | tf_op jit(solution)/shard_map/ppermute | solution.py:29
  40.5 2.5 %collective-permute-start.3 = (bf16[32,8,4608]{2,1,0:T(8,128)(2,1)S(1)}, bf16[32,8,4608]{2,1,0:T(8,128)(2,1)S(1)}, u32[]{:S(2)}, u32[]{:S(2)}) collective-permute-start(bf16[32,8,4608]{2,1,0:T(8,128)(2,1)S(1)} %pad_maximum_fusion.3), channel_id=1, source_target_pairs={{0,8},{8,0},{1,9},{9,1},{2,10},{10,2},{3,11},{11,3},{4,12},{12,4},... | collective-permute-start | bytes 7077896 | tf_op jit(solution)/shard_map/ppermute | solution.py:50
  43.0 0.6 collective-permute-start.5
  43.5 2.1 %collective-permute-start.4 = (bf16[8,8,4608]{2,1,0:T(8,128)(2,1)S(1)}, bf16[8,8,4608]{2,1,0:T(8,128)(2,1)S(1)}, u32[]{:S(2)}, u32[]{:S(2)}) collective-permute-start(bf16[8,8,4608]{2,1,0:T(8,128)(2,1)S(1)} %collective-permute-done.1), channel_id=1, source_target_pairs={{6,0},{10,8},{4,2},{8,10},{2,4},{14,12},{0,6},{12,14},{7,1},{11,9}... | collective-permute-start | bytes 1769480 | tf_op jit(solution)/shard_map/ppermute | solution.py:29
  46.1 1.0 collective-permute-done.3
  47.5 4.6 %convolution_add_fusion = f32[512,512]{1,0:T(8,128)S(1)} fusion(bf16[4608,512]{1,0:T(8,128)(2,1)} %param.7, f32[512]{0:T(512)S(1)} %copy-done.10, bf16[64,8,4608]{2,1,0:T(8,128)(2,1)S(1)} %pad_maximum_fusion), kind=kOutput, calls=%fused_computation.22 | convolution fusion | flops 2416181248 | bytes 10487808 | tf_op jit(solution)/shard_map/dot_general | solution.py:99
  52.1 1.3 fusion.37
  53.4 4.9 %collective-permute-done.5 = bf16[8,8,4608]{2,1,0:T(8,128)(2,1)S(1)} collective-permute-done((bf16[8,8,4608]{2,1,0:T(8,128)(2,1)S(1)}, bf16[8,8,4608]{2,1,0:T(8,128)(2,1)S(1)}, u32[]{:S(2)}, u32[]{:S(2)}) %collective-permute-start.5) | collective-permute-done | bytes 589856 | tf_op jit(solution)/shard_map/ppermute | solution.py:29
  59.0 3.7 %collective-permute-start.8 = (bf16[32,8,4608]{2,1,0:T(8,128)(2,1)S(1)}, bf16[32,8,4608]{2,1,0:T(8,128)(2,1)S(1)}, u32[]{:S(2)}, u32[]{:S(2)}) collective-permute-start(bf16[32,8,4608]{2,1,0:T(8,128)(2,1)S(1)} %pad_maximum_fusion.4), channel_id=1, source_target_pairs={{0,8},{8,0},{1,9},{9,1},{2,10},{10,2},{3,11},{11,3},{4,12},{12,4},... | collective-permute-start | bytes 7077896 | tf_op jit(solution)/shard_map/ppermute | solution.py:50
  62.7 3.7 %convolution_add_fusion.4 = f32[256,512]{1,0:T(8,128)S(1)} fusion(bf16[4608,512]{1,0:T(8,128)(2,1)} %param.7, f32[512]{0:T(512)S(1)} %copy-done.10, bf16[32,8,4608]{2,1,0:T(8,128)(2,1)S(1)} %pad_maximum_fusion.4), kind=kOutput, calls=%fused_computation.29 | convolution fusion | flops 1208090624 | bytes 7604224 | tf_op jit(solution)/shard_map/dot_general | solution.py:99
  66.4 0.9 fusion.35
  67.4 1.4 convolution_convert_fusion.3
  69.0 1.4 convolution_add_fusion.3
  70.4 0.9 fusion.33
  71.4 1.4 convolution_convert_fusion.1
  73.1 1.4 convolution_convert_fusion.2
  74.4 2.9 %collective-permute-done.9 = bf16[256,4608]{1,0:T(8,128)(2,1)S(1)} collective-permute-done((bf16[256,4608]{1,0:T(8,128)(2,1)S(1)}, bf16[256,4608]{1,0:T(8,128)(2,1)S(1)}, u32[]{:S(2)}, u32[]{:S(2)}) %collective-permute-start.9) | collective-permute-done | bytes 2359328 | tf_op jit(solution)/shard_map/ppermute | solution.py:50
  77.4 1.4 fusion.20
  79.0 0.6 collective-permute-start.11
  79.5 1.4 convolution_convert_fusion.4
  81.1 3.1 %collective-permute-start.17 = (bf16[8,8,4608]{2,1,0:T(8,128)(2,1)}, bf16[8,8,4608]{2,1,0:T(8,128)(2,1)}, u32[]{:S(2)}, u32[]{:S(2)}) collective-permute-start(bf16[8,8,4608]{2,1,0:T(8,128)(2,1)} %get-tuple-element.64), channel_id=1, source_target_pairs={{119,0},{43,8},{117,2},{41,10},{115,4},{47,12},{113,6},{45,14},{11... | collective-permute-start | bytes 1769480 | tf_op jit(solution)/shard_map/ppermute | solution.py:29
  84.3 3.7 %collective-permute-done.11 = bf16[8,8,4608]{2,1,0:T(8,128)(2,1)S(1)} collective-permute-done((bf16[8,8,4608]{2,1,0:T(8,128)(2,1)S(1)}, bf16[8,8,4608]{2,1,0:T(8,128)(2,1)S(1)}, u32[]{:S(2)}, u32[]{:S(2)}) %collective-permute-start.11) | collective-permute-done | bytes 589856 | tf_op jit(solution)/shard_map/ppermute | solution.py:29
  88.0 1.0 multiply_reduce_fusion
  90.5 6.0 %collective-permute-done.15 = bf16[8,8,4608]{2,1,0:T(8,128)(2,1)S(1)} collective-permute-done((bf16[8,8,4608]{2,1,0:T(8,128)(2,1)S(1)}, bf16[8,8,4608]{2,1,0:T(8,128)(2,1)S(1)}, u32[]{:S(2)}, u32[]{:S(2)}) %collective-permute-start.15) | collective-permute-done | bytes 589856 | tf_op jit(solution)/shard_map/ppermute | solution.py:29
  96.7 1.0 collective-permute-start.16
  98.0 4.8 %collective-permute-done.14 = bf16[8,8,4608]{2,1,0:T(8,128)(2,1)S(1)} collective-permute-done((bf16[8,8,4608]{2,1,0:T(8,128)(2,1)S(1)}, bf16[8,8,4608]{2,1,0:T(8,128)(2,1)S(1)}, u32[]{:S(2)}, u32[]{:S(2)}) %collective-permute-start.14) | collective-permute-done | bytes 589856 | tf_op jit(solution)/shard_map/ppermute | solution.py:29
  102.8 3.0 %collective-permute-done.16 = bf16[8,8,4608]{2,1,0:T(8,128)(2,1)S(1)} collective-permute-done((bf16[8,8,4608]{2,1,0:T(8,128)(2,1)S(1)}, bf16[8,8,4608]{2,1,0:T(8,128)(2,1)S(1)}, u32[]{:S(2)}, u32[]{:S(2)}) %collective-permute-start.16) | collective-permute-done | bytes 589856 | tf_op jit(solution)/shard_map/ppermute | solution.py:29
  105.8 1.5 add_convert_fusion.3
  107.3 14.2 %all_to_all.30 = bf16[8,8,4608]{2,1,0:T(8,128)(2,1)S(1)} all-to-all(bf16[8,8,4608]{2,1,0:T(8,128)(2,1)S(1)} %add_convert_fusion.3), channel_id=1, replica_groups={{0,2,1,3,32,34,33,35},{4,6,5,7,36,38,37,39},{16,18,17,19,48,50,49,51},{..., dimensions={0} | all-to-all | bytes 1179648 | tf_op jit(solution)/shard_map/all_to_all | solution.py:46
  121.6 13.6 %all_to_all.31 = bf16[8,8,4608]{2,1,0:T(8,128)(2,1)S(1)} all-to-all(bf16[8,8,4608]{2,1,0:T(8,128)(2,1)S(1)} %broadcast_in_dim.5), channel_id=1, replica_groups={{0,2,1,3,32,34,33,35},{4,6,5,7,36,38,37,39},{16,18,17,19,48,50,49,51},{..., dimensions={0} | all-to-all | bytes 1179648 | tf_op jit(solution)/shard_map/all_to_all | solution.py:46
  135.2 9.1 %collective-permute-done.20 = bf16[8,8,4608]{2,1,0:T(8,128)(2,1)} collective-permute-done((bf16[8,8,4608]{2,1,0:T(8,128)(2,1)S(1)}, bf16[8,8,4608]{2,1,0:T(8,128)(2,1)}, u32[]{:S(2)}, u32[]{:S(2)}) %collective-permute-start.20) | collective-permute-done | bytes 589856 | tf_op jit(solution)/shard_map/ppermute | solution.py:29
  144.4 1.7 pad_maximum_fusion.5
  146.1 4.9 %collective-permute-start.21 = (bf16[32,8,4608]{2,1,0:T(8,128)(2,1)S(1)}, bf16[32,8,4608]{2,1,0:T(8,128)(2,1)S(1)}, u32[]{:S(2)}, u32[]{:S(2)}) collective-permute-start(bf16[32,8,4608]{2,1,0:T(8,128)(2,1)S(1)} %pad_maximum_fusion.5), channel_id=1, source_target_pairs={{0,8},{8,0},{1,9},{9,1},{2,10},{10,2},{3,11},{11,3},{4,12},{12,4},... | collective-permute-start | bytes 7077896 | tf_op jit(solution)/shard_map/ppermute | solution.py:50
  151.0 1.7 collective-permute-start.25
  154.0 1.1 collective-permute-done.21
  155.5 3.7 %fusion.9 = bf16[512,512]{1,0:T(8,128)(2,1)S(1)} fusion(bf16[512,4608]{1,0:T(8,128)(2,1)S(1)} %bitcast.69, bf16[64,8,4608]{2,1,0:T(8,128)(2,1)S(1)} %pad_maximum_fusion.1, bf16[512,512]{1,0:T(8,128)(2,1)} %get-tuple-element.52, f32[512]{0:T(512)S(1)} %get-tuple-element.88), kind=kOutput, calls=%fused_computation.23 | convolution fusion | flops 2416967680 | bytes 10487808 | tf_op jit(solution)/shard_map/dot_general | solution.py:148
  159.2 4.3 %convolution_convert_fusion = bf16[4608,512]{1,0:T(8,128)(2,1)} fusion(bf16[4608,512]{0,1:T(8,128)(2,1)S(1)} %bitcast.72, bf16[512,512]{1,0:T(8,128)(2,1)S(1)} %fusion.9), kind=kOutput, calls=%fused_computation.4 | convolution fusion | flops 2418278400 | bytes 9961472 | tf_op jit(solution)/shard_map/dot_general | solution.py:157
  163.5 4.0 %collective-permute-done.23 = bf16[8,8,4608]{2,1,0:T(8,128)(2,1)} collective-permute-done((bf16[8,8,4608]{2,1,0:T(8,128)(2,1)}, bf16[8,8,4608]{2,1,0:T(8,128)(2,1)}, u32[]{:S(2)}, u32[]{:S(2)}) %collective-permute-start.23) | collective-permute-done | bytes 589856 | tf_op jit(solution)/shard_map/ppermute | solution.py:29
  167.5 1.9 %pad_maximum_fusion.6 = bf16[32,8,4608]{2,1,0:T(8,128)(2,1)S(1)} fusion(bf16[8,8,4608]{2,1,0:T(8,128)(2,1)} %collective-permute-done.25, bf16[8,8,4608]{2,1,0:T(8,128)(2,1)} %collective-permute-done.24, bf16[8,8,4608]{2,1,0:T(8,128)(2,1)} %collective-permute-done.23, bf16[8,8,4608]{2,1,0:T(8,128)(2,1)} %collective-permute-done.22), kind=kLoop, calls=%fused_computation.19 | loop fusion | flops 3538944 | bytes 4718592 | tf_op jit(solution)/shard_map/concatenate | solution.py:76
  169.4 3.7 %collective-permute-start.26 = (bf16[32,8,4608]{2,1,0:T(8,128)(2,1)S(1)}, bf16[32,8,4608]{2,1,0:T(8,128)(2,1)S(1)}, u32[]{:S(2)}, u32[]{:S(2)}) collective-permute-start(bf16[32,8,4608]{2,1,0:T(8,128)(2,1)S(1)} %pad_maximum_fusion.6), channel_id=1, source_target_pairs={{0,8},{8,0},{1,9},{9,1},{2,10},{10,2},{3,11},{11,3},{4,12},{12,4},... | collective-permute-start | bytes 7077896 | tf_op jit(solution)/shard_map/ppermute | solution.py:50
  173.1 3.1 %add_convert_fusion.2 = bf16[512,4608]{1,0:T(8,128)(2,1)S(1)} fusion(bf16[512,4608]{1,0:T(8,128)(2,1)S(1)} %bitcast.69, bf16[512,512]{0,1:T(8,128)(2,1)S(1)} %bitcast.77, bf16[64,8,4608]{2,1,0:T(8,128)(2,1)S(1)} %pad_maximum_fusion.1, f32[512]{0:T(512)S(1)} %get-tuple-element.96), kind=kOutput, calls=%fused_computation.2 | convolution fusion | flops 2425356288 | bytes 14682112 | tf_op jit(solution)/shard_map/dot_general | solution.py:160
  176.2 1.4 fusion.14
  177.7 1.4 fusion.15
  179.5 4.4 %add_convert_fusion = bf16[512,4608]{1,0:T(8,128)(2,1)} fusion(bf16[512,4608]{1,0:T(8,128)(2,1)S(1)} %add_convert_fusion.2, bf16[512,512]{0,1:T(8,128)(2,1)S(1)} %maximum_bitcast_fusion.1, bf16[512,4608]{1,0:T(8,128)(2,1)S(1)} %pad_maximum_fusion.2), kind=kOutput, calls=%fused_computation | convolution fusion | flops 2422996992 | bytes 14680064 | tf_op jit(solution)/shard_map/dot_general | solution.py:168
  183.8 4.4 %add_convert_fusion.1 = bf16[4608,512]{1,0:T(8,128)(2,1)} fusion(bf16[4608,512]{1,0:T(8,128)(2,1)S(1)} %bitcast.82, bf16[4608,512]{0,1:T(8,128)(2,1)S(1)} %maximum_bitcast_fusion, bf16[512,512]{1,0:T(8,128)(2,1)S(1)} %pad_maximum_fusion.7), kind=kOutput, calls=%fused_computation.1 | convolution fusion | flops 2422996992 | bytes 14680064 | tf_op jit(solution)/shard_map/dot_general | solution.py:167
  (90 shorter events, 7.1 us)
Async XLA Ops:
  11.8 28.7 %copy-start.4 = (f32[8,4608]{1,0:T(8,128)}, f32[8,4608]{1,0:T(8,128)S(1)}, u32[]{:S(2)}) copy-start(f32[8,4608]{1,0:T(8,128)S(1)} %reshape.90) | copy-start | bytes 442372
  31.1 9.0 %collective-permute-start.2 = (bf16[8,8,4608]{2,1,0:T(8,128)(2,1)S(1)}, bf16[8,8,4608]{2,1,0:T(8,128)(2,1)S(1)}, u32[]{:S(2)}, u32[]{:S(2)}) collective-permute-start(bf16[8,8,4608]{2,1,0:T(8,128)(2,1)S(1)} %all_to_all.29), channel_id=1, source_target_pairs={{96,0},{40,8},{98,2},{42,10},{100,4},{44,12},{102,6},{46,14},{97,1... | collective-permute-start | bytes 1769480 | tf_op jit(solution)/shard_map/ppermute | solution.py:29
  31.1 9.0 %collective-permute-start.1 = (bf16[8,8,4608]{2,1,0:T(8,128)(2,1)S(1)}, bf16[8,8,4608]{2,1,0:T(8,128)(2,1)S(1)}, u32[]{:S(2)}, u32[]{:S(2)}) collective-permute-start(bf16[8,8,4608]{2,1,0:T(8,128)(2,1)S(1)} %all_to_all.29), channel_id=1, source_target_pairs={{17,0},{9,8},{19,2},{11,10},{21,4},{13,12},{23,6},{15,14},{16,1},{... | collective-permute-start | bytes 1769480 | tf_op jit(solution)/shard_map/ppermute | solution.py:29
  31.1 9.0 %collective-permute-start = (bf16[8,8,4608]{2,1,0:T(8,128)(2,1)S(1)}, bf16[8,8,4608]{2,1,0:T(8,128)(2,1)S(1)}, u32[]{:S(2)}, u32[]{:S(2)}) collective-permute-start(bf16[8,8,4608]{2,1,0:T(8,128)(2,1)S(1)} %all_to_all.29), channel_id=1, source_target_pairs={{6,0},{10,8},{4,2},{8,10},{2,4},{14,12},{0,6},{12,14},{7,1},{11,9}... | collective-permute-start | bytes 1769480 | tf_op jit(solution)/shard_map/ppermute | solution.py:29
  40.5 7.0 %copy-start.10 = (f32[512]{0:T(512)S(1)}, f32[512]{0:T(512)}, u32[]{:S(2)}) copy-start(f32[512]{0:T(512)} %param.8) | copy-start | bytes 6148
  40.5 6.6 %collective-permute-start.3 = (bf16[32,8,4608]{2,1,0:T(8,128)(2,1)S(1)}, bf16[32,8,4608]{2,1,0:T(8,128)(2,1)S(1)}, u32[]{:S(2)}, u32[]{:S(2)}) collective-permute-start(bf16[32,8,4608]{2,1,0:T(8,128)(2,1)S(1)} %pad_maximum_fusion.3), channel_id=1, source_target_pairs={{0,8},{8,0},{1,9},{9,1},{2,10},{10,2},{3,11},{11,3},{4,12},{12,4},... | collective-permute-start | bytes 7077896 | tf_op jit(solution)/shard_map/ppermute | solution.py:50
  42.9 10.5 %collective-permute-start.7 = (bf16[8,8,4608]{2,1,0:T(8,128)(2,1)S(1)}, bf16[8,8,4608]{2,1,0:T(8,128)(2,1)S(1)}, u32[]{:S(2)}, u32[]{:S(2)}) collective-permute-start(bf16[8,8,4608]{2,1,0:T(8,128)(2,1)S(1)} %collective-permute-done.2), channel_id=1, source_target_pairs={{23,0},{11,8},{21,2},{9,10},{19,4},{15,12},{17,6},{13,14},{22,1},{... | collective-permute-start | bytes 1769480 | tf_op jit(solution)/shard_map/ppermute | solution.py:29
  43.0 15.3 %collective-permute-start.5 = (bf16[8,8,4608]{2,1,0:T(8,128)(2,1)S(1)}, bf16[8,8,4608]{2,1,0:T(8,128)(2,1)S(1)}, u32[]{:S(2)}, u32[]{:S(2)}) collective-permute-start(bf16[8,8,4608]{2,1,0:T(8,128)(2,1)S(1)} %collective-permute-done.2), channel_id=1, source_target_pairs={{17,0},{9,8},{19,2},{11,10},{21,4},{13,12},{23,6},{15,14},{16,1},{... | collective-permute-start | bytes 1769480 | tf_op jit(solution)/shard_map/ppermute | solution.py:29
  43.5 15.1 %collective-permute-start.4 = (bf16[8,8,4608]{2,1,0:T(8,128)(2,1)S(1)}, bf16[8,8,4608]{2,1,0:T(8,128)(2,1)S(1)}, u32[]{:S(2)}, u32[]{:S(2)}) collective-permute-start(bf16[8,8,4608]{2,1,0:T(8,128)(2,1)S(1)} %collective-permute-done.1), channel_id=1, source_target_pairs={{6,0},{10,8},{4,2},{8,10},{2,4},{14,12},{0,6},{12,14},{7,1},{11,9}... | collective-permute-start | bytes 1769480 | tf_op jit(solution)/shard_map/ppermute | solution.py:29
  45.6 13.0 %collective-permute-start.6 = (bf16[8,8,4608]{2,1,0:T(8,128)(2,1)S(1)}, bf16[8,8,4608]{2,1,0:T(8,128)(2,1)S(1)}, u32[]{:S(2)}, u32[]{:S(2)}) collective-permute-start(bf16[8,8,4608]{2,1,0:T(8,128)(2,1)S(1)} %collective-permute-done), channel_id=1, source_target_pairs={{96,0},{40,8},{98,2},{42,10},{100,4},{44,12},{102,6},{46,14},{97,1... | collective-permute-start | bytes 1769480 | tf_op jit(solution)/shard_map/ppermute | solution.py:29
  47.5 4.6 %copy-start.9 = (f32[512]{0:T(512)S(1)}, f32[512]{0:T(512)}, u32[]{:S(2)}) copy-start(f32[512]{0:T(512)} %param.9) | copy-start | bytes 6148
  53.4 26.1 %copy-start.2 = (bf16[512,512]{1,0:T(8,128)(2,1)}, bf16[512,512]{1,0:T(8,128)(2,1)S(1)}, u32[]{:S(2)}) copy-start(bf16[512,512]{1,0:T(8,128)(2,1)S(1)} %get-tuple-element.72) | copy-start | bytes 1572868
  58.6 8.7 %slice-start = ((s8[4718592]{0:T(1024)(128)(4,1)}), s8[4194304]{0:T(1024)(128)(4,1)S(1)}, s32[]{:S(2)}) async-start(s8[4718592]{0:T(1024)(128)(4,1)} %bitcast.68), calls=%async_computation.4 | async-start | bytes 8388608
  58.9 8.4 %slice-start.1 = ((s8[4718592]{0:T(1024)(128)(4,1)}), s8[524288]{0:T(1024)(128)(4,1)S(1)}, s32[]{:S(2)}) async-start(s8[4718592]{0:T(1024)(128)(4,1)} %bitcast.68), calls=%async_computation.5 | async-start | bytes 1048576
  59.0 9.8 %collective-permute-start.8 = (bf16[32,8,4608]{2,1,0:T(8,128)(2,1)S(1)}, bf16[32,8,4608]{2,1,0:T(8,128)(2,1)S(1)}, u32[]{:S(2)}, u32[]{:S(2)}) collective-permute-start(bf16[32,8,4608]{2,1,0:T(8,128)(2,1)S(1)} %pad_maximum_fusion.4), channel_id=1, source_target_pairs={{0,8},{8,0},{1,9},{9,1},{2,10},{10,2},{3,11},{11,3},{4,12},{12,4},... | collective-permute-start | bytes 7077896 | tf_op jit(solution)/shard_map/ppermute | solution.py:50
  66.4 2.4 %slice-start.2 = ((s8[4718592]{0:T(1024)(128)(4,1)}), s8[4194304]{0:T(1024)(128)(4,1)S(1)}, s32[]{:S(2)}) async-start(s8[4718592]{0:T(1024)(128)(4,1)} %bitcast.79), calls=%async_computation.6 | async-start | bytes 8388608
  67.4 1.7 slice-start.3
  68.8 1.6 copy-start
  72.8 4.6 %collective-permute-start.9 = (bf16[256,4608]{1,0:T(8,128)(2,1)S(1)}, bf16[256,4608]{1,0:T(8,128)(2,1)S(1)}, u32[]{:S(2)}, u32[]{:S(2)}) collective-permute-start(bf16[256,4608]{1,0:T(8,128)(2,1)S(1)} %convolution_convert_fusion.1), channel_id=1, source_target_pairs={{0,8},{8,0},{1,9},{9,1},{2,10},{10,2},{3,11},{11,3},{4,12},{12,4},... | collective-permute-start | bytes 7077896 | tf_op jit(solution)/shard_map/ppermute | solution.py:50
  78.7 10.3 %collective-permute-start.10 = (bf16[256,4608]{1,0:T(8,128)(2,1)S(1)}, bf16[256,4608]{1,0:T(8,128)(2,1)S(1)}, u32[]{:S(2)}, u32[]{:S(2)}) collective-permute-start(bf16[256,4608]{1,0:T(8,128)(2,1)S(1)} %convolution_convert_fusion.3), channel_id=1, source_target_pairs={{0,8},{8,0},{1,9},{9,1},{2,10},{10,2},{3,11},{11,3},{4,12},{12,4},... | collective-permute-start | bytes 7077896 | tf_op jit(solution)/shard_map/ppermute | solution.py:50
  79.0 9.0 %collective-permute-start.11 = (bf16[8,8,4608]{2,1,0:T(8,128)(2,1)S(1)}, bf16[8,8,4608]{2,1,0:T(8,128)(2,1)S(1)}, u32[]{:S(2)}, u32[]{:S(2)}) collective-permute-start(bf16[8,8,4608]{2,1,0:T(8,128)(2,1)S(1)} %get-tuple-element.63), channel_id=1, source_target_pairs={{96,0},{40,8},{98,2},{42,10},{100,4},{44,12},{102,6},{46,14},{97,1... | collective-permute-start | bytes 1769480 | tf_op jit(solution)/shard_map/ppermute | solution.py:29
  80.9 9.1 %collective-permute-start.13 = (bf16[8,8,4608]{2,1,0:T(8,128)(2,1)S(1)}, bf16[8,8,4608]{2,1,0:T(8,128)(2,1)S(1)}, u32[]{:S(2)}, u32[]{:S(2)}) collective-permute-start(bf16[8,8,4608]{2,1,0:T(8,128)(2,1)S(1)} %get-tuple-element.61), channel_id=1, source_target_pairs={{6,0},{10,8},{4,2},{8,10},{2,4},{14,12},{0,6},{12,14},{7,1},{11,9}... | collective-permute-start | bytes 1769480 | tf_op jit(solution)/shard_map/ppermute | solution.py:29
  81.0 15.5 %collective-permute-start.15 = (bf16[8,8,4608]{2,1,0:T(8,128)(2,1)S(1)}, bf16[8,8,4608]{2,1,0:T(8,128)(2,1)S(1)}, u32[]{:S(2)}, u32[]{:S(2)}) collective-permute-start(bf16[8,8,4608]{2,1,0:T(8,128)(2,1)S(1)} %get-tuple-element.62), channel_id=1, source_target_pairs={{17,0},{9,8},{19,2},{11,10},{21,4},{13,12},{23,6},{15,14},{16,1},{... | collective-permute-start | bytes 1769480 | tf_op jit(solution)/shard_map/ppermute | solution.py:29
  81.1 16.9 %collective-permute-start.17 = (bf16[8,8,4608]{2,1,0:T(8,128)(2,1)}, bf16[8,8,4608]{2,1,0:T(8,128)(2,1)}, u32[]{:S(2)}, u32[]{:S(2)}) collective-permute-start(bf16[8,8,4608]{2,1,0:T(8,128)(2,1)} %get-tuple-element.64), channel_id=1, source_target_pairs={{119,0},{43,8},{117,2},{41,10},{115,4},{47,12},{113,6},{45,14},{11... | collective-permute-start | bytes 1769480 | tf_op jit(solution)/shard_map/ppermute | solution.py:29
  89.6 8.1 %copy-start.1 = (bf16[32,8,4608]{2,1,0:T(8,128)(2,1)S(1)}, bf16[32,8,4608]{2,1,0:T(8,128)(2,1)}, u32[]{:S(2)}) copy-start(bf16[32,8,4608]{2,1,0:T(8,128)(2,1)} %copy-done) | copy-start | bytes 7077892
  90.2 12.6 %collective-permute-start.14 = (bf16[8,8,4608]{2,1,0:T(8,128)(2,1)S(1)}, bf16[8,8,4608]{2,1,0:T(8,128)(2,1)S(1)}, u32[]{:S(2)}, u32[]{:S(2)}) collective-permute-start(bf16[8,8,4608]{2,1,0:T(8,128)(2,1)S(1)} %add_convert_fusion.5), channel_id=1, source_target_pairs={{17,0},{9,8},{19,2},{11,10},{21,4},{13,12},{23,6},{15,14},{16,1},{... | collective-permute-start | bytes 1769480 | tf_op jit(solution)/shard_map/ppermute | solution.py:29
  90.4 12.4 %collective-permute-start.12 = (bf16[8,8,4608]{2,1,0:T(8,128)(2,1)S(1)}, bf16[8,8,4608]{2,1,0:T(8,128)(2,1)S(1)}, u32[]{:S(2)}, u32[]{:S(2)}) collective-permute-start(bf16[8,8,4608]{2,1,0:T(8,128)(2,1)S(1)} %add_convert_fusion.6), channel_id=1, source_target_pairs={{6,0},{10,8},{4,2},{8,10},{2,4},{14,12},{0,6},{12,14},{7,1},{11,9}... | collective-permute-start | bytes 1769480 | tf_op jit(solution)/shard_map/ppermute | solution.py:29
  96.7 9.1 %collective-permute-start.16 = (bf16[8,8,4608]{2,1,0:T(8,128)(2,1)S(1)}, bf16[8,8,4608]{2,1,0:T(8,128)(2,1)S(1)}, u32[]{:S(2)}, u32[]{:S(2)}) collective-permute-start(bf16[8,8,4608]{2,1,0:T(8,128)(2,1)S(1)} %add_convert_fusion.4), channel_id=1, source_target_pairs={{96,0},{40,8},{98,2},{42,10},{100,4},{44,12},{102,6},{46,14},{97,1... | collective-permute-start | bytes 1769480 | tf_op jit(solution)/shard_map/ppermute | solution.py:29
  105.8 15.7 %copy-start.5 = (f32[8,4608]{1,0:T(8,128)S(1)}, f32[8,4608]{1,0:T(8,128)}, u32[]{:S(2)}) copy-start(f32[8,4608]{1,0:T(8,128)} %copy-done.4) | copy-start | bytes 442372
  105.8 15.7 %copy-start.8 = (f32[4608]{0:T(1024)S(1)}, f32[4608]{0:T(1024)}, u32[]{:S(2)}) copy-start(f32[4608]{0:T(1024)} %param.11) | copy-start | bytes 55300
  135.2 9.1 %collective-permute-start.20 = (bf16[8,8,4608]{2,1,0:T(8,128)(2,1)S(1)}, bf16[8,8,4608]{2,1,0:T(8,128)(2,1)}, u32[]{:S(2)}, u32[]{:S(2)}) collective-permute-start(bf16[8,8,4608]{2,1,0:T(8,128)(2,1)S(1)} %all_to_all.31), channel_id=1, source_target_pairs={{96,0},{40,8},{98,2},{42,10},{100,4},{44,12},{102,6},{46,14},{97,1... | collective-permute-start | bytes 1769480 | tf_op jit(solution)/shard_map/ppermute | solution.py:29
  135.2 9.1 %collective-permute-start.19 = (bf16[8,8,4608]{2,1,0:T(8,128)(2,1)S(1)}, bf16[8,8,4608]{2,1,0:T(8,128)(2,1)}, u32[]{:S(2)}, u32[]{:S(2)}) collective-permute-start(bf16[8,8,4608]{2,1,0:T(8,128)(2,1)S(1)} %all_to_all.31), channel_id=1, source_target_pairs={{17,0},{9,8},{19,2},{11,10},{21,4},{13,12},{23,6},{15,14},{16,1},{... | collective-permute-start | bytes 1769480 | tf_op jit(solution)/shard_map/ppermute | solution.py:29
  135.2 9.1 %collective-permute-start.18 = (bf16[8,8,4608]{2,1,0:T(8,128)(2,1)S(1)}, bf16[8,8,4608]{2,1,0:T(8,128)(2,1)}, u32[]{:S(2)}, u32[]{:S(2)}) collective-permute-start(bf16[8,8,4608]{2,1,0:T(8,128)(2,1)S(1)} %all_to_all.31), channel_id=1, source_target_pairs={{6,0},{10,8},{4,2},{8,10},{2,4},{14,12},{0,6},{12,14},{7,1},{11,9}... | collective-permute-start | bytes 1769480 | tf_op jit(solution)/shard_map/ppermute | solution.py:29
  146.1 9.1 %collective-permute-start.21 = (bf16[32,8,4608]{2,1,0:T(8,128)(2,1)S(1)}, bf16[32,8,4608]{2,1,0:T(8,128)(2,1)S(1)}, u32[]{:S(2)}, u32[]{:S(2)}) collective-permute-start(bf16[32,8,4608]{2,1,0:T(8,128)(2,1)S(1)} %pad_maximum_fusion.5), channel_id=1, source_target_pairs={{0,8},{8,0},{1,9},{9,1},{2,10},{10,2},{3,11},{11,3},{4,12},{12,4},... | collective-permute-start | bytes 7077896 | tf_op jit(solution)/shard_map/ppermute | solution.py:50
  151.0 12.6 %collective-permute-start.25 = (bf16[8,8,4608]{2,1,0:T(8,128)(2,1)}, bf16[8,8,4608]{2,1,0:T(8,128)(2,1)}, u32[]{:S(2)}, u32[]{:S(2)}) collective-permute-start(bf16[8,8,4608]{2,1,0:T(8,128)(2,1)} %collective-permute-done.20), channel_id=1, source_target_pairs={{23,0},{11,8},{21,2},{9,10},{19,4},{15,12},{17,6},{13,14},{22,1},{... | collective-permute-start | bytes 1769480 | tf_op jit(solution)/shard_map/ppermute | solution.py:29
  152.7 14.8 %collective-permute-start.23 = (bf16[8,8,4608]{2,1,0:T(8,128)(2,1)}, bf16[8,8,4608]{2,1,0:T(8,128)(2,1)}, u32[]{:S(2)}, u32[]{:S(2)}) collective-permute-start(bf16[8,8,4608]{2,1,0:T(8,128)(2,1)} %collective-permute-done.20), channel_id=1, source_target_pairs={{17,0},{9,8},{19,2},{11,10},{21,4},{13,12},{23,6},{15,14},{16,1},{... | collective-permute-start | bytes 1769480 | tf_op jit(solution)/shard_map/ppermute | solution.py:29
  153.2 14.3 %collective-permute-start.22 = (bf16[8,8,4608]{2,1,0:T(8,128)(2,1)}, bf16[8,8,4608]{2,1,0:T(8,128)(2,1)}, u32[]{:S(2)}, u32[]{:S(2)}) collective-permute-start(bf16[8,8,4608]{2,1,0:T(8,128)(2,1)} %collective-permute-done.19), channel_id=1, source_target_pairs={{6,0},{10,8},{4,2},{8,10},{2,4},{14,12},{0,6},{12,14},{7,1},{11,9}... | collective-permute-start | bytes 1769480 | tf_op jit(solution)/shard_map/ppermute | solution.py:29
  153.6 13.9 %collective-permute-start.24 = (bf16[8,8,4608]{2,1,0:T(8,128)(2,1)}, bf16[8,8,4608]{2,1,0:T(8,128)(2,1)}, u32[]{:S(2)}, u32[]{:S(2)}) collective-permute-start(bf16[8,8,4608]{2,1,0:T(8,128)(2,1)} %collective-permute-done.18), channel_id=1, source_target_pairs={{96,0},{40,8},{98,2},{42,10},{100,4},{44,12},{102,6},{46,14},{97,1... | collective-permute-start | bytes 1769480 | tf_op jit(solution)/shard_map/ppermute | solution.py:29
  163.5 9.6 %copy-start.3 = (bf16[512,512]{1,0:T(8,128)(2,1)S(1)}, bf16[512,512]{1,0:T(8,128)(2,1)}, u32[]{:S(2)}) copy-start(bf16[512,512]{1,0:T(8,128)(2,1)} %copy-done.2) | copy-start | bytes 1572868
  169.4 6.8 %copy-start.6 = (bf16[256,512]{1,0:T(8,128)(2,1)S(1)}, bf16[256,512]{1,0:T(8,128)(2,1)}, u32[]{:S(2)}) copy-start(bf16[256,512]{1,0:T(8,128)(2,1)} %get-tuple-element.94) | copy-start | bytes 786436
  169.4 8.2 %collective-permute-start.26 = (bf16[32,8,4608]{2,1,0:T(8,128)(2,1)S(1)}, bf16[32,8,4608]{2,1,0:T(8,128)(2,1)S(1)}, u32[]{:S(2)}, u32[]{:S(2)}) collective-permute-start(bf16[32,8,4608]{2,1,0:T(8,128)(2,1)S(1)} %pad_maximum_fusion.6), channel_id=1, source_target_pairs={{0,8},{8,0},{1,9},{9,1},{2,10},{10,2},{3,11},{11,3},{4,12},{12,4},... | collective-permute-start | bytes 7077896 | tf_op jit(solution)/shard_map/ppermute | solution.py:50
  176.2 1.4 copy-start.7
  179.4 4.4 %slice-start.4 = ((s8[4718592]{0:T(1024)(128)(4,1)}), s8[4194304]{0:T(1024)(128)(4,1)S(1)}, s32[]{:S(2)}) async-start(s8[4718592]{0:T(1024)(128)(4,1)} %bitcast.81), calls=%async_computation.8 | async-start | bytes 8388608
  179.5 4.4 %slice-start.5 = ((s8[4718592]{0:T(1024)(128)(4,1)}), s8[524288]{0:T(1024)(128)(4,1)S(1)}, s32[]{:S(2)}) async-start(s8[4718592]{0:T(1024)(128)(4,1)} %bitcast.81), calls=%async_computation.9 | async-start | bytes 1048576

commit v6 on v4

--- a/solution.py
+++ b/solution.py
@@ -77,10 +77,16 @@
     return near, done, flat(distant), flat(swap(distant))
 
 
+def sums(mine, theirs):
+    pairs = zip(*(jnp.split(rows.reshape(32, 8, -1), 4) for rows in (mine, theirs)))
+    return barrier(*(add(*pair).astype(bf16) for pair in pairs))
+
+
 def scatter(near, distant, work):
-    (own, x, y, z), (xy, yz, zx, xyz) = near, distant
+    xy, yz, zx, xyz = distant
     y_more, z_more, x_more = receive(xy, "x", 1), receive(yz, "y", 1), receive(zx, "z", 1)
     xyz = receive(xyz, "xyz", 1)
+    own, x, y, z = sums(*barrier(*near, y_more)[:2])
     x, y, z = (add(*pair).astype(bf16) for pair in ((x, x_more), (y, y_more), (z, z_more)))
     done = work(x_more)
     x, y, z = receive(x, "x", 1), receive(y, "y", 1), receive(z, "z", 1)
@@ -114,11 +120,10 @@
             barrier(jnp.dot(rows, dec_weight, preferred_element_type=f32).astype(bf16))[0]
             for rows in (theirs, mine)
         )
-        pairs = zip(*(jnp.split(rows.reshape(32, 8, -1), 4) for rows in (mine, swap(theirs))))
-        return barrier(*(add(*pair).astype(bf16) for pair in pairs))
+        return mine, swap(theirs)
 
     recon_near = decode(code_near[:256], code_near[256:])
-    recon_distant = decode(code_mine, code_theirs)
+    recon_distant = sums(*decode(code_mine, code_theirs))
 
     def side_work(received):
         *rest, dec, _ = barrier(

time: 186 us -> 187 us (level)
  starting transfers between devices: 24.6 us -> 26.8 us
  transfers between devices with their start and end apart: 27 -> 27, of which waited for: 15 -> 16; matrix products, arithmetic and copies ran while one was open for 16% -> 15% of each run, Pallas kernels for 0% -> 0%
where the time goes in v6:
time: 187 us
  blocking collectives  57.3 us (31%)
  waiting for transfers between devices  51.4 us (27%)
  matrix products  33.6 us (18%)
  starting transfers between devices  26.8 us (14%)
  other arithmetic  15.7 us (8%)
    ppermute x21, waiting for transfers between devices, receive(): return lax.ppermute(block, MESH, pairs)  46.5 us
    all_to_all x3, blocking collectives, trade(): return lax.all_to_all(blocks, MESH, 0, 0, axis_index_groups=cubes(pairing))  46.3 us
    ppermute x6, starting transfers between devices, swap(): return lax.ppermute(block, 'core', [(0, 1), (1, 0)])  14.4 us
    ppermute x21, starting transfers between devices, receive(): return lax.ppermute(block, MESH, pairs)  12.4 us
    all_to_all x1, blocking collectives, on_device(): lax.all_to_all(activations, ('x', 'yl'), split_axis=0, concat_axis=1, til...  11 us
    dot_general x3, matrix products, preact_grad(): lax.dot_general(delta, dec_weight, (((1,), (1,)), ((), ())), preferred_el...  6.67 us
    dot_general x4, matrix products, decode(): jnp.dot(rows, dec_weight, preferred_element_type=f32).astype(bf16)  5.54 us
    dot_general x3, matrix products, encode(): jnp.dot(rows, enc_weight, preferred_element_type=f32) + enc_bias  5.34 us
  transfers between devices with their start and end apart: 27, of which 16 were waited for; matrix products, arithmetic and copies ran while one was open for 15% of the time, Pallas kernels for 0%

profile of v6, /device:TPU:1, one launch (start us, length us, event | category | flops | bytes accessed | tf_op | source)
XLA Modules:
  0.0 187.0 jit_solution(18288526207387572901)
XLA Ops:
  0.6 11.0 %all_to_all.28 = bf16[8,8,576]{2,1,0:T(8,128)(2,1)S(1)} all-to-all(bf16[8,8,576]{2,1,0:T(8,128)(2,1)} %bitcast.78), channel_id=1, replica_groups=mesh['z'=4,'yh'=2,'core'=2,'x'=4,'yl'=2] {'x','yl'}, dimensions={0} | all-to-all | bytes 147456 | tf_op jit(solution)/shard_map/all_to_all | solution.py:100
  12.6 18.5 %all_to_all.29 = bf16[8,8,4608]{2,1,0:T(8,128)(2,1)S(1)} all-to-all(bf16[8,8,4608]{2,1,0:T(8,128)(2,1)S(1)} %broadcast_in_dim.4), channel_id=1, replica_groups={{0,2,1,3,32,34,33,35},{4,6,5,7,36,38,37,39},{16,18,17,19,48,50,49,51},{..., dimensions={0} | all-to-all | bytes 1179648 | tf_op jit(solution)/shard_map/all_to_all | solution.py:46
  31.1 9.0 %collective-permute-done.2 = bf16[8,8,4608]{2,1,0:T(8,128)(2,1)S(1)} collective-permute-done((bf16[8,8,4608]{2,1,0:T(8,128)(2,1)S(1)}, bf16[8,8,4608]{2,1,0:T(8,128)(2,1)S(1)}, u32[]{:S(2)}, u32[]{:S(2)}) %collective-permute-start.2) | collective-permute-done | bytes 589856 | tf_op jit(solution)/shard_map/ppermute | solution.py:29
  40.5 2.4 %collective-permute-start.3 = (bf16[32,8,4608]{2,1,0:T(8,128)(2,1)S(1)}, bf16[32,8,4608]{2,1,0:T(8,128)(2,1)S(1)}, u32[]{:S(2)}, u32[]{:S(2)}) collective-permute-start(bf16[32,8,4608]{2,1,0:T(8,128)(2,1)S(1)} %pad_maximum_fusion.3), channel_id=1, source_target_pairs={{0,8},{8,0},{1,9},{9,1},{2,10},{10,2},{3,11},{11,3},{4,12},{12,4},... | collective-permute-start | bytes 7077896 | tf_op jit(solution)/shard_map/ppermute | solution.py:50
  43.5 2.1 %collective-permute-start.5 = (bf16[8,8,4608]{2,1,0:T(8,128)(2,1)S(1)}, bf16[8,8,4608]{2,1,0:T(8,128)(2,1)S(1)}, u32[]{:S(2)}, u32[]{:S(2)}) collective-permute-start(bf16[8,8,4608]{2,1,0:T(8,128)(2,1)S(1)} %collective-permute-done.1), channel_id=1, source_target_pairs={{6,0},{10,8},{4,2},{8,10},{2,4},{14,12},{0,6},{12,14},{7,1},{11,9}... | collective-permute-start | bytes 1769480 | tf_op jit(solution)/shard_map/ppermute | solution.py:29
  46.1 1.0 collective-permute-done.3
  47.6 2.6 %convolution_add_fusion = f32[512,512]{1,0:T(8,128)S(1)} fusion(bf16[4608,512]{1,0:T(8,128)(2,1)S(1)} %bitcast.80, f32[512]{0:T(512)S(1)} %copy-done.9, bf16[64,8,4608]{2,1,0:T(8,128)(2,1)S(1)} %pad_maximum_fusion), kind=kOutput, calls=%fused_computation.22 | convolution fusion | flops 2416181248 | bytes 10487808 | tf_op jit(solution)/shard_map/dot_general | solution.py:105
  50.2 1.4 fusion.37
  51.6 1.3 collective-permute-done.8
  52.9 5.4 %collective-permute-done.6 = bf16[8,8,4608]{2,1,0:T(8,128)(2,1)S(1)} collective-permute-done((bf16[8,8,4608]{2,1,0:T(8,128)(2,1)S(1)}, bf16[8,8,4608]{2,1,0:T(8,128)(2,1)S(1)}, u32[]{:S(2)}, u32[]{:S(2)}) %collective-permute-start.6) | collective-permute-done | bytes 589856 | tf_op jit(solution)/shard_map/ppermute | solution.py:29
  59.0 3.7 %collective-permute-start.9 = (bf16[32,8,4608]{2,1,0:T(8,128)(2,1)S(1)}, bf16[32,8,4608]{2,1,0:T(8,128)(2,1)S(1)}, u32[]{:S(2)}, u32[]{:S(2)}) collective-permute-start(bf16[32,8,4608]{2,1,0:T(8,128)(2,1)S(1)} %pad_maximum_fusion.4), channel_id=1, source_target_pairs={{0,8},{8,0},{1,9},{9,1},{2,10},{10,2},{3,11},{11,3},{4,12},{12,4},... | collective-permute-start | bytes 7077896 | tf_op jit(solution)/shard_map/ppermute | solution.py:50
  62.7 1.4 convolution_add_fusion.4
  64.1 1.1 fusion.35
  65.1 1.7 collective-permute-done.9
  66.9 1.4 convolution_add_fusion.3
  68.3 1.0 fusion.33
  69.3 1.4 convolution_convert_fusion.1
  71.2 1.4 convolution_convert_fusion.3
  72.8 1.4 convolution_convert_fusion.2
  74.2 1.2 collective-permute-done.10
  75.3 1.4 fusion.20
  76.7 1.4 convolution_convert_fusion.4
  78.8 3.2 %collective-permute-start.17 = (bf16[8,8,4608]{2,1,0:T(8,128)(2,1)}, bf16[8,8,4608]{2,1,0:T(8,128)(2,1)}, u32[]{:S(2)}, u32[]{:S(2)}) collective-permute-start(bf16[8,8,4608]{2,1,0:T(8,128)(2,1)} %get-tuple-element.70), channel_id=1, source_target_pairs={{119,0},{43,8},{117,2},{41,10},{115,4},{47,12},{113,6},{45,14},{11... | collective-permute-start | bytes 1769480 | tf_op jit(solution)/shard_map/ppermute | solution.py:29
  82.0 3.7 %collective-permute-done.11 = bf16[8,8,4608]{2,1,0:T(8,128)(2,1)S(1)} collective-permute-done((bf16[8,8,4608]{2,1,0:T(8,128)(2,1)S(1)}, bf16[8,8,4608]{2,1,0:T(8,128)(2,1)S(1)}, u32[]{:S(2)}, u32[]{:S(2)}) %collective-permute-start.11) | collective-permute-done | bytes 589856 | tf_op jit(solution)/shard_map/ppermute | solution.py:29
  86.5 7.1 %collective-permute-done.12 = bf16[8,8,4608]{2,1,0:T(8,128)(2,1)S(1)} collective-permute-done((bf16[8,8,4608]{2,1,0:T(8,128)(2,1)S(1)}, bf16[8,8,4608]{2,1,0:T(8,128)(2,1)S(1)}, u32[]{:S(2)}, u32[]{:S(2)}) %collective-permute-start.12) | collective-permute-done | bytes 589856 | tf_op jit(solution)/shard_map/ppermute | solution.py:29
  93.8 1.4 collective-permute-start.13
  95.2 1.0 multiply_reduce_fusion
  98.2 2.2 %collective-permute-done.14 = bf16[8,8,4608]{2,1,0:T(8,128)(2,1)S(1)} collective-permute-done((bf16[8,8,4608]{2,1,0:T(8,128)(2,1)S(1)}, bf16[8,8,4608]{2,1,0:T(8,128)(2,1)S(1)}, u32[]{:S(2)}, u32[]{:S(2)}) %collective-permute-start.14) | collective-permute-done | bytes 589856 | tf_op jit(solution)/shard_map/ppermute | solution.py:29
  100.4 2.5 %collective-permute-done.13 = bf16[8,8,4608]{2,1,0:T(8,128)(2,1)S(1)} collective-permute-done((bf16[8,8,4608]{2,1,0:T(8,128)(2,1)S(1)}, bf16[8,8,4608]{2,1,0:T(8,128)(2,1)S(1)}, u32[]{:S(2)}, u32[]{:S(2)}) %collective-permute-start.13) | collective-permute-done | bytes 589856 | tf_op jit(solution)/shard_map/ppermute | solution.py:29
  102.9 2.6 %collective-permute-done.16 = bf16[8,8,4608]{2,1,0:T(8,128)(2,1)S(1)} collective-permute-done((bf16[8,8,4608]{2,1,0:T(8,128)(2,1)S(1)}, bf16[8,8,4608]{2,1,0:T(8,128)(2,1)S(1)}, u32[]{:S(2)}, u32[]{:S(2)}) %collective-permute-start.16) | collective-permute-done | bytes 589856 | tf_op jit(solution)/shard_map/ppermute | solution.py:29
  105.5 1.5 add_convert_fusion.3
  107.0 14.2 %all_to_all.30 = bf16[8,8,4608]{2,1,0:T(8,128)(2,1)S(1)} all-to-all(bf16[8,8,4608]{2,1,0:T(8,128)(2,1)S(1)} %add_convert_fusion.3), channel_id=1, replica_groups={{0,2,1,3,32,34,33,35},{4,6,5,7,36,38,37,39},{16,18,17,19,48,50,49,51},{..., dimensions={0} | all-to-all | bytes 1179648 | tf_op jit(solution)/shard_map/all_to_all | solution.py:46
  121.3 13.6 %all_to_all.31 = bf16[8,8,4608]{2,1,0:T(8,128)(2,1)S(1)} all-to-all(bf16[8,8,4608]{2,1,0:T(8,128)(2,1)S(1)} %broadcast_in_dim.5), channel_id=1, replica_groups={{0,2,1,3,32,34,33,35},{4,6,5,7,36,38,37,39},{16,18,17,19,48,50,49,51},{..., dimensions={0} | all-to-all | bytes 1179648 | tf_op jit(solution)/shard_map/all_to_all | solution.py:46
  135.0 9.1 %collective-permute-done.20 = bf16[8,8,4608]{2,1,0:T(8,128)(2,1)} collective-permute-done((bf16[8,8,4608]{2,1,0:T(8,128)(2,1)S(1)}, bf16[8,8,4608]{2,1,0:T(8,128)(2,1)}, u32[]{:S(2)}, u32[]{:S(2)}) %collective-permute-start.20) | collective-permute-done | bytes 589856 | tf_op jit(solution)/shard_map/ppermute | solution.py:29
  144.1 1.7 pad_maximum_fusion.5
  145.8 3.5 %collective-permute-start.21 = (bf16[32,8,4608]{2,1,0:T(8,128)(2,1)S(1)}, bf16[32,8,4608]{2,1,0:T(8,128)(2,1)S(1)}, u32[]{:S(2)}, u32[]{:S(2)}) collective-permute-start(bf16[32,8,4608]{2,1,0:T(8,128)(2,1)S(1)} %pad_maximum_fusion.5), channel_id=1, source_target_pairs={{0,8},{8,0},{1,9},{9,1},{2,10},{10,2},{3,11},{11,3},{4,12},{12,4},... | collective-permute-start | bytes 7077896 | tf_op jit(solution)/shard_map/ppermute | solution.py:50
  149.9 2.0 %collective-permute-start.22 = (bf16[8,8,4608]{2,1,0:T(8,128)(2,1)}, bf16[8,8,4608]{2,1,0:T(8,128)(2,1)}, u32[]{:S(2)}, u32[]{:S(2)}) collective-permute-start(bf16[8,8,4608]{2,1,0:T(8,128)(2,1)} %collective-permute-done.19), channel_id=1, source_target_pairs={{6,0},{10,8},{4,2},{8,10},{2,4},{14,12},{0,6},{12,14},{7,1},{11,9}... | collective-permute-start | bytes 1769480 | tf_op jit(solution)/shard_map/ppermute | solution.py:29
  152.5 1.0 collective-permute-done.21
  153.9 3.9 %fusion.9 = bf16[512,512]{1,0:T(8,128)(2,1)S(1)} fusion(f32[512,512]{1,0:T(8,128)} %get-tuple-element.53, bf16[512,4608]{1,0:T(8,128)(2,1)S(1)} %bitcast.69, bf16[64,8,4608]{2,1,0:T(8,128)(2,1)S(1)} %pad_maximum_fusion.1, f32[512]{0:T(512)S(1)} %get-tuple-element.90), kind=kOutput, calls=%fused_computation.23 | convolution fusion | flops 2416705536 | bytes 11012096 | tf_op jit(solution)/shard_map/dot_general | solution.py:152
  157.7 4.3 %convolution_convert_fusion = bf16[4608,512]{1,0:T(8,128)(2,1)} fusion(bf16[4608,512]{0,1:T(8,128)(2,1)S(1)} %bitcast.72, bf16[512,512]{1,0:T(8,128)(2,1)S(1)} %fusion.9), kind=kOutput, calls=%fused_computation.4 | convolution fusion | flops 2418278400 | bytes 9961472 | tf_op jit(solution)/shard_map/dot_general | solution.py:161
  162.1 2.9 %collective-permute-done.23 = bf16[8,8,4608]{2,1,0:T(8,128)(2,1)} collective-permute-done((bf16[8,8,4608]{2,1,0:T(8,128)(2,1)}, bf16[8,8,4608]{2,1,0:T(8,128)(2,1)}, u32[]{:S(2)}, u32[]{:S(2)}) %collective-permute-start.23) | collective-permute-done | bytes 589856 | tf_op jit(solution)/shard_map/ppermute | solution.py:29
  165.3 1.9 %pad_maximum_fusion.6 = bf16[32,8,4608]{2,1,0:T(8,128)(2,1)S(1)} fusion(bf16[8,8,4608]{2,1,0:T(8,128)(2,1)} %collective-permute-done.25, bf16[8,8,4608]{2,1,0:T(8,128)(2,1)} %collective-permute-done.24, bf16[8,8,4608]{2,1,0:T(8,128)(2,1)} %collective-permute-done.23, bf16[8,8,4608]{2,1,0:T(8,128)(2,1)} %collective-permute-done.22), kind=kLoop, calls=%fused_computation.19 | loop fusion | flops 3538944 | bytes 4718592 | tf_op jit(solution)/shard_map/concatenate | solution.py:76
  167.2 4.0 %collective-permute-start.26 = (bf16[32,8,4608]{2,1,0:T(8,128)(2,1)S(1)}, bf16[32,8,4608]{2,1,0:T(8,128)(2,1)S(1)}, u32[]{:S(2)}, u32[]{:S(2)}) collective-permute-start(bf16[32,8,4608]{2,1,0:T(8,128)(2,1)S(1)} %pad_maximum_fusion.6), channel_id=1, source_target_pairs={{0,8},{8,0},{1,9},{9,1},{2,10},{10,2},{3,11},{11,3},{4,12},{12,4},... | collective-permute-start | bytes 7077896 | tf_op jit(solution)/shard_map/ppermute | solution.py:50
  171.2 3.1 %add_convert_fusion.2 = bf16[512,4608]{1,0:T(8,128)(2,1)S(1)} fusion(bf16[512,4608]{1,0:T(8,128)(2,1)S(1)} %bitcast.69, bf16[512,512]{0,1:T(8,128)(2,1)S(1)} %bitcast.77, bf16[64,8,4608]{2,1,0:T(8,128)(2,1)S(1)} %pad_maximum_fusion.1, f32[512]{0:T(512)S(1)} %get-tuple-element.98), kind=kOutput, calls=%fused_computation.2 | convolution fusion | flops 2425356288 | bytes 14682112 | tf_op jit(solution)/shard_map/dot_general | solution.py:164
  174.3 1.4 fusion.14
  175.8 1.4 fusion.15
  178.3 4.3 %add_convert_fusion = bf16[512,4608]{1,0:T(8,128)(2,1)} fusion(bf16[512,4608]{1,0:T(8,128)(2,1)S(1)} %add_convert_fusion.2, bf16[512,512]{0,1:T(8,128)(2,1)S(1)} %copy-done.2, bf16[512,4608]{1,0:T(8,128)(2,1)S(1)} %pad_maximum_fusion.2), kind=kOutput, calls=%fused_computation | convolution fusion | flops 2422996992 | bytes 14680064 | tf_op jit(solution)/shard_map/dot_general | solution.py:172
  182.6 4.4 %add_convert_fusion.1 = bf16[4608,512]{1,0:T(8,128)(2,1)} fusion(bf16[4608,512]{1,0:T(8,128)(2,1)S(1)} %bitcast.82, bf16[4608,512]{0,1:T(8,128)(2,1)S(1)} %maximum_bitcast_fusion, bf16[512,512]{1,0:T(8,128)(2,1)S(1)} %pad_maximum_fusion.7), kind=kOutput, calls=%fused_computation.1 | convolution fusion | flops 2422996992 | bytes 14680064 | tf_op jit(solution)/shard_map/dot_general | solution.py:171
  (88 shorter events, 10.7 us)
Async XLA Ops:
  11.8 28.7 %copy-start.3 = (f32[8,4608]{1,0:T(8,128)}, f32[8,4608]{1,0:T(8,128)S(1)}, u32[]{:S(2)}) copy-start(f32[8,4608]{1,0:T(8,128)S(1)} %reshape.90) | copy-start | bytes 442372
  31.1 9.0 %collective-permute-start.2 = (bf16[8,8,4608]{2,1,0:T(8,128)(2,1)S(1)}, bf16[8,8,4608]{2,1,0:T(8,128)(2,1)S(1)}, u32[]{:S(2)}, u32[]{:S(2)}) collective-permute-start(bf16[8,8,4608]{2,1,0:T(8,128)(2,1)S(1)} %all_to_all.29), channel_id=1, source_target_pairs={{96,0},{40,8},{98,2},{42,10},{100,4},{44,12},{102,6},{46,14},{97,1... | collective-permute-start | bytes 1769480 | tf_op jit(solution)/shard_map/ppermute | solution.py:29
  31.1 9.0 %collective-permute-start.1 = (bf16[8,8,4608]{2,1,0:T(8,128)(2,1)S(1)}, bf16[8,8,4608]{2,1,0:T(8,128)(2,1)S(1)}, u32[]{:S(2)}, u32[]{:S(2)}) collective-permute-start(bf16[8,8,4608]{2,1,0:T(8,128)(2,1)S(1)} %all_to_all.29), channel_id=1, source_target_pairs={{17,0},{9,8},{19,2},{11,10},{21,4},{13,12},{23,6},{15,14},{16,1},{... | collective-permute-start | bytes 1769480 | tf_op jit(solution)/shard_map/ppermute | solution.py:29
  31.1 9.0 %collective-permute-start = (bf16[8,8,4608]{2,1,0:T(8,128)(2,1)S(1)}, bf16[8,8,4608]{2,1,0:T(8,128)(2,1)S(1)}, u32[]{:S(2)}, u32[]{:S(2)}) collective-permute-start(bf16[8,8,4608]{2,1,0:T(8,128)(2,1)S(1)} %all_to_all.29), channel_id=1, source_target_pairs={{6,0},{10,8},{4,2},{8,10},{2,4},{14,12},{0,6},{12,14},{7,1},{11,9}... | collective-permute-start | bytes 1769480 | tf_op jit(solution)/shard_map/ppermute | solution.py:29
  40.2 7.4 %slice-start.2 = ((s8[4718592]{0:T(1024)(128)(4,1)}), s8[4194304]{0:T(1024)(128)(4,1)S(1)}, s32[]{:S(2)}) async-start(s8[4718592]{0:T(1024)(128)(4,1)} %bitcast.79), calls=%async_computation.6 | async-start | bytes 8388608
  40.5 7.1 %slice-start.3 = ((s8[4718592]{0:T(1024)(128)(4,1)}), s8[524288]{0:T(1024)(128)(4,1)S(1)}, s32[]{:S(2)}) async-start(s8[4718592]{0:T(1024)(128)(4,1)} %bitcast.79), calls=%async_computation.7 | async-start | bytes 1048576
  40.5 7.1 %copy-start.9 = (f32[512]{0:T(512)S(1)}, f32[512]{0:T(512)}, u32[]{:S(2)}) copy-start(f32[512]{0:T(512)} %param.8) | copy-start | bytes 6148
  40.5 6.6 %collective-permute-start.3 = (bf16[32,8,4608]{2,1,0:T(8,128)(2,1)S(1)}, bf16[32,8,4608]{2,1,0:T(8,128)(2,1)S(1)}, u32[]{:S(2)}, u32[]{:S(2)}) collective-permute-start(bf16[32,8,4608]{2,1,0:T(8,128)(2,1)S(1)} %pad_maximum_fusion.3), channel_id=1, source_target_pairs={{0,8},{8,0},{1,9},{9,1},{2,10},{10,2},{3,11},{11,3},{4,12},{12,4},... | collective-permute-start | bytes 7077896 | tf_op jit(solution)/shard_map/ppermute | solution.py:50
  43.0 10.0 %collective-permute-start.8 = (bf16[8,8,4608]{2,1,0:T(8,128)(2,1)S(1)}, bf16[8,8,4608]{2,1,0:T(8,128)(2,1)S(1)}, u32[]{:S(2)}, u32[]{:S(2)}) collective-permute-start(bf16[8,8,4608]{2,1,0:T(8,128)(2,1)S(1)} %collective-permute-done.2), channel_id=1, source_target_pairs={{23,0},{11,8},{21,2},{9,10},{19,4},{15,12},{17,6},{13,14},{22,1},{... | collective-permute-start | bytes 1769480 | tf_op jit(solution)/shard_map/ppermute | solution.py:29
  43.0 15.3 %collective-permute-start.6 = (bf16[8,8,4608]{2,1,0:T(8,128)(2,1)S(1)}, bf16[8,8,4608]{2,1,0:T(8,128)(2,1)S(1)}, u32[]{:S(2)}, u32[]{:S(2)}) collective-permute-start(bf16[8,8,4608]{2,1,0:T(8,128)(2,1)S(1)} %collective-permute-done.2), channel_id=1, source_target_pairs={{17,0},{9,8},{19,2},{11,10},{21,4},{13,12},{23,6},{15,14},{16,1},{... | collective-permute-start | bytes 1769480 | tf_op jit(solution)/shard_map/ppermute | solution.py:29
  43.5 15.1 %collective-permute-start.5 = (bf16[8,8,4608]{2,1,0:T(8,128)(2,1)S(1)}, bf16[8,8,4608]{2,1,0:T(8,128)(2,1)S(1)}, u32[]{:S(2)}, u32[]{:S(2)}) collective-permute-start(bf16[8,8,4608]{2,1,0:T(8,128)(2,1)S(1)} %collective-permute-done.1), channel_id=1, source_target_pairs={{6,0},{10,8},{4,2},{8,10},{2,4},{14,12},{0,6},{12,14},{7,1},{11,9}... | collective-permute-start | bytes 1769480 | tf_op jit(solution)/shard_map/ppermute | solution.py:29
  45.6 13.0 %collective-permute-start.7 = (bf16[8,8,4608]{2,1,0:T(8,128)(2,1)S(1)}, bf16[8,8,4608]{2,1,0:T(8,128)(2,1)S(1)}, u32[]{:S(2)}, u32[]{:S(2)}) collective-permute-start(bf16[8,8,4608]{2,1,0:T(8,128)(2,1)S(1)} %collective-permute-done), channel_id=1, source_target_pairs={{96,0},{40,8},{98,2},{42,10},{100,4},{44,12},{102,6},{46,14},{97,1... | collective-permute-start | bytes 1769480 | tf_op jit(solution)/shard_map/ppermute | solution.py:29
  47.6 2.6 %copy-start.8 = (f32[512]{0:T(512)S(1)}, f32[512]{0:T(512)}, u32[]{:S(2)}) copy-start(f32[512]{0:T(512)} %param.9) | copy-start | bytes 6148
  59.0 7.9 %collective-permute-start.9 = (bf16[32,8,4608]{2,1,0:T(8,128)(2,1)S(1)}, bf16[32,8,4608]{2,1,0:T(8,128)(2,1)S(1)}, u32[]{:S(2)}, u32[]{:S(2)}) collective-permute-start(bf16[32,8,4608]{2,1,0:T(8,128)(2,1)S(1)} %pad_maximum_fusion.4), channel_id=1, source_target_pairs={{0,8},{8,0},{1,9},{9,1},{2,10},{10,2},{3,11},{11,3},{4,12},{12,4},... | collective-permute-start | bytes 7077896 | tf_op jit(solution)/shard_map/ppermute | solution.py:50
  64.1 5.2 %slice-start = ((s8[4718592]{0:T(1024)(128)(4,1)}), s8[4194304]{0:T(1024)(128)(4,1)S(1)}, s32[]{:S(2)}) async-start(s8[4718592]{0:T(1024)(128)(4,1)} %bitcast.68), calls=%async_computation.4 | async-start | bytes 8388608
  66.9 1.4 copy-start
  66.9 2.5 %slice-start.1 = ((s8[4718592]{0:T(1024)(128)(4,1)}), s8[524288]{0:T(1024)(128)(4,1)S(1)}, s32[]{:S(2)}) async-start(s8[4718592]{0:T(1024)(128)(4,1)} %bitcast.68), calls=%async_computation.5 | async-start | bytes 1048576
  70.7 4.6 %collective-permute-start.10 = (bf16[256,4608]{1,0:T(8,128)(2,1)S(1)}, bf16[256,4608]{1,0:T(8,128)(2,1)S(1)}, u32[]{:S(2)}, u32[]{:S(2)}) collective-permute-start(bf16[256,4608]{1,0:T(8,128)(2,1)S(1)} %convolution_convert_fusion.1), channel_id=1, source_target_pairs={{0,8},{8,0},{1,9},{9,1},{2,10},{10,2},{3,11},{11,3},{4,12},{12,4},... | collective-permute-start | bytes 7077896 | tf_op jit(solution)/shard_map/ppermute | solution.py:50
  72.6 9.5 %collective-permute-start.4 = (bf16[256,4608]{1,0:T(8,128)(2,1)S(1)}, bf16[256,4608]{1,0:T(8,128)(2,1)S(1)}, u32[]{:S(2)}, u32[]{:S(2)}) collective-permute-start(bf16[256,4608]{1,0:T(8,128)(2,1)S(1)} %convolution_convert_fusion.3), channel_id=1, source_target_pairs={{0,8},{8,0},{1,9},{9,1},{2,10},{10,2},{3,11},{11,3},{4,12},{12,4},... | collective-permute-start | bytes 7077896 | tf_op jit(solution)/shard_map/ppermute | solution.py:50
  76.7 9.0 %collective-permute-start.11 = (bf16[8,8,4608]{2,1,0:T(8,128)(2,1)S(1)}, bf16[8,8,4608]{2,1,0:T(8,128)(2,1)S(1)}, u32[]{:S(2)}, u32[]{:S(2)}) collective-permute-start(bf16[8,8,4608]{2,1,0:T(8,128)(2,1)S(1)} %get-tuple-element.62), channel_id=1, source_target_pairs={{6,0},{10,8},{4,2},{8,10},{2,4},{14,12},{0,6},{12,14},{7,1},{11,9}... | collective-permute-start | bytes 1769480 | tf_op jit(solution)/shard_map/ppermute | solution.py:29
  78.1 15.5 %collective-permute-start.12 = (bf16[8,8,4608]{2,1,0:T(8,128)(2,1)S(1)}, bf16[8,8,4608]{2,1,0:T(8,128)(2,1)S(1)}, u32[]{:S(2)}, u32[]{:S(2)}) collective-permute-start(bf16[8,8,4608]{2,1,0:T(8,128)(2,1)S(1)} %get-tuple-element.66), channel_id=1, source_target_pairs={{96,0},{40,8},{98,2},{42,10},{100,4},{44,12},{102,6},{46,14},{97,1... | collective-permute-start | bytes 1769480 | tf_op jit(solution)/shard_map/ppermute | solution.py:29
  78.8 17.5 %collective-permute-start.15 = (bf16[8,8,4608]{2,1,0:T(8,128)(2,1)S(1)}, bf16[8,8,4608]{2,1,0:T(8,128)(2,1)S(1)}, u32[]{:S(2)}, u32[]{:S(2)}) collective-permute-start(bf16[8,8,4608]{2,1,0:T(8,128)(2,1)S(1)} %get-tuple-element.69), channel_id=1, source_target_pairs={{17,0},{9,8},{19,2},{11,10},{21,4},{13,12},{23,6},{15,14},{16,1},{... | collective-permute-start | bytes 1769480 | tf_op jit(solution)/shard_map/ppermute | solution.py:29
  78.8 19.4 %collective-permute-start.17 = (bf16[8,8,4608]{2,1,0:T(8,128)(2,1)}, bf16[8,8,4608]{2,1,0:T(8,128)(2,1)}, u32[]{:S(2)}, u32[]{:S(2)}) collective-permute-start(bf16[8,8,4608]{2,1,0:T(8,128)(2,1)} %get-tuple-element.70), channel_id=1, source_target_pairs={{119,0},{43,8},{117,2},{41,10},{115,4},{47,12},{113,6},{45,14},{11... | collective-permute-start | bytes 1769480 | tf_op jit(solution)/shard_map/ppermute | solution.py:29
  86.4 14.0 %collective-permute-start.14 = (bf16[8,8,4608]{2,1,0:T(8,128)(2,1)S(1)}, bf16[8,8,4608]{2,1,0:T(8,128)(2,1)S(1)}, u32[]{:S(2)}, u32[]{:S(2)}) collective-permute-start(bf16[8,8,4608]{2,1,0:T(8,128)(2,1)S(1)} %add_convert_fusion.5), channel_id=1, source_target_pairs={{17,0},{9,8},{19,2},{11,10},{21,4},{13,12},{23,6},{15,14},{16,1},{... | collective-permute-start | bytes 1769480 | tf_op jit(solution)/shard_map/ppermute | solution.py:29
  93.8 9.1 %collective-permute-start.13 = (bf16[8,8,4608]{2,1,0:T(8,128)(2,1)S(1)}, bf16[8,8,4608]{2,1,0:T(8,128)(2,1)S(1)}, u32[]{:S(2)}, u32[]{:S(2)}) collective-permute-start(bf16[8,8,4608]{2,1,0:T(8,128)(2,1)S(1)} %add_convert_fusion.6), channel_id=1, source_target_pairs={{6,0},{10,8},{4,2},{8,10},{2,4},{14,12},{0,6},{12,14},{7,1},{11,9}... | collective-permute-start | bytes 1769480 | tf_op jit(solution)/shard_map/ppermute | solution.py:29
  96.2 1.7 copy-start.1
  96.4 9.1 %collective-permute-start.16 = (bf16[8,8,4608]{2,1,0:T(8,128)(2,1)S(1)}, bf16[8,8,4608]{2,1,0:T(8,128)(2,1)S(1)}, u32[]{:S(2)}, u32[]{:S(2)}) collective-permute-start(bf16[8,8,4608]{2,1,0:T(8,128)(2,1)S(1)} %add_convert_fusion.4), channel_id=1, source_target_pairs={{96,0},{40,8},{98,2},{42,10},{100,4},{44,12},{102,6},{46,14},{97,1... | collective-permute-start | bytes 1769480 | tf_op jit(solution)/shard_map/ppermute | solution.py:29
  105.5 15.8 %copy-start.4 = (f32[8,4608]{1,0:T(8,128)S(1)}, f32[8,4608]{1,0:T(8,128)}, u32[]{:S(2)}) copy-start(f32[8,4608]{1,0:T(8,128)} %copy-done.3) | copy-start | bytes 442372
  105.5 15.8 %copy-start.7 = (f32[4608]{0:T(1024)S(1)}, f32[4608]{0:T(1024)}, u32[]{:S(2)}) copy-start(f32[4608]{0:T(1024)} %param.11) | copy-start | bytes 55300
  134.9 9.1 %collective-permute-start.20 = (bf16[8,8,4608]{2,1,0:T(8,128)(2,1)S(1)}, bf16[8,8,4608]{2,1,0:T(8,128)(2,1)}, u32[]{:S(2)}, u32[]{:S(2)}) collective-permute-start(bf16[8,8,4608]{2,1,0:T(8,128)(2,1)S(1)} %all_to_all.31), channel_id=1, source_target_pairs={{96,0},{40,8},{98,2},{42,10},{100,4},{44,12},{102,6},{46,14},{97,1... | collective-permute-start | bytes 1769480 | tf_op jit(solution)/shard_map/ppermute | solution.py:29
  134.9 9.1 %collective-permute-start.19 = (bf16[8,8,4608]{2,1,0:T(8,128)(2,1)S(1)}, bf16[8,8,4608]{2,1,0:T(8,128)(2,1)}, u32[]{:S(2)}, u32[]{:S(2)}) collective-permute-start(bf16[8,8,4608]{2,1,0:T(8,128)(2,1)S(1)} %all_to_all.31), channel_id=1, source_target_pairs={{17,0},{9,8},{19,2},{11,10},{21,4},{13,12},{23,6},{15,14},{16,1},{... | collective-permute-start | bytes 1769480 | tf_op jit(solution)/shard_map/ppermute | solution.py:29
  134.9 9.1 %collective-permute-start.18 = (bf16[8,8,4608]{2,1,0:T(8,128)(2,1)S(1)}, bf16[8,8,4608]{2,1,0:T(8,128)(2,1)}, u32[]{:S(2)}, u32[]{:S(2)}) collective-permute-start(bf16[8,8,4608]{2,1,0:T(8,128)(2,1)S(1)} %all_to_all.31), channel_id=1, source_target_pairs={{6,0},{10,8},{4,2},{8,10},{2,4},{14,12},{0,6},{12,14},{7,1},{11,9}... | collective-permute-start | bytes 1769480 | tf_op jit(solution)/shard_map/ppermute | solution.py:29
  145.8 7.7 %collective-permute-start.21 = (bf16[32,8,4608]{2,1,0:T(8,128)(2,1)S(1)}, bf16[32,8,4608]{2,1,0:T(8,128)(2,1)S(1)}, u32[]{:S(2)}, u32[]{:S(2)}) collective-permute-start(bf16[32,8,4608]{2,1,0:T(8,128)(2,1)S(1)} %pad_maximum_fusion.5), channel_id=1, source_target_pairs={{0,8},{8,0},{1,9},{9,1},{2,10},{10,2},{3,11},{11,3},{4,12},{12,4},... | collective-permute-start | bytes 7077896 | tf_op jit(solution)/shard_map/ppermute | solution.py:50
  149.3 12.7 %collective-permute-start.25 = (bf16[8,8,4608]{2,1,0:T(8,128)(2,1)}, bf16[8,8,4608]{2,1,0:T(8,128)(2,1)}, u32[]{:S(2)}, u32[]{:S(2)}) collective-permute-start(bf16[8,8,4608]{2,1,0:T(8,128)(2,1)} %collective-permute-done.20), channel_id=1, source_target_pairs={{23,0},{11,8},{21,2},{9,10},{19,4},{15,12},{17,6},{13,14},{22,1},{... | collective-permute-start | bytes 1769480 | tf_op jit(solution)/shard_map/ppermute | solution.py:29
  149.3 15.7 %collective-permute-start.23 = (bf16[8,8,4608]{2,1,0:T(8,128)(2,1)}, bf16[8,8,4608]{2,1,0:T(8,128)(2,1)}, u32[]{:S(2)}, u32[]{:S(2)}) collective-permute-start(bf16[8,8,4608]{2,1,0:T(8,128)(2,1)} %collective-permute-done.20), channel_id=1, source_target_pairs={{17,0},{9,8},{19,2},{11,10},{21,4},{13,12},{23,6},{15,14},{16,1},{... | collective-permute-start | bytes 1769480 | tf_op jit(solution)/shard_map/ppermute | solution.py:29
  149.9 15.4 %collective-permute-start.22 = (bf16[8,8,4608]{2,1,0:T(8,128)(2,1)}, bf16[8,8,4608]{2,1,0:T(8,128)(2,1)}, u32[]{:S(2)}, u32[]{:S(2)}) collective-permute-start(bf16[8,8,4608]{2,1,0:T(8,128)(2,1)} %collective-permute-done.19), channel_id=1, source_target_pairs={{6,0},{10,8},{4,2},{8,10},{2,4},{14,12},{0,6},{12,14},{7,1},{11,9}... | collective-permute-start | bytes 1769480 | tf_op jit(solution)/shard_map/ppermute | solution.py:29
  152.0 13.4 %collective-permute-start.24 = (bf16[8,8,4608]{2,1,0:T(8,128)(2,1)}, bf16[8,8,4608]{2,1,0:T(8,128)(2,1)}, u32[]{:S(2)}, u32[]{:S(2)}) collective-permute-start(bf16[8,8,4608]{2,1,0:T(8,128)(2,1)} %collective-permute-done.18), channel_id=1, source_target_pairs={{96,0},{40,8},{98,2},{42,10},{100,4},{44,12},{102,6},{46,14},{97,1... | collective-permute-start | bytes 1769480 | tf_op jit(solution)/shard_map/ppermute | solution.py:29
  167.2 7.1 %copy-start.5 = (f32[256,512]{1,0:T(8,128)S(1)}, f32[256,512]{1,0:T(8,128)}, u32[]{:S(2)}) copy-start(f32[256,512]{1,0:T(8,128)} %get-tuple-element.96) | copy-start | bytes 1572868
  167.2 8.5 %collective-permute-start.26 = (bf16[32,8,4608]{2,1,0:T(8,128)(2,1)S(1)}, bf16[32,8,4608]{2,1,0:T(8,128)(2,1)S(1)}, u32[]{:S(2)}, u32[]{:S(2)}) collective-permute-start(bf16[32,8,4608]{2,1,0:T(8,128)(2,1)S(1)} %pad_maximum_fusion.6), channel_id=1, source_target_pairs={{0,8},{8,0},{1,9},{9,1},{2,10},{10,2},{3,11},{11,3},{4,12},{12,4},... | collective-permute-start | bytes 7077896 | tf_op jit(solution)/shard_map/ppermute | solution.py:50
  174.3 1.4 copy-start.6
  177.2 1.0 copy-start.2
  177.5 5.1 %slice-start.4 = ((s8[4718592]{0:T(1024)(128)(4,1)}), s8[4194304]{0:T(1024)(128)(4,1)S(1)}, s32[]{:S(2)}) async-start(s8[4718592]{0:T(1024)(128)(4,1)} %bitcast.81), calls=%async_computation.8 | async-start | bytes 8388608
  178.2 4.3 %slice-start.5 = ((s8[4718592]{0:T(1024)(128)(4,1)}), s8[524288]{0:T(1024)(128)(4,1)S(1)}, s32[]{:S(2)}) async-start(s8[4718592]{0:T(1024)(128)(4,1)} %bitcast.81), calls=%async_computation.9 | async-start | bytes 1048576

commit v7 on v4

--- a/solution.py
+++ b/solution.py
@@ -97,16 +97,18 @@
 
     def encode(rows):
         pre_act, = barrier(jnp.dot(rows, enc_weight, preferred_element_type=f32) + enc_bias)
+        code_values = pre_act * jax.nn.sigmoid((pre_act - thresholds) / band_width)
+        return barrier(code_values.astype(bf16), pre_act, jnp.sum(code_values, axis=0))
+
+    def slopes_of(pre_act):
         gating = jax.nn.sigmoid((pre_act - thresholds) / band_width)
-        code_values = pre_act * gating
-        slopes = gating + pre_act * gating * (1.0 - gating) / band_width
-        return barrier(code_values.astype(bf16), slopes, jnp.sum(code_values, axis=0))
+        return gating + pre_act * gating * (1.0 - gating) / band_width
 
     near, encoded, mine, theirs = gather(own_centered, encode)
-    code_near, slopes_near, totals_near = encoded
-    code_mine, slopes_mine, totals_mine = encode(mine)
+    code_near, pre_near, totals_near = encoded
+    code_mine, pre_mine, totals_mine = encode(mine)
     theirs, _ = barrier(theirs, code_mine)
-    code_theirs, slopes_theirs, totals_theirs = encode(theirs)
+    code_theirs, pre_theirs, totals_theirs = encode(theirs)
     totals = totals_near + totals_mine + totals_theirs
 
     def decode(mine, theirs):
@@ -122,24 +124,24 @@
 
     def side_work(received):
         *rest, dec, _ = barrier(
-            near, code_near, mine, theirs, code_mine, code_theirs, slopes_mine, slopes_theirs,
+            near, code_near, mine, theirs, code_mine, code_theirs, pre_near, pre_mine, pre_theirs,
             dec_weight, received,
         )
-        near_rows, code_rows, mine_rows, their_rows, mine_code, their_code, *slopes = rest
+        near_rows, code_rows, mine_rows, their_rows, mine_code, their_code, *pre_acts = rest
         row_norms = jnp.sqrt(jnp.sum(jnp.square(dec.astype(f32)), axis=1) + 1e-06)
         return (
             near_rows.T,
             code_rows.T,
             jnp.concatenate([mine_rows, their_rows]).T,
             jnp.concatenate([mine_code, their_code]).T,
-            *slopes,
+            *(slopes_of(pre_act) for pre_act in pre_acts),
             sparsity_coeff * row_scale * row_norms,
             sparsity_coeff * row_scale * totals / row_norms,
         )
 
     recon, work = scatter(recon_near, recon_distant, side_work)
-    near_t, code_near_t, distant_t, code_distant_t, slopes_mine, slopes_theirs, *norms = work
-    norm_grad, norm_scale = norms
+    near_t, code_near_t, distant_t, code_distant_t, *slopes, norm_grad, norm_scale = work
+    slopes_near, slopes_mine, slopes_theirs = slopes
     recon_error = recon + dec_bias - own_rows
     own_delta, = barrier((recon_error * row_scale).astype(bf16))
 

time: 186 us -> 187 us (level)
  waiting for transfers between devices: 52.8 us -> 47.4 us
  other arithmetic: 14.8 us -> 18.4 us
  matrix products: 33.7 us -> 36.1 us
    ppermute x21, waiting for transfers between devices: 47.5 us -> 44.5 us  [receive(): return lax.ppermute(block, MESH, pairs)]
    reduce_sum x3, other arithmetic: 3.53 us -> 0.67 us  [encode(): jnp.sum(code_values, axis=0)]
    add x0 -> x2, other arithmetic: none -> 2.76 us  [slopes_of(): return gating + pre_act * gating * (1.0 - gating) / band_width]
    ppermute x6, waiting for transfers between devices: 5.38 us -> 2.84 us  [swap(): return lax.ppermute(block, 'core', [(0, 1), (1, 0)])]
    dot_general x3, matrix products: 5.38 us -> 7.83 us  [encode(): jnp.dot(rows, enc_weight, preferred_element_type=f32) + enc_bias]
  transfers between devices with their start and end apart: 27 -> 27, of which waited for: 15 -> 15; matrix products, arithmetic and copies ran while one was open for 16% -> 19% of each run, Pallas kernels for 0% -> 0%
where the time goes in v7:
time: 187 us; the launch traced here: 186 us
  blocking collectives  57.2 us (31%)
  waiting for transfers between devices  47.4 us (25%)
  matrix products  36.1 us (19%)
  starting transfers between devices  25.3 us (14%)
  other arithmetic  18.4 us (10%)
    all_to_all x3, blocking collectives, trade(): return lax.all_to_all(blocks, MESH, 0, 0, axis_index_groups=cubes(pairing))  46.2 us
    ppermute x21, waiting for transfers between devices, receive(): return lax.ppermute(block, MESH, pairs)  44.5 us
    ppermute x6, starting transfers between devices, swap(): return lax.ppermute(block, 'core', [(0, 1), (1, 0)])  14.6 us
    all_to_all x1, blocking collectives, on_device(): lax.all_to_all(activations, ('x', 'yl'), split_axis=0, concat_axis=1, til...  11 us
    ppermute x21, starting transfers between devices, receive(): return lax.ppermute(block, MESH, pairs)  10.7 us
    dot_general x3, matrix products, encode(): jnp.dot(rows, enc_weight, preferred_element_type=f32) + enc_bias  7.83 us
    dot_general x3, matrix products, preact_grad(): lax.dot_general(delta, dec_weight, (((1,), (1,)), ((), ())), preferred_el...  6.68 us
    dot_general x4, matrix products, decode(): jnp.dot(rows, dec_weight, preferred_element_type=f32).astype(bf16)  5.55 us
  transfers between devices with their start and end apart: 27, of which 15 were waited for; matrix products, arithmetic and copies ran while one was open for 19% of the time, Pallas kernels for 0%

profile of v7, /device:TPU:1, one launch (start us, length us, event | category | flops | bytes accessed | tf_op | source)
XLA Modules:
  0.0 186.4 jit_solution(7434216198634909154)
XLA Ops:
  0.6 11.0 %all_to_all.28 = bf16[8,8,576]{2,1,0:T(8,128)(2,1)S(1)} all-to-all(bf16[8,8,576]{2,1,0:T(8,128)(2,1)} %bitcast.78), channel_id=1, replica_groups=mesh['z'=4,'yh'=2,'core'=2,'x'=4,'yl'=2] {'x','yl'}, dimensions={0} | all-to-all | bytes 147456 | tf_op jit(solution)/shard_map/all_to_all | solution.py:94
  12.6 18.5 %all_to_all.29 = bf16[8,8,4608]{2,1,0:T(8,128)(2,1)S(1)} all-to-all(bf16[8,8,4608]{2,1,0:T(8,128)(2,1)S(1)} %broadcast_in_dim.4), channel_id=1, replica_groups={{0,2,1,3,32,34,33,35},{4,6,5,7,36,38,37,39},{16,18,17,19,48,50,49,51},{..., dimensions={0} | all-to-all | bytes 1179648 | tf_op jit(solution)/shard_map/all_to_all | solution.py:46
  31.1 9.0 %collective-permute-done.2 = bf16[8,8,4608]{2,1,0:T(8,128)(2,1)S(1)} collective-permute-done((bf16[8,8,4608]{2,1,0:T(8,128)(2,1)S(1)}, bf16[8,8,4608]{2,1,0:T(8,128)(2,1)S(1)}, u32[]{:S(2)}, u32[]{:S(2)}) %collective-permute-start.2) | collective-permute-done | bytes 589856 | tf_op jit(solution)/shard_map/ppermute | solution.py:29
  40.5 2.4 %collective-permute-start.3 = (bf16[32,8,4608]{2,1,0:T(8,128)(2,1)S(1)}, bf16[32,8,4608]{2,1,0:T(8,128)(2,1)S(1)}, u32[]{:S(2)}, u32[]{:S(2)}) collective-permute-start(bf16[32,8,4608]{2,1,0:T(8,128)(2,1)S(1)} %pad_maximum_fusion.3), channel_id=1, source_target_pairs={{0,8},{8,0},{1,9},{9,1},{2,10},{10,2},{3,11},{11,3},{4,12},{12,4},... | collective-permute-start | bytes 7077896 | tf_op jit(solution)/shard_map/ppermute | solution.py:50
  43.5 2.1 %collective-permute-start.5 = (bf16[8,8,4608]{2,1,0:T(8,128)(2,1)S(1)}, bf16[8,8,4608]{2,1,0:T(8,128)(2,1)S(1)}, u32[]{:S(2)}, u32[]{:S(2)}) collective-permute-start(bf16[8,8,4608]{2,1,0:T(8,128)(2,1)S(1)} %collective-permute-done.1), channel_id=1, source_target_pairs={{6,0},{10,8},{4,2},{8,10},{2,4},{14,12},{0,6},{12,14},{7,1},{11,9}... | collective-permute-start | bytes 1769480 | tf_op jit(solution)/shard_map/ppermute | solution.py:29
  46.1 1.0 collective-permute-done.3
  47.6 2.6 %convolution_add_fusion = f32[512,512]{1,0:T(8,128)S(1)} fusion(bf16[4608,512]{1,0:T(8,128)(2,1)S(1)} %bitcast.80, f32[512]{0:T(512)S(1)} %copy-done.9, bf16[64,8,4608]{2,1,0:T(8,128)(2,1)S(1)} %pad_maximum_fusion), kind=kOutput, calls=%fused_computation.22 | convolution fusion | flops 2416181248 | bytes 10487808 | tf_op jit(solution)/shard_map/dot_general | solution.py:99
  50.5 2.4 %collective-permute-done.8 = bf16[8,8,4608]{2,1,0:T(8,128)(2,1)S(1)} collective-permute-done((bf16[8,8,4608]{2,1,0:T(8,128)(2,1)S(1)}, bf16[8,8,4608]{2,1,0:T(8,128)(2,1)S(1)}, u32[]{:S(2)}, u32[]{:S(2)}) %collective-permute-start.8) | collective-permute-done | bytes 589856 | tf_op jit(solution)/shard_map/ppermute | solution.py:29
  52.9 5.4 %collective-permute-done.6 = bf16[8,8,4608]{2,1,0:T(8,128)(2,1)S(1)} collective-permute-done((bf16[8,8,4608]{2,1,0:T(8,128)(2,1)S(1)}, bf16[8,8,4608]{2,1,0:T(8,128)(2,1)S(1)}, u32[]{:S(2)}, u32[]{:S(2)}) %collective-permute-start.6) | collective-permute-done | bytes 589856 | tf_op jit(solution)/shard_map/ppermute | solution.py:29
  59.0 3.7 %collective-permute-start.9 = (bf16[32,8,4608]{2,1,0:T(8,128)(2,1)S(1)}, bf16[32,8,4608]{2,1,0:T(8,128)(2,1)S(1)}, u32[]{:S(2)}, u32[]{:S(2)}) collective-permute-start(bf16[32,8,4608]{2,1,0:T(8,128)(2,1)S(1)} %pad_maximum_fusion.4), channel_id=1, source_target_pairs={{0,8},{8,0},{1,9},{9,1},{2,10},{10,2},{3,11},{11,3},{4,12},{12,4},... | collective-permute-start | bytes 7077896 | tf_op jit(solution)/shard_map/ppermute | solution.py:50
  62.7 3.9 %convolution_add_fusion.4 = f32[256,512]{1,0:T(8,128)S(1)} fusion(bf16[4608,512]{1,0:T(8,128)(2,1)} %param.7, f32[512]{0:T(512)S(1)} %copy-done.9, bf16[32,8,4608]{2,1,0:T(8,128)(2,1)S(1)} %pad_maximum_fusion.4), kind=kOutput, calls=%fused_computation.29 | convolution fusion | flops 1208090624 | bytes 7604224 | tf_op jit(solution)/shard_map/dot_general | solution.py:99
  66.9 1.4 convolution_add_fusion.3
  68.5 1.4 convolution_convert_fusion.1
  70.3 1.4 convolution_convert_fusion.3
  72.1 1.4 convolution_convert_fusion.2
  73.5 1.4 convolution_convert_fusion.4
  74.9 1.5 fusion.23
  77.0 0.9 collective-permute-done.4
  78.8 2.8 %collective-permute-start.17 = (bf16[8,8,4608]{2,1,0:T(8,128)(2,1)}, bf16[8,8,4608]{2,1,0:T(8,128)(2,1)S(1)}, u32[]{:S(2)}, u32[]{:S(2)}) collective-permute-start(bf16[8,8,4608]{2,1,0:T(8,128)(2,1)} %get-tuple-element.68), channel_id=1, source_target_pairs={{119,0},{43,8},{117,2},{41,10},{115,4},{47,12},{113,6},{45,14},{11... | collective-permute-start | bytes 1769480 | tf_op jit(solution)/shard_map/ppermute | solution.py:29
  81.6 3.8 %collective-permute-done.11 = bf16[8,8,4608]{2,1,0:T(8,128)(2,1)S(1)} collective-permute-done((bf16[8,8,4608]{2,1,0:T(8,128)(2,1)S(1)}, bf16[8,8,4608]{2,1,0:T(8,128)(2,1)S(1)}, u32[]{:S(2)}, u32[]{:S(2)}) %collective-permute-start.11) | collective-permute-done | bytes 589856 | tf_op jit(solution)/shard_map/ppermute | solution.py:29
  85.4 0.9 add_convert_fusion.6
  86.4 1.3 collective-permute-done.13
  87.7 1.0 add_convert_fusion.5
  88.7 1.0 multiply_reduce_fusion
  89.7 4.4 %collective-permute-done.15 = bf16[8,8,4608]{2,1,0:T(8,128)(2,1)S(1)} collective-permute-done((bf16[8,8,4608]{2,1,0:T(8,128)(2,1)S(1)}, bf16[8,8,4608]{2,1,0:T(8,128)(2,1)S(1)}, u32[]{:S(2)}, u32[]{:S(2)}) %collective-permute-start.15) | collective-permute-done | bytes 589856 | tf_op jit(solution)/shard_map/ppermute | solution.py:29
  94.1 1.0 add_convert_fusion.4
  95.7 1.4 multiply_add_fusion
  97.1 0.8 maximum_bitcast_fusion.1
  97.9 1.4 multiply_add_fusion.1
  100.5 4.0 %collective-permute-done.16 = bf16[8,8,4608]{2,1,0:T(8,128)(2,1)} collective-permute-done((bf16[8,8,4608]{2,1,0:T(8,128)(2,1)}, bf16[8,8,4608]{2,1,0:T(8,128)(2,1)}, u32[]{:S(2)}, u32[]{:S(2)}) %collective-permute-start.16) | collective-permute-done | bytes 589856 | tf_op jit(solution)/shard_map/ppermute | solution.py:29
  104.5 1.5 add_convert_fusion.3
  105.9 14.1 %all_to_all.30 = bf16[8,8,4608]{2,1,0:T(8,128)(2,1)S(1)} all-to-all(bf16[8,8,4608]{2,1,0:T(8,128)(2,1)S(1)} %add_convert_fusion.3), channel_id=1, replica_groups={{0,2,1,3,32,34,33,35},{4,6,5,7,36,38,37,39},{16,18,17,19,48,50,49,51},{..., dimensions={0} | all-to-all | bytes 1179648 | tf_op jit(solution)/shard_map/all_to_all | solution.py:46
  120.2 13.6 %all_to_all.31 = bf16[8,8,4608]{2,1,0:T(8,128)(2,1)S(1)} all-to-all(bf16[8,8,4608]{2,1,0:T(8,128)(2,1)S(1)} %broadcast_in_dim.5), channel_id=1, replica_groups={{0,2,1,3,32,34,33,35},{4,6,5,7,36,38,37,39},{16,18,17,19,48,50,49,51},{..., dimensions={0} | all-to-all | bytes 1179648 | tf_op jit(solution)/shard_map/all_to_all | solution.py:46
  133.8 9.1 %collective-permute-done.20 = bf16[8,8,4608]{2,1,0:T(8,128)(2,1)} collective-permute-done((bf16[8,8,4608]{2,1,0:T(8,128)(2,1)S(1)}, bf16[8,8,4608]{2,1,0:T(8,128)(2,1)}, u32[]{:S(2)}, u32[]{:S(2)}) %collective-permute-start.20) | collective-permute-done | bytes 589856 | tf_op jit(solution)/shard_map/ppermute | solution.py:29
  143.0 1.7 pad_maximum_fusion.5
  144.7 3.6 %collective-permute-start.21 = (bf16[32,8,4608]{2,1,0:T(8,128)(2,1)S(1)}, bf16[32,8,4608]{2,1,0:T(8,128)(2,1)S(1)}, u32[]{:S(2)}, u32[]{:S(2)}) collective-permute-start(bf16[32,8,4608]{2,1,0:T(8,128)(2,1)S(1)} %pad_maximum_fusion.5), channel_id=1, source_target_pairs={{0,8},{8,0},{1,9},{9,1},{2,10},{10,2},{3,11},{11,3},{4,12},{12,4},... | collective-permute-start | bytes 7077896 | tf_op jit(solution)/shard_map/ppermute | solution.py:50
  148.3 1.6 collective-permute-start.25
  151.6 0.8 collective-permute-done.21
  152.9 3.9 %fusion.9 = bf16[512,512]{1,0:T(8,128)(2,1)S(1)} fusion(f32[512,512]{1,0:T(8,128)} %multiply_add_fusion, bf16[512,4608]{1,0:T(8,128)(2,1)S(1)} %bitcast.69, bf16[64,8,4608]{2,1,0:T(8,128)(2,1)S(1)} %pad_maximum_fusion.1, f32[512]{0:T(512)S(1)} %get-tuple-element.89), kind=kOutput, calls=%fused_computation.23 | convolution fusion | flops 2416705536 | bytes 11012096 | tf_op jit(solution)/shard_map/dot_general | solution.py:149
  156.7 4.3 %convolution_convert_fusion = bf16[4608,512]{1,0:T(8,128)(2,1)} fusion(bf16[4608,512]{0,1:T(8,128)(2,1)S(1)} %bitcast.72, bf16[512,512]{1,0:T(8,128)(2,1)S(1)} %fusion.9), kind=kOutput, calls=%fused_computation.4 | convolution fusion | flops 2418278400 | bytes 9961472 | tf_op jit(solution)/shard_map/dot_general | solution.py:158
  161.0 3.8 %collective-permute-done.23 = bf16[8,8,4608]{2,1,0:T(8,128)(2,1)} collective-permute-done((bf16[8,8,4608]{2,1,0:T(8,128)(2,1)}, bf16[8,8,4608]{2,1,0:T(8,128)(2,1)}, u32[]{:S(2)}, u32[]{:S(2)}) %collective-permute-start.23) | collective-permute-done | bytes 589856 | tf_op jit(solution)/shard_map/ppermute | solution.py:29
  164.9 1.9 %pad_maximum_fusion.6 = bf16[32,8,4608]{2,1,0:T(8,128)(2,1)S(1)} fusion(bf16[8,8,4608]{2,1,0:T(8,128)(2,1)} %collective-permute-done.25, bf16[8,8,4608]{2,1,0:T(8,128)(2,1)} %collective-permute-done.24, bf16[8,8,4608]{2,1,0:T(8,128)(2,1)} %collective-permute-done.23, bf16[8,8,4608]{2,1,0:T(8,128)(2,1)} %collective-permute-done.22), kind=kLoop, calls=%fused_computation.19 | loop fusion | flops 3538944 | bytes 4718592 | tf_op jit(solution)/shard_map/concatenate | solution.py:76
  166.8 4.0 %collective-permute-start.26 = (bf16[32,8,4608]{2,1,0:T(8,128)(2,1)S(1)}, bf16[32,8,4608]{2,1,0:T(8,128)(2,1)S(1)}, u32[]{:S(2)}, u32[]{:S(2)}) collective-permute-start(bf16[32,8,4608]{2,1,0:T(8,128)(2,1)S(1)} %pad_maximum_fusion.6), channel_id=1, source_target_pairs={{0,8},{8,0},{1,9},{9,1},{2,10},{10,2},{3,11},{11,3},{4,12},{12,4},... | collective-permute-start | bytes 7077896 | tf_op jit(solution)/shard_map/ppermute | solution.py:50
  170.7 3.1 %add_convert_fusion.2 = bf16[512,4608]{1,0:T(8,128)(2,1)S(1)} fusion(bf16[512,4608]{1,0:T(8,128)(2,1)S(1)} %bitcast.69, bf16[512,512]{0,1:T(8,128)(2,1)S(1)} %bitcast.77, bf16[64,8,4608]{2,1,0:T(8,128)(2,1)S(1)} %pad_maximum_fusion.1, f32[512]{0:T(512)S(1)} %get-tuple-element.98), kind=kOutput, calls=%fused_computation.2 | convolution fusion | flops 2425356288 | bytes 14682112 | tf_op jit(solution)/shard_map/dot_general | solution.py:161
  173.8 1.4 fusion.14
  175.3 1.4 fusion.15
  177.7 4.3 %add_convert_fusion = bf16[512,4608]{1,0:T(8,128)(2,1)} fusion(bf16[512,4608]{1,0:T(8,128)(2,1)S(1)} %add_convert_fusion.2, bf16[512,512]{0,1:T(8,128)(2,1)S(1)} %copy-done.2, bf16[512,4608]{1,0:T(8,128)(2,1)S(1)} %pad_maximum_fusion.2), kind=kOutput, calls=%fused_computation | convolution fusion | flops 2422996992 | bytes 14680064 | tf_op jit(solution)/shard_map/dot_general | solution.py:169
  182.1 4.4 %add_convert_fusion.1 = bf16[4608,512]{1,0:T(8,128)(2,1)} fusion(bf16[4608,512]{1,0:T(8,128)(2,1)S(1)} %bitcast.84, bf16[4608,512]{0,1:T(8,128)(2,1)S(1)} %maximum_bitcast_fusion, bf16[512,512]{1,0:T(8,128)(2,1)S(1)} %pad_maximum_fusion.7), kind=kOutput, calls=%fused_computation.1 | convolution fusion | flops 2422996992 | bytes 14680064 | tf_op jit(solution)/shard_map/dot_general | solution.py:168
  (95 shorter events, 11.6 us)
Async XLA Ops:
  11.8 28.7 %copy-start.3 = (f32[8,4608]{1,0:T(8,128)}, f32[8,4608]{1,0:T(8,128)S(1)}, u32[]{:S(2)}) copy-start(f32[8,4608]{1,0:T(8,128)S(1)} %reshape.90) | copy-start | bytes 442372
  31.1 9.0 %collective-permute-start.2 = (bf16[8,8,4608]{2,1,0:T(8,128)(2,1)S(1)}, bf16[8,8,4608]{2,1,0:T(8,128)(2,1)S(1)}, u32[]{:S(2)}, u32[]{:S(2)}) collective-permute-start(bf16[8,8,4608]{2,1,0:T(8,128)(2,1)S(1)} %all_to_all.29), channel_id=1, source_target_pairs={{96,0},{40,8},{98,2},{42,10},{100,4},{44,12},{102,6},{46,14},{97,1... | collective-permute-start | bytes 1769480 | tf_op jit(solution)/shard_map/ppermute | solution.py:29
  31.1 9.0 %collective-permute-start.1 = (bf16[8,8,4608]{2,1,0:T(8,128)(2,1)S(1)}, bf16[8,8,4608]{2,1,0:T(8,128)(2,1)S(1)}, u32[]{:S(2)}, u32[]{:S(2)}) collective-permute-start(bf16[8,8,4608]{2,1,0:T(8,128)(2,1)S(1)} %all_to_all.29), channel_id=1, source_target_pairs={{17,0},{9,8},{19,2},{11,10},{21,4},{13,12},{23,6},{15,14},{16,1},{... | collective-permute-start | bytes 1769480 | tf_op jit(solution)/shard_map/ppermute | solution.py:29
  31.1 9.0 %collective-permute-start = (bf16[8,8,4608]{2,1,0:T(8,128)(2,1)S(1)}, bf16[8,8,4608]{2,1,0:T(8,128)(2,1)S(1)}, u32[]{:S(2)}, u32[]{:S(2)}) collective-permute-start(bf16[8,8,4608]{2,1,0:T(8,128)(2,1)S(1)} %all_to_all.29), channel_id=1, source_target_pairs={{6,0},{10,8},{4,2},{8,10},{2,4},{14,12},{0,6},{12,14},{7,1},{11,9}... | collective-permute-start | bytes 1769480 | tf_op jit(solution)/shard_map/ppermute | solution.py:29
  40.2 7.4 %slice-start.2 = ((s8[4718592]{0:T(1024)(128)(4,1)}), s8[4194304]{0:T(1024)(128)(4,1)S(1)}, s32[]{:S(2)}) async-start(s8[4718592]{0:T(1024)(128)(4,1)} %bitcast.79), calls=%async_computation.6 | async-start | bytes 8388608
  40.5 7.1 %slice-start.3 = ((s8[4718592]{0:T(1024)(128)(4,1)}), s8[524288]{0:T(1024)(128)(4,1)S(1)}, s32[]{:S(2)}) async-start(s8[4718592]{0:T(1024)(128)(4,1)} %bitcast.79), calls=%async_computation.7 | async-start | bytes 1048576
  40.5 7.1 %copy-start.9 = (f32[512]{0:T(512)S(1)}, f32[512]{0:T(512)}, u32[]{:S(2)}) copy-start(f32[512]{0:T(512)} %param.8) | copy-start | bytes 6148
  40.5 6.6 %collective-permute-start.3 = (bf16[32,8,4608]{2,1,0:T(8,128)(2,1)S(1)}, bf16[32,8,4608]{2,1,0:T(8,128)(2,1)S(1)}, u32[]{:S(2)}, u32[]{:S(2)}) collective-permute-start(bf16[32,8,4608]{2,1,0:T(8,128)(2,1)S(1)} %pad_maximum_fusion.3), channel_id=1, source_target_pairs={{0,8},{8,0},{1,9},{9,1},{2,10},{10,2},{3,11},{11,3},{4,12},{12,4},... | collective-permute-start | bytes 7077896 | tf_op jit(solution)/shard_map/ppermute | solution.py:50
  43.0 10.0 %collective-permute-start.8 = (bf16[8,8,4608]{2,1,0:T(8,128)(2,1)S(1)}, bf16[8,8,4608]{2,1,0:T(8,128)(2,1)S(1)}, u32[]{:S(2)}, u32[]{:S(2)}) collective-permute-start(bf16[8,8,4608]{2,1,0:T(8,128)(2,1)S(1)} %collective-permute-done.2), channel_id=1, source_target_pairs={{23,0},{11,8},{21,2},{9,10},{19,4},{15,12},{17,6},{13,14},{22,1},{... | collective-permute-start | bytes 1769480 | tf_op jit(solution)/shard_map/ppermute | solution.py:29
  43.0 15.3 %collective-permute-start.6 = (bf16[8,8,4608]{2,1,0:T(8,128)(2,1)S(1)}, bf16[8,8,4608]{2,1,0:T(8,128)(2,1)S(1)}, u32[]{:S(2)}, u32[]{:S(2)}) collective-permute-start(bf16[8,8,4608]{2,1,0:T(8,128)(2,1)S(1)} %collective-permute-done.2), channel_id=1, source_target_pairs={{17,0},{9,8},{19,2},{11,10},{21,4},{13,12},{23,6},{15,14},{16,1},{... | collective-permute-start | bytes 1769480 | tf_op jit(solution)/shard_map/ppermute | solution.py:29
  43.5 15.1 %collective-permute-start.5 = (bf16[8,8,4608]{2,1,0:T(8,128)(2,1)S(1)}, bf16[8,8,4608]{2,1,0:T(8,128)(2,1)S(1)}, u32[]{:S(2)}, u32[]{:S(2)}) collective-permute-start(bf16[8,8,4608]{2,1,0:T(8,128)(2,1)S(1)} %collective-permute-done.1), channel_id=1, source_target_pairs={{6,0},{10,8},{4,2},{8,10},{2,4},{14,12},{0,6},{12,14},{7,1},{11,9}... | collective-permute-start | bytes 1769480 | tf_op jit(solution)/shard_map/ppermute | solution.py:29
  45.6 13.0 %collective-permute-start.7 = (bf16[8,8,4608]{2,1,0:T(8,128)(2,1)S(1)}, bf16[8,8,4608]{2,1,0:T(8,128)(2,1)S(1)}, u32[]{:S(2)}, u32[]{:S(2)}) collective-permute-start(bf16[8,8,4608]{2,1,0:T(8,128)(2,1)S(1)} %collective-permute-done), channel_id=1, source_target_pairs={{96,0},{40,8},{98,2},{42,10},{100,4},{44,12},{102,6},{46,14},{97,1... | collective-permute-start | bytes 1769480 | tf_op jit(solution)/shard_map/ppermute | solution.py:29
  47.6 2.6 %copy-start.8 = (f32[512]{0:T(512)S(1)}, f32[512]{0:T(512)}, u32[]{:S(2)}) copy-start(f32[512]{0:T(512)} %param.9) | copy-start | bytes 6148
  58.7 8.2 %slice-start.4 = ((s8[4718592]{0:T(1024)(128)(4,1)}), s8[524288]{0:T(1024)(128)(4,1)S(1)}, s32[]{:S(2)}) async-start(s8[4718592]{0:T(1024)(128)(4,1)} %bitcast.81), calls=%async_computation.8 | async-start | bytes 1048576
  59.0 7.9 %slice-start.5 = ((s8[4718592]{0:T(1024)(128)(4,1)}), s8[4194304]{0:T(1024)(128)(4,1)S(1)}, s32[]{:S(2)}) async-start(s8[4718592]{0:T(1024)(128)(4,1)} %bitcast.81), calls=%async_computation.9 | async-start | bytes 8388608
  59.0 7.9 %collective-permute-start.9 = (bf16[32,8,4608]{2,1,0:T(8,128)(2,1)S(1)}, bf16[32,8,4608]{2,1,0:T(8,128)(2,1)S(1)}, u32[]{:S(2)}, u32[]{:S(2)}) collective-permute-start(bf16[32,8,4608]{2,1,0:T(8,128)(2,1)S(1)} %pad_maximum_fusion.4), channel_id=1, source_target_pairs={{0,8},{8,0},{1,9},{9,1},{2,10},{10,2},{3,11},{11,3},{4,12},{12,4},... | collective-permute-start | bytes 7077896 | tf_op jit(solution)/shard_map/ppermute | solution.py:50
  62.7 5.7 %slice-start = ((s8[4718592]{0:T(1024)(128)(4,1)}), s8[4194304]{0:T(1024)(128)(4,1)S(1)}, s32[]{:S(2)}) async-start(s8[4718592]{0:T(1024)(128)(4,1)} %bitcast.68), calls=%async_computation.4 | async-start | bytes 8388608
  66.8 1.7 slice-start.1
  66.9 1.4 copy-start
  69.9 5.0 %collective-permute-start.10 = (bf16[256,4608]{1,0:T(8,128)(2,1)S(1)}, bf16[256,4608]{1,0:T(8,128)(2,1)S(1)}, u32[]{:S(2)}, u32[]{:S(2)}) collective-permute-start(bf16[256,4608]{1,0:T(8,128)(2,1)S(1)} %convolution_convert_fusion.1), channel_id=1, source_target_pairs={{0,8},{8,0},{1,9},{9,1},{2,10},{10,2},{3,11},{11,3},{4,12},{12,4},... | collective-permute-start | bytes 7077896 | tf_op jit(solution)/shard_map/ppermute | solution.py:50
  71.7 6.1 %collective-permute-start.4 = (bf16[256,4608]{1,0:T(8,128)(2,1)S(1)}, bf16[256,4608]{1,0:T(8,128)(2,1)S(1)}, u32[]{:S(2)}, u32[]{:S(2)}) collective-permute-start(bf16[256,4608]{1,0:T(8,128)(2,1)S(1)} %convolution_convert_fusion.3), channel_id=1, source_target_pairs={{0,8},{8,0},{1,9},{9,1},{2,10},{10,2},{3,11},{11,3},{4,12},{12,4},... | collective-permute-start | bytes 7077896 | tf_op jit(solution)/shard_map/ppermute | solution.py:50
  76.4 9.0 %collective-permute-start.11 = (bf16[8,8,4608]{2,1,0:T(8,128)(2,1)S(1)}, bf16[8,8,4608]{2,1,0:T(8,128)(2,1)S(1)}, u32[]{:S(2)}, u32[]{:S(2)}) collective-permute-start(bf16[8,8,4608]{2,1,0:T(8,128)(2,1)S(1)} %get-tuple-element.63), channel_id=1, source_target_pairs={{96,0},{40,8},{98,2},{42,10},{100,4},{44,12},{102,6},{46,14},{97,1... | collective-permute-start | bytes 1769480 | tf_op jit(solution)/shard_map/ppermute | solution.py:29
  78.6 9.1 %collective-permute-start.13 = (bf16[8,8,4608]{2,1,0:T(8,128)(2,1)S(1)}, bf16[8,8,4608]{2,1,0:T(8,128)(2,1)S(1)}, u32[]{:S(2)}, u32[]{:S(2)}) collective-permute-start(bf16[8,8,4608]{2,1,0:T(8,128)(2,1)S(1)} %get-tuple-element.65), channel_id=1, source_target_pairs={{6,0},{10,8},{4,2},{8,10},{2,4},{14,12},{0,6},{12,14},{7,1},{11,9}... | collective-permute-start | bytes 1769480 | tf_op jit(solution)/shard_map/ppermute | solution.py:29
  78.7 15.4 %collective-permute-start.15 = (bf16[8,8,4608]{2,1,0:T(8,128)(2,1)S(1)}, bf16[8,8,4608]{2,1,0:T(8,128)(2,1)S(1)}, u32[]{:S(2)}, u32[]{:S(2)}) collective-permute-start(bf16[8,8,4608]{2,1,0:T(8,128)(2,1)S(1)} %get-tuple-element.67), channel_id=1, source_target_pairs={{17,0},{9,8},{19,2},{11,10},{21,4},{13,12},{23,6},{15,14},{16,1},{... | collective-permute-start | bytes 1769480 | tf_op jit(solution)/shard_map/ppermute | solution.py:29
  78.8 20.8 %collective-permute-start.17 = (bf16[8,8,4608]{2,1,0:T(8,128)(2,1)}, bf16[8,8,4608]{2,1,0:T(8,128)(2,1)S(1)}, u32[]{:S(2)}, u32[]{:S(2)}) collective-permute-start(bf16[8,8,4608]{2,1,0:T(8,128)(2,1)} %get-tuple-element.68), channel_id=1, source_target_pairs={{119,0},{43,8},{117,2},{41,10},{115,4},{47,12},{113,6},{45,14},{11... | collective-permute-start | bytes 1769480 | tf_op jit(solution)/shard_map/ppermute | solution.py:29
  86.4 14.0 %collective-permute-start.12 = (bf16[8,8,4608]{2,1,0:T(8,128)(2,1)}, bf16[8,8,4608]{2,1,0:T(8,128)(2,1)S(1)}, u32[]{:S(2)}, u32[]{:S(2)}) collective-permute-start(bf16[8,8,4608]{2,1,0:T(8,128)(2,1)} %add_convert_fusion.6), channel_id=1, source_target_pairs={{6,0},{10,8},{4,2},{8,10},{2,4},{14,12},{0,6},{12,14},{7,1},{11,9}... | collective-permute-start | bytes 1769480 | tf_op jit(solution)/shard_map/ppermute | solution.py:29
  88.7 11.8 %collective-permute-start.14 = (bf16[8,8,4608]{2,1,0:T(8,128)(2,1)}, bf16[8,8,4608]{2,1,0:T(8,128)(2,1)S(1)}, u32[]{:S(2)}, u32[]{:S(2)}) collective-permute-start(bf16[8,8,4608]{2,1,0:T(8,128)(2,1)} %add_convert_fusion.5), channel_id=1, source_target_pairs={{17,0},{9,8},{19,2},{11,10},{21,4},{13,12},{23,6},{15,14},{16,1},{... | collective-permute-start | bytes 1769480 | tf_op jit(solution)/shard_map/ppermute | solution.py:29
  95.1 4.2 %copy-start.1 = (bf16[32,8,4608]{2,1,0:T(8,128)(2,1)S(1)}, bf16[32,8,4608]{2,1,0:T(8,128)(2,1)}, u32[]{:S(2)}) copy-start(bf16[32,8,4608]{2,1,0:T(8,128)(2,1)} %copy-done) | copy-start | bytes 7077892
  95.1 9.3 %collective-permute-start.16 = (bf16[8,8,4608]{2,1,0:T(8,128)(2,1)}, bf16[8,8,4608]{2,1,0:T(8,128)(2,1)}, u32[]{:S(2)}, u32[]{:S(2)}) collective-permute-start(bf16[8,8,4608]{2,1,0:T(8,128)(2,1)} %add_convert_fusion.4), channel_id=1, source_target_pairs={{96,0},{40,8},{98,2},{42,10},{100,4},{44,12},{102,6},{46,14},{97,1... | collective-permute-start | bytes 1769480 | tf_op jit(solution)/shard_map/ppermute | solution.py:29
  104.5 15.7 %copy-start.4 = (f32[8,4608]{1,0:T(8,128)S(1)}, f32[8,4608]{1,0:T(8,128)}, u32[]{:S(2)}) copy-start(f32[8,4608]{1,0:T(8,128)} %copy-done.3) | copy-start | bytes 442372
  104.5 15.7 %copy-start.7 = (f32[4608]{0:T(1024)S(1)}, f32[4608]{0:T(1024)}, u32[]{:S(2)}) copy-start(f32[4608]{0:T(1024)} %param.11) | copy-start | bytes 55300
  133.8 9.1 %collective-permute-start.20 = (bf16[8,8,4608]{2,1,0:T(8,128)(2,1)S(1)}, bf16[8,8,4608]{2,1,0:T(8,128)(2,1)}, u32[]{:S(2)}, u32[]{:S(2)}) collective-permute-start(bf16[8,8,4608]{2,1,0:T(8,128)(2,1)S(1)} %all_to_all.31), channel_id=1, source_target_pairs={{96,0},{40,8},{98,2},{42,10},{100,4},{44,12},{102,6},{46,14},{97,1... | collective-permute-start | bytes 1769480 | tf_op jit(solution)/shard_map/ppermute | solution.py:29
  133.8 9.1 %collective-permute-start.19 = (bf16[8,8,4608]{2,1,0:T(8,128)(2,1)S(1)}, bf16[8,8,4608]{2,1,0:T(8,128)(2,1)}, u32[]{:S(2)}, u32[]{:S(2)}) collective-permute-start(bf16[8,8,4608]{2,1,0:T(8,128)(2,1)S(1)} %all_to_all.31), channel_id=1, source_target_pairs={{17,0},{9,8},{19,2},{11,10},{21,4},{13,12},{23,6},{15,14},{16,1},{... | collective-permute-start | bytes 1769480 | tf_op jit(solution)/shard_map/ppermute | solution.py:29
  133.8 9.1 %collective-permute-start.18 = (bf16[8,8,4608]{2,1,0:T(8,128)(2,1)S(1)}, bf16[8,8,4608]{2,1,0:T(8,128)(2,1)}, u32[]{:S(2)}, u32[]{:S(2)}) collective-permute-start(bf16[8,8,4608]{2,1,0:T(8,128)(2,1)S(1)} %all_to_all.31), channel_id=1, source_target_pairs={{6,0},{10,8},{4,2},{8,10},{2,4},{14,12},{0,6},{12,14},{7,1},{11,9}... | collective-permute-start | bytes 1769480 | tf_op jit(solution)/shard_map/ppermute | solution.py:29
  144.7 7.8 %collective-permute-start.21 = (bf16[32,8,4608]{2,1,0:T(8,128)(2,1)S(1)}, bf16[32,8,4608]{2,1,0:T(8,128)(2,1)S(1)}, u32[]{:S(2)}, u32[]{:S(2)}) collective-permute-start(bf16[32,8,4608]{2,1,0:T(8,128)(2,1)S(1)} %pad_maximum_fusion.5), channel_id=1, source_target_pairs={{0,8},{8,0},{1,9},{9,1},{2,10},{10,2},{3,11},{11,3},{4,12},{12,4},... | collective-permute-start | bytes 7077896 | tf_op jit(solution)/shard_map/ppermute | solution.py:50
  148.3 12.7 %collective-permute-start.25 = (bf16[8,8,4608]{2,1,0:T(8,128)(2,1)}, bf16[8,8,4608]{2,1,0:T(8,128)(2,1)}, u32[]{:S(2)}, u32[]{:S(2)}) collective-permute-start(bf16[8,8,4608]{2,1,0:T(8,128)(2,1)} %collective-permute-done.20), channel_id=1, source_target_pairs={{23,0},{11,8},{21,2},{9,10},{19,4},{15,12},{17,6},{13,14},{22,1},{... | collective-permute-start | bytes 1769480 | tf_op jit(solution)/shard_map/ppermute | solution.py:29
  149.9 15.0 %collective-permute-start.23 = (bf16[8,8,4608]{2,1,0:T(8,128)(2,1)}, bf16[8,8,4608]{2,1,0:T(8,128)(2,1)}, u32[]{:S(2)}, u32[]{:S(2)}) collective-permute-start(bf16[8,8,4608]{2,1,0:T(8,128)(2,1)} %collective-permute-done.20), channel_id=1, source_target_pairs={{17,0},{9,8},{19,2},{11,10},{21,4},{13,12},{23,6},{15,14},{16,1},{... | collective-permute-start | bytes 1769480 | tf_op jit(solution)/shard_map/ppermute | solution.py:29
  150.4 14.4 %collective-permute-start.22 = (bf16[8,8,4608]{2,1,0:T(8,128)(2,1)}, bf16[8,8,4608]{2,1,0:T(8,128)(2,1)}, u32[]{:S(2)}, u32[]{:S(2)}) collective-permute-start(bf16[8,8,4608]{2,1,0:T(8,128)(2,1)} %collective-permute-done.19), channel_id=1, source_target_pairs={{6,0},{10,8},{4,2},{8,10},{2,4},{14,12},{0,6},{12,14},{7,1},{11,9}... | collective-permute-start | bytes 1769480 | tf_op jit(solution)/shard_map/ppermute | solution.py:29
  150.9 13.9 %collective-permute-start.24 = (bf16[8,8,4608]{2,1,0:T(8,128)(2,1)}, bf16[8,8,4608]{2,1,0:T(8,128)(2,1)}, u32[]{:S(2)}, u32[]{:S(2)}) collective-permute-start(bf16[8,8,4608]{2,1,0:T(8,128)(2,1)} %collective-permute-done.18), channel_id=1, source_target_pairs={{96,0},{40,8},{98,2},{42,10},{100,4},{44,12},{102,6},{46,14},{97,1... | collective-permute-start | bytes 1769480 | tf_op jit(solution)/shard_map/ppermute | solution.py:29
  166.8 7.1 %copy-start.6 = (f32[256,512]{1,0:T(8,128)S(1)}, f32[256,512]{1,0:T(8,128)}, u32[]{:S(2)}) copy-start(f32[256,512]{1,0:T(8,128)} %get-tuple-element.96) | copy-start | bytes 1572868
  166.8 8.5 %collective-permute-start.26 = (bf16[32,8,4608]{2,1,0:T(8,128)(2,1)S(1)}, bf16[32,8,4608]{2,1,0:T(8,128)(2,1)S(1)}, u32[]{:S(2)}, u32[]{:S(2)}) collective-permute-start(bf16[32,8,4608]{2,1,0:T(8,128)(2,1)S(1)} %pad_maximum_fusion.6), channel_id=1, source_target_pairs={{0,8},{8,0},{1,9},{9,1},{2,10},{10,2},{3,11},{11,3},{4,12},{12,4},... | collective-permute-start | bytes 7077896 | tf_op jit(solution)/shard_map/ppermute | solution.py:50
  173.8 1.4 copy-start.5
  176.7 1.0 copy-start.2
  177.0 5.1 %slice-start.6 = ((s8[4718592]{0:T(1024)(128)(4,1)}), s8[4194304]{0:T(1024)(128)(4,1)S(1)}, s32[]{:S(2)}) async-start(s8[4718592]{0:T(1024)(128)(4,1)} %bitcast.83), calls=%async_computation.10 | async-start | bytes 8388608
  177.7 4.3 %slice-start.7 = ((s8[4718592]{0:T(1024)(128)(4,1)}), s8[524288]{0:T(1024)(128)(4,1)S(1)}, s32[]{:S(2)}) async-start(s8[4718592]{0:T(1024)(128)(4,1)} %bitcast.83), calls=%async_computation.11 | async-start | bytes 1048576

commit v8 on v4

--- a/solution.py
+++ b/solution.py
@@ -109,16 +109,24 @@
     code_theirs, slopes_theirs, totals_theirs = encode(theirs)
     totals = totals_near + totals_mine + totals_theirs
 
-    def decode(mine, theirs):
+    def decode(mine, theirs, parts):
         theirs, mine = (
             barrier(jnp.dot(rows, dec_weight, preferred_element_type=f32).astype(bf16))[0]
             for rows in (theirs, mine)
         )
-        pairs = zip(*(jnp.split(rows.reshape(32, 8, -1), 4) for rows in (mine, swap(theirs))))
-        return barrier(*(add(*pair).astype(bf16) for pair in pairs))
+        blocks = ()
+        for part, other in zip(jnp.split(mine, parts), jnp.split(theirs, parts)):
+            pairs = zip(
+                *(jnp.split(rows.reshape(-1, 8, rows.shape[1]), 4 // parts) for rows in (part, swap(other)))
+            )
+            sums = tuple(add(*pair).astype(bf16) for pair in pairs)
+            if blocks:
+                *sums, _ = barrier(*sums, blocks)
+            blocks += barrier(*sums) if len(blocks) == 0 else tuple(sums)
+        return blocks
 
-    recon_near = decode(code_near[:256], code_near[256:])
-    recon_distant = decode(code_mine, code_theirs)
+    recon_near = decode(code_near[:256], code_near[256:], 1)
+    recon_distant = decode(code_mine, code_theirs, 2)
 
     def side_work(received):
         *rest, dec, _ = barrier(

time: 186 us -> 187 us (level)
    ppermute x6 -> x7, starting transfers between devices: 13.8 us -> 15 us  [swap(): return lax.ppermute(block, 'core', [(0, 1), (1, 0)])]
    ppermute x6 -> x7, waiting for transfers between devices: 5.38 us -> 4.16 us  [swap(): return lax.ppermute(block, 'core', [(0, 1), (1, 0)])]
  transfers between devices with their start and end apart: 27 -> 28, of which waited for: 15 -> 15; matrix products, arithmetic and copies ran while one was open for 16% -> 16% of each run, Pallas kernels for 0% -> 0%
where the time goes in v8:
time: 187 us; the launch traced here: 186 us
  blocking collectives  57.2 us (31%)
  waiting for transfers between devices  51.7 us (28%)
  matrix products  33.7 us (18%)
  starting transfers between devices  25.8 us (14%)
  other arithmetic  15.5 us (8%)
    ppermute x21, waiting for transfers between devices, receive(): return lax.ppermute(block, MESH, pairs)  47.5 us
    all_to_all x3, blocking collectives, trade(): return lax.all_to_all(blocks, MESH, 0, 0, axis_index_groups=cubes(pairing))  46.2 us
    ppermute x7, starting transfers between devices, swap(): return lax.ppermute(block, 'core', [(0, 1), (1, 0)])  15 us
    all_to_all x1, blocking collectives, on_device(): lax.all_to_all(activations, ('x', 'yl'), split_axis=0, concat_axis=1, til...  11 us
    ppermute x21, starting transfers between devices, receive(): return lax.ppermute(block, MESH, pairs)  10.8 us
    dot_general x3, matrix products, preact_grad(): lax.dot_general(delta, dec_weight, (((1,), (1,)), ((), ())), preferred_el...  6.68 us
    dot_general x4, matrix products, decode(): jnp.dot(rows, dec_weight, preferred_element_type=f32).astype(bf16)  5.55 us
    dot_general x3, matrix products, encode(): jnp.dot(rows, enc_weight, preferred_element_type=f32) + enc_bias  5.35 us
  transfers between devices with their start and end apart: 28, of which 15 were waited for; matrix products, arithmetic and copies ran while one was open for 16% of the time, Pallas kernels for 0%

profile of v8, /device:TPU:1, one launch (start us, length us, event | category | flops | bytes accessed | tf_op | source)
XLA Modules:
  0.0 186.1 jit_solution(11593756245009755846)
XLA Ops:
  0.6 11.0 %all_to_all.28 = bf16[8,8,576]{2,1,0:T(8,128)(2,1)S(1)} all-to-all(bf16[8,8,576]{2,1,0:T(8,128)(2,1)} %bitcast.78), channel_id=1, replica_groups=mesh['z'=4,'yh'=2,'core'=2,'x'=4,'yl'=2] {'x','yl'}, dimensions={0} | all-to-all | bytes 147456 | tf_op jit(solution)/shard_map/all_to_all | solution.py:94
  11.8 0.8 subtract_convert_fusion
  12.6 18.5 %all_to_all.29 = bf16[8,8,4608]{2,1,0:T(8,128)(2,1)S(1)} all-to-all(bf16[8,8,4608]{2,1,0:T(8,128)(2,1)S(1)} %broadcast_in_dim.4), channel_id=1, replica_groups={{0,2,1,3,32,34,33,35},{4,6,5,7,36,38,37,39},{16,18,17,19,48,50,49,51},{..., dimensions={0} | all-to-all | bytes 1179648 | tf_op jit(solution)/shard_map/all_to_all | solution.py:46
  31.1 9.0 %collective-permute-done.2 = bf16[8,8,4608]{2,1,0:T(8,128)(2,1)S(1)} collective-permute-done((bf16[8,8,4608]{2,1,0:T(8,128)(2,1)S(1)}, bf16[8,8,4608]{2,1,0:T(8,128)(2,1)S(1)}, u32[]{:S(2)}, u32[]{:S(2)}) %collective-permute-start.2) | collective-permute-done | bytes 589856 | tf_op jit(solution)/shard_map/ppermute | solution.py:29
  40.5 2.4 %collective-permute-start.3 = (bf16[32,8,4608]{2,1,0:T(8,128)(2,1)S(1)}, bf16[32,8,4608]{2,1,0:T(8,128)(2,1)S(1)}, u32[]{:S(2)}, u32[]{:S(2)}) collective-permute-start(bf16[32,8,4608]{2,1,0:T(8,128)(2,1)S(1)} %pad_maximum_fusion.3), channel_id=1, source_target_pairs={{0,8},{8,0},{1,9},{9,1},{2,10},{10,2},{3,11},{11,3},{4,12},{12,4},... | collective-permute-start | bytes 7077896 | tf_op jit(solution)/shard_map/ppermute | solution.py:50
  43.5 2.1 %collective-permute-start.5 = (bf16[8,8,4608]{2,1,0:T(8,128)(2,1)S(1)}, bf16[8,8,4608]{2,1,0:T(8,128)(2,1)S(1)}, u32[]{:S(2)}, u32[]{:S(2)}) collective-permute-start(bf16[8,8,4608]{2,1,0:T(8,128)(2,1)S(1)} %collective-permute-done.1), channel_id=1, source_target_pairs={{6,0},{10,8},{4,2},{8,10},{2,4},{14,12},{0,6},{12,14},{7,1},{11,9}... | collective-permute-start | bytes 1769480 | tf_op jit(solution)/shard_map/ppermute | solution.py:29
  46.1 1.0 collective-permute-done.3
  47.6 2.6 %convolution_add_fusion = f32[512,512]{1,0:T(8,128)S(1)} fusion(bf16[4608,512]{1,0:T(8,128)(2,1)S(1)} %bitcast.80, f32[512]{0:T(512)S(1)} %copy-done.9, bf16[64,8,4608]{2,1,0:T(8,128)(2,1)S(1)} %pad_maximum_fusion), kind=kOutput, calls=%fused_computation.22 | convolution fusion | flops 2416181248 | bytes 10487808 | tf_op jit(solution)/shard_map/dot_general | solution.py:99
  50.2 1.4 fusion.37
  51.6 1.3 collective-permute-done.8
  52.9 5.4 %collective-permute-done.6 = bf16[8,8,4608]{2,1,0:T(8,128)(2,1)S(1)} collective-permute-done((bf16[8,8,4608]{2,1,0:T(8,128)(2,1)S(1)}, bf16[8,8,4608]{2,1,0:T(8,128)(2,1)S(1)}, u32[]{:S(2)}, u32[]{:S(2)}) %collective-permute-start.6) | collective-permute-done | bytes 589856 | tf_op jit(solution)/shard_map/ppermute | solution.py:29
  59.0 3.7 %collective-permute-start.9 = (bf16[32,8,4608]{2,1,0:T(8,128)(2,1)S(1)}, bf16[32,8,4608]{2,1,0:T(8,128)(2,1)S(1)}, u32[]{:S(2)}, u32[]{:S(2)}) collective-permute-start(bf16[32,8,4608]{2,1,0:T(8,128)(2,1)S(1)} %pad_maximum_fusion.4), channel_id=1, source_target_pairs={{0,8},{8,0},{1,9},{9,1},{2,10},{10,2},{3,11},{11,3},{4,12},{12,4},... | collective-permute-start | bytes 7077896 | tf_op jit(solution)/shard_map/ppermute | solution.py:50
  62.7 1.4 convolution_add_fusion.4
  64.1 1.1 fusion.35
  65.2 1.7 collective-permute-done.9
  66.9 1.4 convolution_add_fusion.3
  68.3 1.0 fusion.33
  69.3 1.4 convolution_convert_fusion.1
  71.5 1.4 convolution_convert_fusion.3
  73.5 1.4 convolution_convert_fusion.2
  74.9 1.4 convolution_convert_fusion.4
  76.3 1.4 fusion.24
  79.6 2.8 %collective-permute-start.18 = (bf16[8,8,4608]{2,1,0:T(8,128)(2,1)}, bf16[8,8,4608]{2,1,0:T(8,128)(2,1)S(1)}, u32[]{:S(2)}, u32[]{:S(2)}) collective-permute-start(bf16[8,8,4608]{2,1,0:T(8,128)(2,1)} %get-tuple-element.66), channel_id=1, source_target_pairs={{119,0},{43,8},{117,2},{41,10},{115,4},{47,12},{113,6},{45,14},{11... | collective-permute-start | bytes 1769480 | tf_op jit(solution)/shard_map/ppermute | solution.py:29
  82.5 4.3 %collective-permute-done.12 = bf16[8,8,4608]{2,1,0:T(8,128)(2,1)S(1)} collective-permute-done((bf16[8,8,4608]{2,1,0:T(8,128)(2,1)S(1)}, bf16[8,8,4608]{2,1,0:T(8,128)(2,1)S(1)}, u32[]{:S(2)}, u32[]{:S(2)}) %collective-permute-start.12) | collective-permute-done | bytes 589856 | tf_op jit(solution)/shard_map/ppermute | solution.py:29
  87.0 1.6 collective-permute-done.14
  88.8 1.0 multiply_reduce_fusion
  89.8 5.2 %collective-permute-done.16 = bf16[8,8,4608]{2,1,0:T(8,128)(2,1)S(1)} collective-permute-done((bf16[8,8,4608]{2,1,0:T(8,128)(2,1)S(1)}, bf16[8,8,4608]{2,1,0:T(8,128)(2,1)S(1)}, u32[]{:S(2)}, u32[]{:S(2)}) %collective-permute-start.16) | collective-permute-done | bytes 589856 | tf_op jit(solution)/shard_map/ppermute | solution.py:29
  95.0 1.0 add_convert_fusion.4
  96.5 0.8 maximum_bitcast_fusion.1
  97.7 3.5 %collective-permute-done.13 = bf16[8,8,4608]{2,1,0:T(8,128)(2,1)S(1)} collective-permute-done((bf16[8,8,4608]{2,1,0:T(8,128)(2,1)S(1)}, bf16[8,8,4608]{2,1,0:T(8,128)(2,1)S(1)}, u32[]{:S(2)}, u32[]{:S(2)}) %collective-permute-start.13) | collective-permute-done | bytes 589856 | tf_op jit(solution)/shard_map/ppermute | solution.py:29
  101.3 3.9 %collective-permute-done.17 = bf16[8,8,4608]{2,1,0:T(8,128)(2,1)S(1)} collective-permute-done((bf16[8,8,4608]{2,1,0:T(8,128)(2,1)}, bf16[8,8,4608]{2,1,0:T(8,128)(2,1)S(1)}, u32[]{:S(2)}, u32[]{:S(2)}) %collective-permute-start.17) | collective-permute-done | bytes 589856 | tf_op jit(solution)/shard_map/ppermute | solution.py:29
  105.6 14.1 %all_to_all.30 = bf16[8,8,4608]{2,1,0:T(8,128)(2,1)S(1)} all-to-all(bf16[8,8,4608]{2,1,0:T(8,128)(2,1)S(1)} %add_convert_fusion.3), channel_id=1, replica_groups={{0,2,1,3,32,34,33,35},{4,6,5,7,36,38,37,39},{16,18,17,19,48,50,49,51},{..., dimensions={0} | all-to-all | bytes 1179648 | tf_op jit(solution)/shard_map/all_to_all | solution.py:46
  119.8 13.6 %all_to_all.31 = bf16[8,8,4608]{2,1,0:T(8,128)(2,1)S(1)} all-to-all(bf16[8,8,4608]{2,1,0:T(8,128)(2,1)S(1)} %broadcast_in_dim.5), channel_id=1, replica_groups={{0,2,1,3,32,34,33,35},{4,6,5,7,36,38,37,39},{16,18,17,19,48,50,49,51},{..., dimensions={0} | all-to-all | bytes 1179648 | tf_op jit(solution)/shard_map/all_to_all | solution.py:46
  133.5 9.1 %collective-permute-done.21 = bf16[8,8,4608]{2,1,0:T(8,128)(2,1)} collective-permute-done((bf16[8,8,4608]{2,1,0:T(8,128)(2,1)S(1)}, bf16[8,8,4608]{2,1,0:T(8,128)(2,1)}, u32[]{:S(2)}, u32[]{:S(2)}) %collective-permute-start.21) | collective-permute-done | bytes 589856 | tf_op jit(solution)/shard_map/ppermute | solution.py:29
  142.6 1.7 pad_maximum_fusion.5
  144.3 3.6 %collective-permute-start.22 = (bf16[32,8,4608]{2,1,0:T(8,128)(2,1)S(1)}, bf16[32,8,4608]{2,1,0:T(8,128)(2,1)S(1)}, u32[]{:S(2)}, u32[]{:S(2)}) collective-permute-start(bf16[32,8,4608]{2,1,0:T(8,128)(2,1)S(1)} %pad_maximum_fusion.5), channel_id=1, source_target_pairs={{0,8},{8,0},{1,9},{9,1},{2,10},{10,2},{3,11},{11,3},{4,12},{12,4},... | collective-permute-start | bytes 7077896 | tf_op jit(solution)/shard_map/ppermute | solution.py:50
  147.9 1.6 collective-permute-start.26
  151.3 0.8 collective-permute-done.22
  152.5 3.9 %fusion.9 = bf16[512,512]{1,0:T(8,128)(2,1)S(1)} fusion(f32[512,512]{1,0:T(8,128)} %get-tuple-element.52, bf16[512,4608]{1,0:T(8,128)(2,1)S(1)} %bitcast.69, bf16[64,8,4608]{2,1,0:T(8,128)(2,1)S(1)} %pad_maximum_fusion.1, f32[512]{0:T(512)S(1)} %get-tuple-element.86), kind=kOutput, calls=%fused_computation.23 | convolution fusion | flops 2416705536 | bytes 11012096 | tf_op jit(solution)/shard_map/dot_general | solution.py:155
  156.4 4.3 %convolution_convert_fusion = bf16[4608,512]{1,0:T(8,128)(2,1)} fusion(bf16[4608,512]{0,1:T(8,128)(2,1)S(1)} %bitcast.72, bf16[512,512]{1,0:T(8,128)(2,1)S(1)} %fusion.9), kind=kOutput, calls=%fused_computation.4 | convolution fusion | flops 2418278400 | bytes 9961472 | tf_op jit(solution)/shard_map/dot_general | solution.py:164
  160.7 3.8 %collective-permute-done.24 = bf16[8,8,4608]{2,1,0:T(8,128)(2,1)} collective-permute-done((bf16[8,8,4608]{2,1,0:T(8,128)(2,1)}, bf16[8,8,4608]{2,1,0:T(8,128)(2,1)}, u32[]{:S(2)}, u32[]{:S(2)}) %collective-permute-start.24) | collective-permute-done | bytes 589856 | tf_op jit(solution)/shard_map/ppermute | solution.py:29
  164.5 1.9 %pad_maximum_fusion.6 = bf16[32,8,4608]{2,1,0:T(8,128)(2,1)S(1)} fusion(bf16[8,8,4608]{2,1,0:T(8,128)(2,1)} %collective-permute-done.26, bf16[8,8,4608]{2,1,0:T(8,128)(2,1)} %collective-permute-done.25, bf16[8,8,4608]{2,1,0:T(8,128)(2,1)} %collective-permute-done.24, bf16[8,8,4608]{2,1,0:T(8,128)(2,1)} %collective-permute-done.23), kind=kLoop, calls=%fused_computation.19 | loop fusion | flops 3538944 | bytes 4718592 | tf_op jit(solution)/shard_map/concatenate | solution.py:76
  166.4 4.0 %collective-permute-start.27 = (bf16[32,8,4608]{2,1,0:T(8,128)(2,1)S(1)}, bf16[32,8,4608]{2,1,0:T(8,128)(2,1)S(1)}, u32[]{:S(2)}, u32[]{:S(2)}) collective-permute-start(bf16[32,8,4608]{2,1,0:T(8,128)(2,1)S(1)} %pad_maximum_fusion.6), channel_id=1, source_target_pairs={{0,8},{8,0},{1,9},{9,1},{2,10},{10,2},{3,11},{11,3},{4,12},{12,4},... | collective-permute-start | bytes 7077896 | tf_op jit(solution)/shard_map/ppermute | solution.py:50
  170.4 3.1 %add_convert_fusion.2 = bf16[512,4608]{1,0:T(8,128)(2,1)S(1)} fusion(bf16[512,4608]{1,0:T(8,128)(2,1)S(1)} %bitcast.69, bf16[512,512]{0,1:T(8,128)(2,1)S(1)} %bitcast.77, bf16[64,8,4608]{2,1,0:T(8,128)(2,1)S(1)} %pad_maximum_fusion.1, f32[512]{0:T(512)S(1)} %get-tuple-element.94), kind=kOutput, calls=%fused_computation.2 | convolution fusion | flops 2425356288 | bytes 14682112 | tf_op jit(solution)/shard_map/dot_general | solution.py:167
  173.5 1.4 fusion.14
  174.9 1.4 fusion.15
  177.4 4.3 %add_convert_fusion = bf16[512,4608]{1,0:T(8,128)(2,1)} fusion(bf16[512,4608]{1,0:T(8,128)(2,1)S(1)} %add_convert_fusion.2, bf16[512,512]{0,1:T(8,128)(2,1)S(1)} %copy-done.2, bf16[512,4608]{1,0:T(8,128)(2,1)S(1)} %pad_maximum_fusion.2), kind=kOutput, calls=%fused_computation | convolution fusion | flops 2422996992 | bytes 14680064 | tf_op jit(solution)/shard_map/dot_general | solution.py:175
  181.7 4.4 %add_convert_fusion.1 = bf16[4608,512]{1,0:T(8,128)(2,1)} fusion(bf16[4608,512]{1,0:T(8,128)(2,1)S(1)} %bitcast.84, bf16[4608,512]{0,1:T(8,128)(2,1)S(1)} %maximum_bitcast_fusion, bf16[512,512]{1,0:T(8,128)(2,1)S(1)} %pad_maximum_fusion.7), kind=kOutput, calls=%fused_computation.1 | convolution fusion | flops 2422996992 | bytes 14680064 | tf_op jit(solution)/shard_map/dot_general | solution.py:174
  (96 shorter events, 11.0 us)
Async XLA Ops:
  11.8 28.7 %copy-start.3 = (f32[8,4608]{1,0:T(8,128)}, f32[8,4608]{1,0:T(8,128)S(1)}, u32[]{:S(2)}) copy-start(f32[8,4608]{1,0:T(8,128)S(1)} %reshape.92) | copy-start | bytes 442372
  31.1 9.0 %collective-permute-start.2 = (bf16[8,8,4608]{2,1,0:T(8,128)(2,1)S(1)}, bf16[8,8,4608]{2,1,0:T(8,128)(2,1)S(1)}, u32[]{:S(2)}, u32[]{:S(2)}) collective-permute-start(bf16[8,8,4608]{2,1,0:T(8,128)(2,1)S(1)} %all_to_all.29), channel_id=1, source_target_pairs={{96,0},{40,8},{98,2},{42,10},{100,4},{44,12},{102,6},{46,14},{97,1... | collective-permute-start | bytes 1769480 | tf_op jit(solution)/shard_map/ppermute | solution.py:29
  31.1 9.0 %collective-permute-start.1 = (bf16[8,8,4608]{2,1,0:T(8,128)(2,1)S(1)}, bf16[8,8,4608]{2,1,0:T(8,128)(2,1)S(1)}, u32[]{:S(2)}, u32[]{:S(2)}) collective-permute-start(bf16[8,8,4608]{2,1,0:T(8,128)(2,1)S(1)} %all_to_all.29), channel_id=1, source_target_pairs={{17,0},{9,8},{19,2},{11,10},{21,4},{13,12},{23,6},{15,14},{16,1},{... | collective-permute-start | bytes 1769480 | tf_op jit(solution)/shard_map/ppermute | solution.py:29
  31.1 9.0 %collective-permute-start = (bf16[8,8,4608]{2,1,0:T(8,128)(2,1)S(1)}, bf16[8,8,4608]{2,1,0:T(8,128)(2,1)S(1)}, u32[]{:S(2)}, u32[]{:S(2)}) collective-permute-start(bf16[8,8,4608]{2,1,0:T(8,128)(2,1)S(1)} %all_to_all.29), channel_id=1, source_target_pairs={{6,0},{10,8},{4,2},{8,10},{2,4},{14,12},{0,6},{12,14},{7,1},{11,9}... | collective-permute-start | bytes 1769480 | tf_op jit(solution)/shard_map/ppermute | solution.py:29
  40.2 7.4 %slice-start.2 = ((s8[4718592]{0:T(1024)(128)(4,1)}), s8[4194304]{0:T(1024)(128)(4,1)S(1)}, s32[]{:S(2)}) async-start(s8[4718592]{0:T(1024)(128)(4,1)} %bitcast.79), calls=%async_computation.6 | async-start | bytes 8388608
  40.5 7.1 %slice-start.3 = ((s8[4718592]{0:T(1024)(128)(4,1)}), s8[524288]{0:T(1024)(128)(4,1)S(1)}, s32[]{:S(2)}) async-start(s8[4718592]{0:T(1024)(128)(4,1)} %bitcast.79), calls=%async_computation.7 | async-start | bytes 1048576
  40.5 7.1 %copy-start.9 = (f32[512]{0:T(512)S(1)}, f32[512]{0:T(512)}, u32[]{:S(2)}) copy-start(f32[512]{0:T(512)} %param.8) | copy-start | bytes 6148
  40.5 6.6 %collective-permute-start.3 = (bf16[32,8,4608]{2,1,0:T(8,128)(2,1)S(1)}, bf16[32,8,4608]{2,1,0:T(8,128)(2,1)S(1)}, u32[]{:S(2)}, u32[]{:S(2)}) collective-permute-start(bf16[32,8,4608]{2,1,0:T(8,128)(2,1)S(1)} %pad_maximum_fusion.3), channel_id=1, source_target_pairs={{0,8},{8,0},{1,9},{9,1},{2,10},{10,2},{3,11},{11,3},{4,12},{12,4},... | collective-permute-start | bytes 7077896 | tf_op jit(solution)/shard_map/ppermute | solution.py:50
  43.0 10.0 %collective-permute-start.8 = (bf16[8,8,4608]{2,1,0:T(8,128)(2,1)S(1)}, bf16[8,8,4608]{2,1,0:T(8,128)(2,1)S(1)}, u32[]{:S(2)}, u32[]{:S(2)}) collective-permute-start(bf16[8,8,4608]{2,1,0:T(8,128)(2,1)S(1)} %collective-permute-done.2), channel_id=1, source_target_pairs={{23,0},{11,8},{21,2},{9,10},{19,4},{15,12},{17,6},{13,14},{22,1},{... | collective-permute-start | bytes 1769480 | tf_op jit(solution)/shard_map/ppermute | solution.py:29
  43.0 15.3 %collective-permute-start.6 = (bf16[8,8,4608]{2,1,0:T(8,128)(2,1)S(1)}, bf16[8,8,4608]{2,1,0:T(8,128)(2,1)S(1)}, u32[]{:S(2)}, u32[]{:S(2)}) collective-permute-start(bf16[8,8,4608]{2,1,0:T(8,128)(2,1)S(1)} %collective-permute-done.2), channel_id=1, source_target_pairs={{17,0},{9,8},{19,2},{11,10},{21,4},{13,12},{23,6},{15,14},{16,1},{... | collective-permute-start | bytes 1769480 | tf_op jit(solution)/shard_map/ppermute | solution.py:29
  43.5 15.1 %collective-permute-start.5 = (bf16[8,8,4608]{2,1,0:T(8,128)(2,1)S(1)}, bf16[8,8,4608]{2,1,0:T(8,128)(2,1)S(1)}, u32[]{:S(2)}, u32[]{:S(2)}) collective-permute-start(bf16[8,8,4608]{2,1,0:T(8,128)(2,1)S(1)} %collective-permute-done.1), channel_id=1, source_target_pairs={{6,0},{10,8},{4,2},{8,10},{2,4},{14,12},{0,6},{12,14},{7,1},{11,9}... | collective-permute-start | bytes 1769480 | tf_op jit(solution)/shard_map/ppermute | solution.py:29
  45.6 13.0 %collective-permute-start.7 = (bf16[8,8,4608]{2,1,0:T(8,128)(2,1)S(1)}, bf16[8,8,4608]{2,1,0:T(8,128)(2,1)S(1)}, u32[]{:S(2)}, u32[]{:S(2)}) collective-permute-start(bf16[8,8,4608]{2,1,0:T(8,128)(2,1)S(1)} %collective-permute-done), channel_id=1, source_target_pairs={{96,0},{40,8},{98,2},{42,10},{100,4},{44,12},{102,6},{46,14},{97,1... | collective-permute-start | bytes 1769480 | tf_op jit(solution)/shard_map/ppermute | solution.py:29
  47.6 2.6 %copy-start.8 = (f32[512]{0:T(512)S(1)}, f32[512]{0:T(512)}, u32[]{:S(2)}) copy-start(f32[512]{0:T(512)} %param.9) | copy-start | bytes 6148
  58.7 8.2 %slice-start.4 = ((s8[4718592]{0:T(1024)(128)(4,1)}), s8[4194304]{0:T(1024)(128)(4,1)S(1)}, s32[]{:S(2)}) async-start(s8[4718592]{0:T(1024)(128)(4,1)} %bitcast.81), calls=%async_computation.8 | async-start | bytes 8388608
  59.0 7.9 %slice-start.5 = ((s8[4718592]{0:T(1024)(128)(4,1)}), s8[524288]{0:T(1024)(128)(4,1)S(1)}, s32[]{:S(2)}) async-start(s8[4718592]{0:T(1024)(128)(4,1)} %bitcast.81), calls=%async_computation.9 | async-start | bytes 1048576
  59.0 7.9 %collective-permute-start.9 = (bf16[32,8,4608]{2,1,0:T(8,128)(2,1)S(1)}, bf16[32,8,4608]{2,1,0:T(8,128)(2,1)S(1)}, u32[]{:S(2)}, u32[]{:S(2)}) collective-permute-start(bf16[32,8,4608]{2,1,0:T(8,128)(2,1)S(1)} %pad_maximum_fusion.4), channel_id=1, source_target_pairs={{0,8},{8,0},{1,9},{9,1},{2,10},{10,2},{3,11},{11,3},{4,12},{12,4},... | collective-permute-start | bytes 7077896 | tf_op jit(solution)/shard_map/ppermute | solution.py:50
  64.1 5.2 %slice-start = ((s8[4718592]{0:T(1024)(128)(4,1)}), s8[4194304]{0:T(1024)(128)(4,1)S(1)}, s32[]{:S(2)}) async-start(s8[4718592]{0:T(1024)(128)(4,1)} %bitcast.68), calls=%async_computation.4 | async-start | bytes 8388608
  66.9 1.4 copy-start
  66.9 2.4 %slice-start.1 = ((s8[4718592]{0:T(1024)(128)(4,1)}), s8[524288]{0:T(1024)(128)(4,1)S(1)}, s32[]{:S(2)}) async-start(s8[4718592]{0:T(1024)(128)(4,1)} %bitcast.68), calls=%async_computation.5 | async-start | bytes 1048576
  70.9 5.4 %collective-permute-start.11 = (bf16[128,4608]{1,0:T(8,128)(2,1)S(1)}, bf16[128,4608]{1,0:T(8,128)(2,1)S(1)}, u32[]{:S(2)}, u32[]{:S(2)}) collective-permute-start(bf16[128,4608]{1,0:T(8,128)(2,1)S(1)} %get-tuple-element.108), channel_id=1, source_target_pairs={{0,8},{8,0},{1,9},{9,1},{2,10},{10,2},{3,11},{11,3},{4,12},{12,4},... | collective-permute-start | bytes 3538952 | tf_op jit(solution)/shard_map/ppermute | solution.py:50
  71.4 5.0 %collective-permute-start.10 = (bf16[128,4608]{1,0:T(8,128)(2,1)S(1)}, bf16[128,4608]{1,0:T(8,128)(2,1)S(1)}, u32[]{:S(2)}, u32[]{:S(2)}) collective-permute-start(bf16[128,4608]{1,0:T(8,128)(2,1)S(1)} %get-tuple-element.109), channel_id=1, source_target_pairs={{0,8},{8,0},{1,9},{9,1},{2,10},{10,2},{3,11},{11,3},{4,12},{12,4},... | collective-permute-start | bytes 3538952 | tf_op jit(solution)/shard_map/ppermute | solution.py:50
  72.9 6.0 %collective-permute-start.4 = (bf16[256,4608]{1,0:T(8,128)(2,1)S(1)}, bf16[256,4608]{1,0:T(8,128)(2,1)S(1)}, u32[]{:S(2)}, u32[]{:S(2)}) collective-permute-start(bf16[256,4608]{1,0:T(8,128)(2,1)S(1)} %convolution_convert_fusion.3), channel_id=1, source_target_pairs={{0,8},{8,0},{1,9},{9,1},{2,10},{10,2},{3,11},{11,3},{4,12},{12,4},... | collective-permute-start | bytes 7077896 | tf_op jit(solution)/shard_map/ppermute | solution.py:50
  77.7 9.0 %collective-permute-start.12 = (bf16[8,8,4608]{2,1,0:T(8,128)(2,1)S(1)}, bf16[8,8,4608]{2,1,0:T(8,128)(2,1)S(1)}, u32[]{:S(2)}, u32[]{:S(2)}) collective-permute-start(bf16[8,8,4608]{2,1,0:T(8,128)(2,1)S(1)} %get-tuple-element.63), channel_id=1, source_target_pairs={{96,0},{40,8},{98,2},{42,10},{100,4},{44,12},{102,6},{46,14},{97,1... | collective-permute-start | bytes 1769480 | tf_op jit(solution)/shard_map/ppermute | solution.py:29
  79.4 9.1 %collective-permute-start.14 = (bf16[8,8,4608]{2,1,0:T(8,128)(2,1)S(1)}, bf16[8,8,4608]{2,1,0:T(8,128)(2,1)S(1)}, u32[]{:S(2)}, u32[]{:S(2)}) collective-permute-start(bf16[8,8,4608]{2,1,0:T(8,128)(2,1)S(1)} %get-tuple-element.61), channel_id=1, source_target_pairs={{6,0},{10,8},{4,2},{8,10},{2,4},{14,12},{0,6},{12,14},{7,1},{11,9}... | collective-permute-start | bytes 1769480 | tf_op jit(solution)/shard_map/ppermute | solution.py:29
  79.5 15.4 %collective-permute-start.16 = (bf16[8,8,4608]{2,1,0:T(8,128)(2,1)S(1)}, bf16[8,8,4608]{2,1,0:T(8,128)(2,1)S(1)}, u32[]{:S(2)}, u32[]{:S(2)}) collective-permute-start(bf16[8,8,4608]{2,1,0:T(8,128)(2,1)S(1)} %get-tuple-element.62), channel_id=1, source_target_pairs={{17,0},{9,8},{19,2},{11,10},{21,4},{13,12},{23,6},{15,14},{16,1},{... | collective-permute-start | bytes 1769480 | tf_op jit(solution)/shard_map/ppermute | solution.py:29
  79.6 18.1 %collective-permute-start.18 = (bf16[8,8,4608]{2,1,0:T(8,128)(2,1)}, bf16[8,8,4608]{2,1,0:T(8,128)(2,1)S(1)}, u32[]{:S(2)}, u32[]{:S(2)}) collective-permute-start(bf16[8,8,4608]{2,1,0:T(8,128)(2,1)} %get-tuple-element.66), channel_id=1, source_target_pairs={{119,0},{43,8},{117,2},{41,10},{115,4},{47,12},{113,6},{45,14},{11... | collective-permute-start | bytes 1769480 | tf_op jit(solution)/shard_map/ppermute | solution.py:29
  86.9 14.4 %collective-permute-start.13 = (bf16[8,8,4608]{2,1,0:T(8,128)(2,1)S(1)}, bf16[8,8,4608]{2,1,0:T(8,128)(2,1)S(1)}, u32[]{:S(2)}, u32[]{:S(2)}) collective-permute-start(bf16[8,8,4608]{2,1,0:T(8,128)(2,1)S(1)} %add_convert_fusion.6), channel_id=1, source_target_pairs={{6,0},{10,8},{4,2},{8,10},{2,4},{14,12},{0,6},{12,14},{7,1},{11,9}... | collective-permute-start | bytes 1769480 | tf_op jit(solution)/shard_map/ppermute | solution.py:29
  88.7 12.6 %collective-permute-start.15 = (bf16[8,8,4608]{2,1,0:T(8,128)(2,1)S(1)}, bf16[8,8,4608]{2,1,0:T(8,128)(2,1)S(1)}, u32[]{:S(2)}, u32[]{:S(2)}) collective-permute-start(bf16[8,8,4608]{2,1,0:T(8,128)(2,1)S(1)} %add_convert_fusion.5), channel_id=1, source_target_pairs={{17,0},{9,8},{19,2},{11,10},{21,4},{13,12},{23,6},{15,14},{16,1},{... | collective-permute-start | bytes 1769480 | tf_op jit(solution)/shard_map/ppermute | solution.py:29
  89.8 7.6 %copy-start.1 = (bf16[32,8,4608]{2,1,0:T(8,128)(2,1)S(1)}, bf16[32,8,4608]{2,1,0:T(8,128)(2,1)}, u32[]{:S(2)}) copy-start(bf16[32,8,4608]{2,1,0:T(8,128)(2,1)} %copy-done) | copy-start | bytes 7077892
  95.9 9.2 %collective-permute-start.17 = (bf16[8,8,4608]{2,1,0:T(8,128)(2,1)}, bf16[8,8,4608]{2,1,0:T(8,128)(2,1)S(1)}, u32[]{:S(2)}, u32[]{:S(2)}) collective-permute-start(bf16[8,8,4608]{2,1,0:T(8,128)(2,1)} %add_convert_fusion.4), channel_id=1, source_target_pairs={{96,0},{40,8},{98,2},{42,10},{100,4},{44,12},{102,6},{46,14},{97,1... | collective-permute-start | bytes 1769480 | tf_op jit(solution)/shard_map/ppermute | solution.py:29
  105.2 14.6 %copy-start.4 = (f32[8,4608]{1,0:T(8,128)S(1)}, f32[8,4608]{1,0:T(8,128)}, u32[]{:S(2)}) copy-start(f32[8,4608]{1,0:T(8,128)} %copy-done.3) | copy-start | bytes 442372
  105.2 14.6 %copy-start.7 = (f32[4608]{0:T(1024)S(1)}, f32[4608]{0:T(1024)}, u32[]{:S(2)}) copy-start(f32[4608]{0:T(1024)} %param.11) | copy-start | bytes 55300
  133.4 9.1 %collective-permute-start.21 = (bf16[8,8,4608]{2,1,0:T(8,128)(2,1)S(1)}, bf16[8,8,4608]{2,1,0:T(8,128)(2,1)}, u32[]{:S(2)}, u32[]{:S(2)}) collective-permute-start(bf16[8,8,4608]{2,1,0:T(8,128)(2,1)S(1)} %all_to_all.31), channel_id=1, source_target_pairs={{96,0},{40,8},{98,2},{42,10},{100,4},{44,12},{102,6},{46,14},{97,1... | collective-permute-start | bytes 1769480 | tf_op jit(solution)/shard_map/ppermute | solution.py:29
  133.4 9.1 %collective-permute-start.20 = (bf16[8,8,4608]{2,1,0:T(8,128)(2,1)S(1)}, bf16[8,8,4608]{2,1,0:T(8,128)(2,1)}, u32[]{:S(2)}, u32[]{:S(2)}) collective-permute-start(bf16[8,8,4608]{2,1,0:T(8,128)(2,1)S(1)} %all_to_all.31), channel_id=1, source_target_pairs={{17,0},{9,8},{19,2},{11,10},{21,4},{13,12},{23,6},{15,14},{16,1},{... | collective-permute-start | bytes 1769480 | tf_op jit(solution)/shard_map/ppermute | solution.py:29
  133.4 9.1 %collective-permute-start.19 = (bf16[8,8,4608]{2,1,0:T(8,128)(2,1)S(1)}, bf16[8,8,4608]{2,1,0:T(8,128)(2,1)}, u32[]{:S(2)}, u32[]{:S(2)}) collective-permute-start(bf16[8,8,4608]{2,1,0:T(8,128)(2,1)S(1)} %all_to_all.31), channel_id=1, source_target_pairs={{6,0},{10,8},{4,2},{8,10},{2,4},{14,12},{0,6},{12,14},{7,1},{11,9}... | collective-permute-start | bytes 1769480 | tf_op jit(solution)/shard_map/ppermute | solution.py:29
  144.3 7.8 %collective-permute-start.22 = (bf16[32,8,4608]{2,1,0:T(8,128)(2,1)S(1)}, bf16[32,8,4608]{2,1,0:T(8,128)(2,1)S(1)}, u32[]{:S(2)}, u32[]{:S(2)}) collective-permute-start(bf16[32,8,4608]{2,1,0:T(8,128)(2,1)S(1)} %pad_maximum_fusion.5), channel_id=1, source_target_pairs={{0,8},{8,0},{1,9},{9,1},{2,10},{10,2},{3,11},{11,3},{4,12},{12,4},... | collective-permute-start | bytes 7077896 | tf_op jit(solution)/shard_map/ppermute | solution.py:50
  147.9 12.7 %collective-permute-start.26 = (bf16[8,8,4608]{2,1,0:T(8,128)(2,1)}, bf16[8,8,4608]{2,1,0:T(8,128)(2,1)}, u32[]{:S(2)}, u32[]{:S(2)}) collective-permute-start(bf16[8,8,4608]{2,1,0:T(8,128)(2,1)} %collective-permute-done.21), channel_id=1, source_target_pairs={{23,0},{11,8},{21,2},{9,10},{19,4},{15,12},{17,6},{13,14},{22,1},{... | collective-permute-start | bytes 1769480 | tf_op jit(solution)/shard_map/ppermute | solution.py:29
  149.5 15.0 %collective-permute-start.24 = (bf16[8,8,4608]{2,1,0:T(8,128)(2,1)}, bf16[8,8,4608]{2,1,0:T(8,128)(2,1)}, u32[]{:S(2)}, u32[]{:S(2)}) collective-permute-start(bf16[8,8,4608]{2,1,0:T(8,128)(2,1)} %collective-permute-done.21), channel_id=1, source_target_pairs={{17,0},{9,8},{19,2},{11,10},{21,4},{13,12},{23,6},{15,14},{16,1},{... | collective-permute-start | bytes 1769480 | tf_op jit(solution)/shard_map/ppermute | solution.py:29
  150.1 14.4 %collective-permute-start.23 = (bf16[8,8,4608]{2,1,0:T(8,128)(2,1)}, bf16[8,8,4608]{2,1,0:T(8,128)(2,1)}, u32[]{:S(2)}, u32[]{:S(2)}) collective-permute-start(bf16[8,8,4608]{2,1,0:T(8,128)(2,1)} %collective-permute-done.20), channel_id=1, source_target_pairs={{6,0},{10,8},{4,2},{8,10},{2,4},{14,12},{0,6},{12,14},{7,1},{11,9}... | collective-permute-start | bytes 1769480 | tf_op jit(solution)/shard_map/ppermute | solution.py:29
  150.6 13.9 %collective-permute-start.25 = (bf16[8,8,4608]{2,1,0:T(8,128)(2,1)}, bf16[8,8,4608]{2,1,0:T(8,128)(2,1)}, u32[]{:S(2)}, u32[]{:S(2)}) collective-permute-start(bf16[8,8,4608]{2,1,0:T(8,128)(2,1)} %collective-permute-done.19), channel_id=1, source_target_pairs={{96,0},{40,8},{98,2},{42,10},{100,4},{44,12},{102,6},{46,14},{97,1... | collective-permute-start | bytes 1769480 | tf_op jit(solution)/shard_map/ppermute | solution.py:29
  166.4 7.1 %copy-start.5 = (f32[256,512]{1,0:T(8,128)S(1)}, f32[256,512]{1,0:T(8,128)}, u32[]{:S(2)}) copy-start(f32[256,512]{1,0:T(8,128)} %get-tuple-element.92) | copy-start | bytes 1572868
  166.4 8.5 %collective-permute-start.27 = (bf16[32,8,4608]{2,1,0:T(8,128)(2,1)S(1)}, bf16[32,8,4608]{2,1,0:T(8,128)(2,1)S(1)}, u32[]{:S(2)}, u32[]{:S(2)}) collective-permute-start(bf16[32,8,4608]{2,1,0:T(8,128)(2,1)S(1)} %pad_maximum_fusion.6), channel_id=1, source_target_pairs={{0,8},{8,0},{1,9},{9,1},{2,10},{10,2},{3,11},{11,3},{4,12},{12,4},... | collective-permute-start | bytes 7077896 | tf_op jit(solution)/shard_map/ppermute | solution.py:50
  173.5 1.4 copy-start.6
  176.3 1.0 copy-start.2
  176.7 5.1 %slice-start.6 = ((s8[4718592]{0:T(1024)(128)(4,1)}), s8[4194304]{0:T(1024)(128)(4,1)S(1)}, s32[]{:S(2)}) async-start(s8[4718592]{0:T(1024)(128)(4,1)} %bitcast.83), calls=%async_computation.10 | async-start | bytes 8388608
  177.4 4.3 %slice-start.7 = ((s8[4718592]{0:T(1024)(128)(4,1)}), s8[524288]{0:T(1024)(128)(4,1)S(1)}, s32[]{:S(2)}) async-start(s8[4718592]{0:T(1024)(128)(4,1)} %bitcast.83), calls=%async_computation.11 | async-start | bytes 1048576
